TPU v7x, 32 devices: a whole 2x2x4 slice. The times are simulated.
32 devices in a mesh: pipe: 8 (over z, y), expert: 4 (over x, core).
Axes of the slice: x: 2, y: 2, z: 4, core: 2. Of those that a mesh axis runs over, the one named last changes fastest.
Arguments:
- section_in_a: bfloat16 [8, 512, 4096], P('pipe', 'expert'), may hold values from -6 to 6
- route_a: int32 [8, 512, 8], P('pipe', 'expert'), may hold values from 0 to 127, as said below
- router: bfloat16 [8, 4096, 128], P('pipe'), may hold values from -0.09375 to 0.09375
- gate_up: bfloat16 [8, 2, 4096, 1024], P('pipe', None, None, 'expert'), may hold values from -0.09375 to 0.09375
- down_proj: bfloat16 [8, 1024, 4096], P('pipe', 'expert'), may hold values from -1 to 1
- section_in_b: bfloat16 [8, 512, 4096], P('pipe', 'expert'), may hold values from -6 to 6
- route_b: int32 [8, 512, 8], P('pipe', 'expert'), may hold values from 0 to 127, as said below
- grad_out_b: bfloat16 [8, 512, 4096], P('pipe', 'expert'), may hold values from -6 to 6
Outputs:
- section_out_a: bfloat16 [8, 512, 4096], P('pipe', 'expert')
- grad_in_b: bfloat16 [8, 512, 4096], P('pipe', 'expert')
- grad_gate_up: bfloat16 [8, 2, 4096, 1024], P('pipe', None, None, 'expert')
- grad_down: bfloat16 [8, 1024, 4096], P('pipe', 'expert')
- grad_router: bfloat16 [8, 4096, 128], P('pipe', 'expert')
Inputs may be any that keep to these rules, and one draw needn't show every extreme that they name: `route_a`: each row names 8 different experts in no particular order. Of the 128 rows of one device, at most 16 name any one expert below 1; for each such expert some section has every device's rows name it exactly 16 times. `route_b`: as for route_a.
All inputs are finite; a program needn't handle non-finite values.
Results may differ from a plain program's by a relative error of at most 0.0095.
Values may be sent and summed in bfloat16 or wider, within the bound.
No kernel may reach another device: no remote copies, remote signals or barrier semaphores. Data moves between devices by JAX's collectives and lax.ppermute only.
A program may use at most 128 MiB of HBM per device.

v0:
```python
import jax
import jax.numpy as jnp
from jax import lax
from jax.sharding import PartitionSpec as P

best_precision = lax.Precision.HIGHEST
contract_last = (((1,), (1,)), ((), ()))
contract_first = (((0,), (0,)), ((), ()))


def passed_along(block, axis, distance):
    devices = range(lax.axis_size(axis))
    route = [((i - distance) % len(devices), i) for i in devices]
    return lax.ppermute(block, axis, route)


def swapped(block, axis, bit):
    count = lax.axis_size(axis)
    route = []
    for low in range(count):
        high = low | 1 << bit
        if high != low and high < count:
            route += [(low, high), (high, low)]
    return lax.ppermute(block, axis, route)


def routing(expert_ids, flight, slot_count):
    tok_rows = expert_ids.shape[0]
    named_mask = jnp.stack(
        [jnp.any(expert_ids == expert_id, axis=1) for expert_id in range(flight)]
    ).astype(jnp.float32)
    earlier = (jnp.arange(tok_rows)[:, None] < jnp.arange(tok_rows)[None, :]).astype(jnp.float32)
    order_rank = jnp.dot(named_mask, earlier, precision=best_precision)
    slot_ids = jnp.arange(slot_count, dtype=jnp.float32)
    return named_mask[:, None, :] * (order_rank[:, None, :] == slot_ids[None, :, None]).astype(
        jnp.float32
    )


def gating(tokens_in, expert_ids, router_table, flight):
    experts = router_table.shape[1]
    logits = jnp.dot(tokens_in, router_table, preferred_element_type=jnp.float32)
    onehot = (expert_ids[:, :, None] == jnp.arange(experts, dtype=jnp.int32)[None, None, :]).astype(
        jnp.float32
    )
    chosen = jnp.sum(onehot * logits[:, None, :], axis=2)
    gate_prob = jax.nn.softmax(chosen, axis=-1)
    weights = jnp.stack(
        [
            jnp.sum(gate_prob * (expert_ids == expert_id).astype(jnp.float32), axis=1)
            for expert_id in range(flight)
        ],
        axis=1,
    )
    return (onehot, gate_prob, weights.astype(jnp.bfloat16))


def gather_slots(select, values):
    return jnp.einsum(
        "fst,td->fsd", select.astype(jnp.bfloat16), values, preferred_element_type=jnp.float32
    ).astype(jnp.bfloat16)


def slot_weights(select, weights):
    return jnp.einsum(
        "fst,tf->fs", select, weights.astype(jnp.float32), precision=best_precision
    ).astype(jnp.bfloat16)


def on_device(section_in_a, route_a, router, gate_up, down_proj, section_in_b, route_b, grad_out_b):
    groups = lax.axis_size("expert")
    wsplit = min(8, groups)
    flight = groups // wsplit
    tokens_a = section_in_a[0]
    tok_rows, model_width = tokens_a.shape
    slot_count = tok_rows // 8
    router_table = router[0]
    w_gate = gate_up[0, 0]
    w_up = gate_up[0, 1]
    w_down = down_proj[0]
    hidden_width = w_gate.shape[1]

    def expert_front(gathered):
        act_gate = jnp.dot(gathered, w_gate, preferred_element_type=jnp.float32)
        act_up = jnp.dot(gathered, w_up, preferred_element_type=jnp.float32)
        return (act_gate, act_up, (jax.nn.silu(act_gate) * act_up).astype(jnp.bfloat16))

    def to_partial(hidden):
        return jnp.dot(hidden, w_down, preferred_element_type=jnp.float32).astype(jnp.bfloat16)

    def fold_groups(returned):
        return (
            returned.astype(jnp.float32)
            .reshape(flight, wsplit, slot_count, model_width)
            .sum(axis=1)
        )

    select_a = routing(route_a[0], flight, slot_count)
    onehot_a, gate_a, weights_a = gating(tokens_a, route_a[0], router_table, flight)
    rows_a = gather_slots(select_a, tokens_a)
    slot_weight_a = slot_weights(select_a, weights_a)
    received = lax.all_to_all(
        jnp.repeat(rows_a, wsplit, axis=0), "expert", split_axis=0, concat_axis=0, tiled=True
    )
    row_count = received.shape[1]
    hidden = expert_front(received.reshape(-1, model_width))[2]
    partial_value = to_partial(hidden).reshape(groups, row_count, model_width)
    returned_a = lax.all_to_all(partial_value, "expert", split_axis=0, concat_axis=0, tiled=True)
    expert_out_a = fold_groups(returned_a)
    update_a = jnp.einsum(
        "fst,fsd->td",
        select_a,
        expert_out_a * slot_weight_a.astype(jnp.float32)[:, :, None],
        precision=best_precision,
    )
    section_result = (tokens_a.astype(jnp.float32) + update_a).astype(jnp.bfloat16)
    section_out_a = passed_along(section_result[None], "pipe", 1)
    tokens_b = section_in_b[0]
    grad_out = grad_out_b[0]
    expert_ids = route_b[0]
    select_b = routing(expert_ids, flight, slot_count)
    onehot_b, gate_b, weights_b = gating(tokens_b, expert_ids, router_table, flight)
    rows_b = gather_slots(select_b, tokens_b)
    grad_rows = gather_slots(select_b, grad_out)
    slot_weight_b = slot_weights(select_b, weights_b)
    recv_rows, recv_grads, recv_weights = (
        lax.all_to_all(
            jnp.repeat(rows_b, wsplit, axis=0), "expert", split_axis=0, concat_axis=0, tiled=True
        ),
        lax.all_to_all(
            jnp.repeat(grad_rows, wsplit, axis=0), "expert", split_axis=0, concat_axis=0, tiled=True
        ),
        lax.all_to_all(
            jnp.repeat(slot_weight_b, wsplit, axis=0),
            "expert",
            split_axis=0,
            concat_axis=0,
            tiled=True,
        ),
    )
    packed_rows = recv_rows.reshape(-1, model_width)
    packed_grads = recv_grads.reshape(-1, model_width)
    packed_weights = recv_weights.reshape(-1)
    act_gate, act_up, hidden = expert_front(packed_rows)
    scaled = (
        packed_weights.astype(jnp.float32)[:, None] * packed_grads.astype(jnp.float32)
    ).astype(jnp.bfloat16)
    d_hidden = lax.dot_general(scaled, w_down, contract_last, preferred_element_type=jnp.float32)
    logistic = jax.nn.sigmoid(act_gate)
    d_gate = (d_hidden * act_up * logistic * (1.0 + act_gate * (1.0 - logistic))).astype(
        jnp.bfloat16
    )
    d_up = (d_hidden * act_gate * logistic).astype(jnp.bfloat16)
    slot_part = (
        lax.dot_general(d_gate, w_gate, contract_last, preferred_element_type=jnp.float32)
        + lax.dot_general(d_up, w_up, contract_last, preferred_element_type=jnp.float32)
    ).astype(jnp.bfloat16)
    partial_b = to_partial(hidden)
    back_slots, back_outs = (
        lax.all_to_all(
            slot_part.reshape(groups, slot_count, model_width),
            "expert",
            split_axis=0,
            concat_axis=0,
            tiled=True,
        ),
        lax.all_to_all(
            partial_b.reshape(groups, slot_count, model_width),
            "expert",
            split_axis=0,
            concat_axis=0,
            tiled=True,
        ),
    )
    local_gate = lax.dot_general(
        packed_rows, d_gate, contract_first, preferred_element_type=jnp.float32
    )
    local_up = lax.dot_general(
        packed_rows, d_up, contract_first, preferred_element_type=jnp.float32
    )
    local_down = lax.dot_general(hidden, scaled, contract_first, preferred_element_type=jnp.float32)
    slot_back = fold_groups(back_slots)
    expert_out_b = fold_groups(back_outs)
    gate_score = jnp.sum(grad_rows.astype(jnp.float32) * expert_out_b, axis=2)
    token_score = jnp.einsum("fst,fs->tf", select_b, gate_score, precision=best_precision)
    gate_grad = jnp.zeros(expert_ids.shape, jnp.float32)
    for expert_id in range(flight):
        gate_grad = gate_grad + token_score[:, expert_id][:, None] * (
            expert_ids == expert_id
        ).astype(jnp.float32)
    logit_grad = gate_b * (gate_grad - jnp.sum(gate_b * gate_grad, axis=1, keepdims=True))
    logits_grad = jnp.sum(logit_grad[:, :, None] * onehot_b, axis=1).astype(jnp.bfloat16)
    token_back = jnp.einsum("fst,fsd->td", select_b, slot_back, precision=best_precision)
    router_back = lax.dot_general(
        logits_grad, router_table, contract_last, preferred_element_type=jnp.float32
    )
    back_grad = (grad_out.astype(jnp.float32) + token_back + router_back).astype(jnp.bfloat16)
    grad_in_b = passed_along(back_grad[None], "pipe", -1)
    experts = router_table.shape[1]
    share_rows = model_width // groups
    full_router = lax.dot_general(
        tokens_b, logits_grad, contract_first, preferred_element_type=jnp.float32
    )
    router_part = lax.psum_scatter(full_router, "expert", scatter_dimension=0, tiled=True)
    packed = jnp.concatenate(
        [
            jnp.stack([local_gate, local_up]).astype(jnp.bfloat16).reshape(-1),
            local_down.astype(jnp.bfloat16).reshape(-1),
            router_part.astype(jnp.bfloat16).reshape(-1),
        ]
    )
    partner = packed
    for bit_number in range(lax.axis_size("pipe").bit_length() - 1):
        partner = swapped(partner, "pipe", bit_number)
    summed_grads = (packed.astype(jnp.float32) + partner.astype(jnp.float32)).astype(jnp.bfloat16)
    inner_size = 2 * model_width * hidden_width
    down_size = hidden_width * model_width
    grad_gate_up = summed_grads[:inner_size].reshape(1, 2, model_width, hidden_width)
    grad_down = summed_grads[inner_size : inner_size + down_size].reshape(
        1, hidden_width, model_width
    )
    grad_router = summed_grads[inner_size + down_size :].reshape(1, share_rows, experts)
    return (section_out_a, grad_in_b, grad_gate_up, grad_down, grad_router)


def solution(mesh):
    return jax.shard_map(
        on_device,
        mesh=mesh,
        in_specs=(
            P("pipe", "expert", None),
            P("pipe", "expert", None),
            P("pipe", None, None),
            P("pipe", None, None, "expert"),
            P("pipe", "expert", None),
            P("pipe", "expert", None),
            P("pipe", "expert", None),
            P("pipe", "expert", None),
        ),
        out_specs=(
            P("pipe", "expert", None),
            P("pipe", "expert", None),
            P("pipe", None, None, "expert"),
            P("pipe", "expert", None),
            P("pipe", "expert", None),
        ),
        check_vma=False,
    )
```

profile of v0, /device:TPU:17, one launch (start us, length us, event | category | flops | bytes accessed | tf_op | source)
XLA Modules:
  0.0 751.4 jit_solution(3528943055285936381)
XLA Ops:
  8.4 1.6 convolution_convert_fusion.5
  10.1 11.0 %all_to_all.36 = bf16[4,16,4096]{2,1,0:T(8,128)(2,1)S(1)} all-to-all(bf16[4,16,4096]{2,1,0:T(8,128)(2,1)S(1)} %reshape.413), channel_id=1, replica_groups=mesh['pipe'=8,'expert'=4] {'expert'}, dimensions={0} | all-to-all | bytes 1048576 | tf_op jit(solution)/shard_map/all_to_all | solution.py:127
  21.1 2.3 fusion.18
  23.4 1.1 multiply_convert_fusion.1
  24.5 1.3 convolution_convert_fusion.3
  25.8 5.1 all-to-all-start.6
  30.9 1.6 fusion.43
  33.2 5.8 all-to-all-done.6
  39.0 1.1 convert_reduce_fusion
  40.1 1.6 multiply_reduce_fusion
  42.6 1.8 convolution_bitcast_fusion
  44.6 6.3 all_to_all.37
  51.7 4.1 all-to-all-start.3
  55.9 7.9 %all-to-all-done.3 = bf16[4,16,4096]{2,1,0:T(8,128)(2,1)S(1)} async-done(((bf16[4,16,4096]{2,1,0:T(8,128)(2,1)}), bf16[4,16,4096]{2,1,0:T(8,128)(2,1)S(1)}, u32[]{:S(2)}, u32[]{:S(2)}) %all-to-all-start.3) | async-done | bytes 524320 | tf_op jit(solution)/shard_map/all_to_all | solution.py:130
  64.0 1.6 multiply_convert_fusion.2
  67.6 6.3 copy.27
  73.9 1.2 fusion.40
  75.8 1.8 copy.28
  77.6 1.1 convert_element_type.224
  78.9 17.0 %pad_maximum_fusion = bf16[3276800]{0:T(1024)(128)(2,1)S(1)} fusion(bf16[131072]{0:T(1024)(128)(2,1)S(1)} %bitcast.149, bf16[1048576]{0:T(1024)(128)(2,1)} %bitcast.142, bf16[2097152]{0:T(1024)(128)(2,1)} %bitcast.140), kind=kLoop, calls=%fused_computation.1 | loop fusion | flops 19660800 | bytes 13107200 | tf_op jit(solution)/shard_map/concatenate | solution.py:205
  95.9 1.3 collective-permute-start.2
  97.2 140.5 %collective-permute-done.2 = bf16[3276800]{0:T(1024)(128)(2,1)S(1)} collective-permute-done((bf16[3276800]{0:T(1024)(128)(2,1)S(1)}, bf16[3276800]{0:T(1024)(128)(2,1)S(1)}, u32[]{:S(2)}, u32[]{:S(2)}) %collective-permute-start.2) | collective-permute-done | bytes 6553632 | tf_op jit(solution)/shard_map/ppermute | solution.py:24
  237.8 1.2 collective-permute-start.3
  239.0 139.7 %collective-permute-done.3 = bf16[3276800]{0:T(1024)(128)(2,1)} collective-permute-done((bf16[3276800]{0:T(1024)(128)(2,1)S(1)}, bf16[3276800]{0:T(1024)(128)(2,1)}, u32[]{:S(2)}, u32[]{:S(2)}) %collective-permute-start.3) | collective-permute-done | bytes 6553632 | tf_op jit(solution)/shard_map/ppermute | solution.py:24
  378.9 1.6 fusion.48
  381.7 1.4 select_reduce_fusion.4
  383.7 13.6 %all_to_all.38 = bf16[4,16,4096]{2,1,0:T(8,128)(2,1)S(1)} all-to-all(bf16[4,16,4096]{2,1,0:T(8,128)(2,1)S(1)} %reshape.408), channel_id=1, replica_groups=mesh['pipe'=8,'expert'=4] {'expert'}, dimensions={0} | all-to-all | bytes 1048576 | tf_op jit(solution)/shard_map/all_to_all | solution.py:102
  398.1 2.1 fusion.20
  400.2 4.0 convolution_convert_fusion.4
  404.1 4.1 all-to-all-start.1
  408.2 2.3 fusion.16
  410.6 3.1 fusion.6
  413.7 2.6 all-to-all-done.1
  416.3 5.0 all-to-all-start.5
  421.5 2.9 fusion.5
  424.4 1.2 collective-permute-start
  425.6 3.8 all-to-all-done.5
  429.4 1.3 convert_reduce_fusion.1
  430.7 3.2 convolution_add_fusion.1
  433.9 1.7 fusion.4
  435.6 3.3 collective-permute-start.1
  439.0 247.6 %collective-permute-done = bf16[1,128,4096]{2,1,0:T(8,128)(2,1)S(1)} collective-permute-done((bf16[1,128,4096]{2,1,0:T(8,128)(2,1)}, bf16[1,128,4096]{2,1,0:T(8,128)(2,1)S(1)}, u32[]{:S(2)}, u32[]{:S(2)}) %collective-permute-start) | collective-permute-done | bytes 1048608 | tf_op jit(solution)/shard_map/ppermute | solution.py:14
  687.6 38.0 %add_convert_fusion = bf16[3276800]{0:T(1024)(128)(2,1)S(1)} fusion(bf16[3276800]{0:T(1024)(128)(2,1)} %collective-permute-done.4, bf16[131072]{0:T(1024)(128)(2,1)S(1)} %bitcast.150, bf16[1048576]{0:T(1024)(128)(2,1)S(1)} %bitcast.143, bf16[2097152]{0:T(1024)(128)(2,1)S(1)} %bitcast.141), kind=kLoop, calls=%fused_computation | loop fusion | flops 29491200 | bytes 19660800 | tf_op jit(solution)/shard_map/convert_element_type | solution.py:215
  725.6 2.1 slice.31
  727.7 1.5 slice.32
  729.9 7.2 reshape.419
  737.1 4.2 reshape.420
  742.3 2.3 copy.32
  (93 shorter events, 12.4 us)
Async XLA Ops:
  7.2 17.3 %copy-start = (bf16[1,256,4096]{2,1,0:T(8,128)(2,1)S(1)}, bf16[1,256,4096]{2,1,0:T(8,128)(2,1)}, u32[]{:S(2)}) copy-start(bf16[1,256,4096]{2,1,0:T(8,128)(2,1)} %param.12) | copy-start | bytes 6291460
  8.1 15.3 %copy-start.6 = (bf16[1,2,4096,256]{3,2,1,0:T(8,128)(2,1)S(1)}, bf16[1,2,4096,256]{3,2,1,0:T(8,128)(2,1)}, u32[]{:S(2)}) copy-start(bf16[1,2,4096,256]{3,2,1,0:T(8,128)(2,1)} %param.11) | copy-start | bytes 12582916
  8.2 36.2 %copy-start.18 = (f32[128]{0:T(128)}, f32[128]{0:T(128)S(1)}, u32[]{:S(2)}) copy-start(f32[128]{0:T(128)S(1)} %convert_element_type.196) | copy-start | bytes 1540
  8.4 36.0 %copy-start.20 = (f32[128]{0:T(128)}, f32[128]{0:T(128)S(1)}, u32[]{:S(2)}) copy-start(f32[128]{0:T(128)S(1)} %convolution_bitcast_fusion.3) | copy-start | bytes 1540
  21.1 4.7 copy-start.8
  21.1 9.8 %copy-start.4 = (bf16[1,128,4096]{2,1,0:T(8,128)(2,1)S(1)}, bf16[1,128,4096]{2,1,0:T(8,128)(2,1)}, u32[]{:S(2)}) copy-start(bf16[1,128,4096]{2,1,0:T(8,128)(2,1)} %param.13) | copy-start | bytes 3145732
  25.8 13.2 %all-to-all-start.6 = ((bf16[4,16,4096]{2,1,0:T(8,128)(2,1)}), bf16[4,16,4096]{2,1,0:T(8,128)(2,1)}, u32[]{:S(2)}, u32[]{:S(2)}) async-start(bf16[4,16,4096]{2,1,0:T(8,128)(2,1)} %bitcast.151), calls=%async_computation.6 | async-start | bytes 1048576 | tf_op jit(solution)/shard_map/all_to_all | solution.py:167
  30.9 46.7 %reduce-scatter.2.cloned.1.call-start = ((), (), s32[]{:S(2)}) async-start(), calls=%async_computation.8 | async-start | bytes 2621440 | tf_op jit(solution)/shard_map/reduce_scatter | solution.py:204
  42.6 23.0 %copy-start.12 = (bf16[128,128]{1,0:T(8,128)(2,1)}, bf16[128,128]{1,0:T(8,128)(2,1)S(1)}, u32[]{:S(2)}) copy-start(bf16[128,128]{1,0:T(8,128)(2,1)S(1)} %select_reduce_fusion) | copy-start | bytes 98308
  44.4 21.2 %copy-start.9 = (bf16[4,16,4096]{2,1,0:T(8,128)(2,1)S(1)}, bf16[4,16,4096]{2,1,0:T(8,128)(2,1)}, u32[]{:S(2)}) copy-start(bf16[4,16,4096]{2,1,0:T(8,128)(2,1)} %copy-done.8) | copy-start | bytes 1572868
  51.7 12.1 %all-to-all-start.3 = ((bf16[4,16,4096]{2,1,0:T(8,128)(2,1)}), bf16[4,16,4096]{2,1,0:T(8,128)(2,1)S(1)}, u32[]{:S(2)}, u32[]{:S(2)}) async-start(bf16[4,16,4096]{2,1,0:T(8,128)(2,1)} %reshape.412), calls=%async_computation.3 | async-start | bytes 1048576 | tf_op jit(solution)/shard_map/all_to_all | solution.py:130
  63.8 2.6 copy-start.7
  65.6 0.8 copy-start.14
  65.6 0.8 copy-start.16
  78.9 299.9 %copy-start.23 = (s32[1,128,8]{1,2,0:T(8,128)S(1)}, s32[1,128,8]{1,2,0:T(8,128)}, u32[]{:S(2)}) copy-start(s32[1,128,8]{1,2,0:T(8,128)} %param.9) | copy-start | bytes 12292
  78.9 300.0 %copy-start.5 = (bf16[1,128,4096]{2,1,0:T(8,128)(2,1)S(1)}, bf16[1,128,4096]{2,1,0:T(8,128)(2,1)}, u32[]{:S(2)}) copy-start(bf16[1,128,4096]{2,1,0:T(8,128)(2,1)} %param.8) | copy-start | bytes 3145732
  95.9 141.8 %collective-permute-start.2 = (bf16[3276800]{0:T(1024)(128)(2,1)S(1)}, bf16[3276800]{0:T(1024)(128)(2,1)S(1)}, u32[]{:S(2)}, u32[]{:S(2)}) collective-permute-start(bf16[3276800]{0:T(1024)(128)(2,1)S(1)} %pad_maximum_fusion), channel_id=1, source_target_pairs={{0,4},{4,0},{8,12},{12,8},{16,20},{20,16},{24,28},{28,24},{1,5},{5... | collective-permute-start | bytes 19660808 | tf_op jit(solution)/shard_map/ppermute | solution.py:24
  237.8 141.0 %collective-permute-start.3 = (bf16[3276800]{0:T(1024)(128)(2,1)S(1)}, bf16[3276800]{0:T(1024)(128)(2,1)}, u32[]{:S(2)}, u32[]{:S(2)}) collective-permute-start(bf16[3276800]{0:T(1024)(128)(2,1)S(1)} %collective-permute-done.2), channel_id=1, source_target_pairs={{0,8},{8,0},{4,12},{12,4},{16,24},{24,16},{20,28},{28,20},{1,9},{9... | collective-permute-start | bytes 19660808 | tf_op jit(solution)/shard_map/ppermute | solution.py:24
  378.7 308.9 %collective-permute-start.4 = (bf16[3276800]{0:T(1024)(128)(2,1)}, bf16[3276800]{0:T(1024)(128)(2,1)}, u32[]{:S(2)}, u32[]{:S(2)}) collective-permute-start(bf16[3276800]{0:T(1024)(128)(2,1)} %collective-permute-done.3), channel_id=1, source_target_pairs={{0,16},{16,0},{4,20},{20,4},{8,24},{24,8},{12,28},{28,12},{1,17},{... | collective-permute-start | bytes 19660808 | tf_op jit(solution)/shard_map/ppermute | solution.py:24
  381.0 0.5 copy-start.22
  397.3 0.8 copy-start.10
  398.1 10.1 %copy-start.17 = (bf16[64,256]{1,0:T(8,128)(2,1)S(1)}, bf16[64,256]{1,0:T(8,128)(2,1)}, u32[]{:S(2)}) copy-start(bf16[64,256]{1,0:T(8,128)(2,1)} %copy-done.16) | copy-start | bytes 98308
  400.2 10.4 %copy-start.15 = (bf16[64,256]{1,0:T(8,128)(2,1)S(1)}, bf16[64,256]{1,0:T(8,128)(2,1)}, u32[]{:S(2)}) copy-start(bf16[64,256]{1,0:T(8,128)(2,1)} %copy-done.14) | copy-start | bytes 98308
  404.1 12.2 %all-to-all-start.1 = ((bf16[4,16,4096]{2,1,0:T(8,128)(2,1)}), bf16[4,16,4096]{2,1,0:T(8,128)(2,1)S(1)}, u32[]{:S(2)}, u32[]{:S(2)}) async-start(bf16[4,16,4096]{2,1,0:T(8,128)(2,1)} %bitcast.153), calls=%async_computation.1 | async-start | bytes 1048576 | tf_op jit(solution)/shard_map/all_to_all | solution.py:108
  408.2 13.1 %copy-start.24 = (bf16[128]{0:T(256)(128)(2,1)S(1)}, bf16[128]{0:T(256)(128)(2,1)}, u32[]{:S(2)}) copy-start(bf16[128]{0:T(256)(128)(2,1)} %get-tuple-element.9) | copy-start | bytes 772
  410.6 20.1 %copy-start.19 = (f32[128]{0:T(128)S(1)}, f32[128]{0:T(128)}, u32[]{:S(2)}) copy-start(f32[128]{0:T(128)} %copy-done.18) | copy-start | bytes 1540
  410.6 20.1 %copy-start.21 = (f32[128]{0:T(128)S(1)}, f32[128]{0:T(128)}, u32[]{:S(2)}) copy-start(f32[128]{0:T(128)} %copy-done.20) | copy-start | bytes 1540
  416.3 17.6 %copy-start.13 = (bf16[128,128]{1,0:T(8,128)(2,1)S(1)}, bf16[128,128]{1,0:T(8,128)(2,1)}, u32[]{:S(2)}) copy-start(bf16[128,128]{1,0:T(8,128)(2,1)} %copy-done.12) | copy-start | bytes 98308
  416.3 13.1 %all-to-all-start.5 = ((bf16[4,16,4096]{2,1,0:T(8,128)(2,1)}), bf16[4,16,4096]{2,1,0:T(8,128)(2,1)}, u32[]{:S(2)}, u32[]{:S(2)}) async-start(bf16[4,16,4096]{2,1,0:T(8,128)(2,1)} %bitcast.23), calls=%async_computation.5 | async-start | bytes 1048576 | tf_op jit(solution)/shard_map/all_to_all | solution.py:160
  424.4 263.3 %copy-start.3 = (bf16[32,32,8,128]{3,1,2,0:T(8,128)(2,1)S(1)}, bf16[32,32,8,128]{3,1,2,0:T(8,128)(2,1)}, u32[]{:S(2)}) copy-start(bf16[32,32,8,128]{3,1,2,0:T(8,128)(2,1)} %copy.28) | copy-start | bytes 6291460
  424.4 262.2 %collective-permute-start = (bf16[1,128,4096]{2,1,0:T(8,128)(2,1)}, bf16[1,128,4096]{2,1,0:T(8,128)(2,1)S(1)}, u32[]{:S(2)}, u32[]{:S(2)}) collective-permute-start(bf16[1,128,4096]{2,1,0:T(8,128)(2,1)} %fusion.5), channel_id=1, source_target_pairs={{28,0},{0,4},{4,8},{8,12},{12,16},{16,20},{20,24},{24,28},{29,1},{... | collective-permute-start | bytes 3145736 | tf_op jit(solution)/shard_map/ppermute | solution.py:14
  429.4 258.3 %copy-start.2 = (bf16[1024,2,8,128]{3,1,2,0:T(2,128)(2,1)S(1)}, bf16[1024,2,8,128]{3,1,2,0:T(2,128)(2,1)}, u32[]{:S(2)}) copy-start(bf16[1024,2,8,128]{3,1,2,0:T(2,128)(2,1)} %copy.27) | copy-start | bytes 12582916
  435.6 251.0 %collective-permute-start.1 = (bf16[1,128,4096]{2,1,0:T(8,128)(2,1)S(1)}, bf16[1,128,4096]{2,1,0:T(8,128)(2,1)S(1)}, u32[]{:S(2)}, u32[]{:S(2)}) collective-permute-start(bf16[1,128,4096]{2,1,0:T(8,128)(2,1)S(1)} %fusion.4), channel_id=1, source_target_pairs={{4,0},{8,4},{12,8},{16,12},{20,16},{24,20},{28,24},{0,28},{5,1},{9... | collective-permute-start | bytes 3145736 | tf_op jit(solution)/shard_map/ppermute | solution.py:14
  686.6 1.0 copy-start.11
  729.9 14.6 %copy-start.1 = (bf16[1,256,4096]{2,1,0:T(8,128)(2,1)S(1)}, bf16[1,256,4096]{2,1,0:T(8,128)(2,1)}, u32[]{:S(2)}) copy-start(bf16[1,256,4096]{2,1,0:T(8,128)(2,1)} %param.12) | copy-start | bytes 6291460
Sparse Core Ops, SparseCore 0:
  44.5 31.7 reduce-scatter.1
where the time goes:
time: 753 us; the launch traced here: 751 us
  waiting for transfers between devices  548 us (73%)
  other arithmetic  64 us (8%)
  matrix products  37 us (5%)
  local copies, waits for them, and re-layouts  31.6 us (4%)
  blocking collectives  30.9 us (4%)
  starting transfers between devices  25.5 us (3%)
  between operations  14.5 us (2%)
    ppermute x3, waiting for transfers between devices, swapped(): return lax.ppermute(block, axis, route)  280 us
    ppermute x2, waiting for transfers between devices, passed_along(): return lax.ppermute(block, axis, route)  248 us
    convert_element_type x1, other arithmetic, on_device(): (packed.astype(jnp.float32) + partner.astype(jnp.float32)).astype(jnp.bfl...  38 us
    concatenate x1, other arithmetic, on_device(): jnp.concatenate([jnp.stack([local_gate, local_up]).astype(jnp.bfloat16).r...  17 us
  transfers between devices with their start and end apart: 10, of which 7 were waited for; matrix products, arithmetic and copies ran while one was open for 6% of the time, Pallas kernels for 0%

commit v1 on v0

v1 whole, which is shorter than its diff:
```python
import jax
import jax.numpy as jnp
from jax import lax
from jax.sharding import PartitionSpec as P

contract_last = (((1,), (1,)), ((), ()))
contract_first = (((0,), (0,)), ((), ()))


def ahead(count):
    return [(i, (i + 1) % count) for i in range(count)]


def behind(count):
    return [((i + 1) % count, i) for i in range(count)]


def twins(count):
    return [(i, count - 1 - i) for i in range(count)]


def across(count, bit):
    return [(i, i ^ bit) for i in range(count)]


def bits_of(count):
    return [1 << k for k in reversed(range(count.bit_length() - 1))]


def gathered_all(block, groups):
    me = lax.axis_index("expert")
    held = block[None]
    for bit in bits_of(groups):
        other = lax.ppermute(held, "expert", across(groups, bit))
        low = (me & bit) == 0
        held = jnp.stack([jnp.where(low, held, other), jnp.where(low, other, held)])
        held = held.reshape((-1,) + block.shape)
    steps = groups.bit_length() - 1
    held = held.reshape((2,) * steps + block.shape)
    held = held.transpose(tuple(reversed(range(steps))) + tuple(range(steps, held.ndim)))
    return held.reshape((groups,) + block.shape)


def scattered_sum(parts, groups):
    me = lax.axis_index("expert")
    steps = groups.bit_length() - 1
    rest = parts.shape[1:]
    held = parts.reshape((2,) * steps + rest)
    for step in range(steps):
        bit = 1 << step
        axis = steps - 1 - step
        first, second = (jnp.squeeze(h, axis) for h in jnp.split(held, 2, axis=axis))
        low = (me & bit) == 0
        other = lax.ppermute(jnp.where(low, second, first), "expert", across(groups, bit))
        total = jnp.where(low, first, second).astype(jnp.float32) + other.astype(jnp.float32)
        held = total if step == steps - 1 else total.astype(jnp.bfloat16)
    return held


def routing(expert_ids, flight, slot_count):
    tok_rows = expert_ids.shape[0]
    named_mask = jnp.stack(
        [jnp.any(expert_ids == expert_id, axis=1) for expert_id in range(flight)]
    ).astype(jnp.float32)
    earlier = (jnp.arange(tok_rows)[:, None] < jnp.arange(tok_rows)[None, :]).astype(jnp.bfloat16)
    order_rank = jnp.dot(
        named_mask.astype(jnp.bfloat16), earlier, preferred_element_type=jnp.float32
    )
    slot_ids = jnp.arange(slot_count, dtype=jnp.float32)
    chosen = named_mask[:, None, :] * (order_rank[:, None, :] == slot_ids[None, :, None])
    return chosen.astype(jnp.bfloat16).reshape(flight * slot_count, tok_rows)


def take(select, values):
    return jnp.dot(select, values, preferred_element_type=jnp.float32).astype(jnp.bfloat16)


def gating(rows, select, expert_ids, router_table, flight):
    experts = router_table.shape[1]
    slots = select.shape[0]
    ids = jnp.dot(select, expert_ids.astype(jnp.bfloat16), preferred_element_type=jnp.float32)
    filled = jnp.sum(select.astype(jnp.float32), axis=1)
    own = jnp.repeat(jnp.arange(flight, dtype=jnp.float32), slots // flight)
    logits = jnp.dot(rows, router_table, preferred_element_type=jnp.float32)
    lanes = jnp.arange(experts, dtype=jnp.float32)
    onehot = (ids[:, :, None] == lanes[None, None, :]).astype(jnp.float32)
    chosen = jnp.sum(onehot * logits[:, None, :], axis=2)
    gate_prob = jax.nn.softmax(chosen, axis=-1)
    named = (ids == own[:, None]).astype(jnp.float32) * filled[:, None]
    weight = jnp.sum(gate_prob * named, axis=1)
    slope = gate_prob * (named - weight[:, None])
    basis = jnp.sum(slope[:, :, None] * onehot, axis=1)
    return weight.astype(jnp.bfloat16), basis


def on_device(section_in_a, route_a, router, gate_up, down_proj, section_in_b, route_b, grad_out_b):
    groups = lax.axis_size("expert")
    pipe = lax.axis_size("pipe")
    me = lax.axis_index("expert")
    wsplit = min(8, groups)
    flight = groups // wsplit
    mine = me // wsplit
    tokens_a, tokens_b, grad_out = section_in_a[0], section_in_b[0], grad_out_b[0]
    tok_rows, model_width = tokens_a.shape
    slot_count = tok_rows // 8
    slots = flight * slot_count
    router_table = router[0]
    w_gate, w_up, w_down = gate_up[0, 0], gate_up[0, 1], down_proj[0]
    hidden_width = w_gate.shape[1]
    experts = router_table.shape[1]

    relayed_a = lax.ppermute(section_in_a, "pipe", ahead(pipe))[0]
    relayed_g = lax.ppermute(grad_out_b, "pipe", behind(pipe))[0]

    select_a = routing(route_a[0], flight, slot_count)
    select_b = routing(route_b[0], flight, slot_count)
    rows_a, rows_b, rows_g = (
        take(select_a, tokens_a),
        take(select_b, tokens_b),
        take(select_b, grad_out),
    )
    away_a = lax.ppermute(select_a, "pipe", ahead(pipe))
    away_b = lax.ppermute(select_b, "pipe", behind(pipe))

    packed = jnp.concatenate([rows_b, rows_g, rows_a])
    everywhere = gathered_all(packed, groups).reshape(groups, 3, flight, slot_count, model_width)
    twin_packed = lax.ppermute(packed[: 2 * slots], "pipe", twins(pipe))
    twin_rows = gathered_all(twin_packed, groups).reshape(
        groups, 2, flight, slot_count, model_width
    )

    weight_a, _ = gating(rows_a, select_a, route_a[0], router_table, flight)
    weight_b, basis = gating(rows_b, select_b, route_b[0], router_table, flight)
    small = gathered_all(
        jnp.concatenate([basis, weight_b.astype(jnp.float32)[:, None] * jnp.ones((1, experts))], 1),
        groups,
    )
    basis_all = small[:, :, :experts].reshape(groups * slots, experts)
    weight_all = small[:, :, experts].reshape(groups, flight, slot_count)

    def of_mine(values):
        return lax.dynamic_index_in_dim(values, mine, axis=1, keepdims=False)

    def flat(values):
        return of_mine(values).reshape(groups * slot_count, -1)

    def spread(values):
        values = values.reshape(groups, 1, slot_count, -1)
        here = (jnp.arange(flight) == mine)[None, :, None, None]
        return jnp.where(here, values, jnp.zeros((), values.dtype)).reshape(groups, slots, -1)

    def front(rows):
        act_gate = jnp.dot(rows, w_gate, preferred_element_type=jnp.float32)
        act_up = jnp.dot(rows, w_up, preferred_element_type=jnp.float32)
        return act_gate, act_up

    packed_rows, packed_grads = flat(everywhere[:, 0]), flat(everywhere[:, 1])
    weights = of_mine(weight_all).reshape(-1, 1)
    act_gate, act_up = front(packed_rows)
    back = lax.dot_general(packed_grads, w_down, contract_last, preferred_element_type=jnp.float32)
    logistic = jax.nn.sigmoid(act_gate)
    hidden = act_gate * logistic * act_up
    score_part = jnp.sum(hidden * back, axis=1)
    scores = jnp.sum(gathered_all(spread(score_part[:, None])[:, :, 0], groups), axis=0)
    logits_grad = (scores.reshape(-1, 1) * basis_all).astype(jnp.bfloat16)
    d_hidden = weights * back
    d_gate = (d_hidden * act_up * logistic * (1.0 + act_gate * (1.0 - logistic))).astype(
        jnp.bfloat16
    )
    d_up = (d_hidden * act_gate * logistic).astype(jnp.bfloat16)
    weighed = (hidden * weights).astype(jnp.bfloat16)
    slot_part = (
        lax.dot_general(d_gate, w_gate, contract_last, preferred_element_type=jnp.float32)
        + lax.dot_general(d_up, w_up, contract_last, preferred_element_type=jnp.float32)
    ).astype(jnp.bfloat16)
    slot_back = scattered_sum(spread(slot_part), groups)
    my_logits_grad = lax.dynamic_index_in_dim(
        logits_grad.reshape(groups, slots, experts), me, axis=0, keepdims=False
    )
    router_back = lax.dot_general(
        my_logits_grad, router_table, contract_last, preferred_element_type=jnp.float32
    )
    sent_b = lax.ppermute(
        (slot_back + router_back).astype(jnp.bfloat16), "pipe", behind(pipe)
    )
    grad_in_b = (
        relayed_g.astype(jnp.float32)
        + lax.dot_general(away_b, sent_b, contract_first, preferred_element_type=jnp.float32)
    ).astype(jnp.bfloat16)

    gate_a, up_a = front(flat(everywhere[:, 2]))
    hidden_a = (jax.nn.silu(gate_a) * up_a).astype(jnp.bfloat16)
    part_a = jnp.dot(hidden_a, w_down, preferred_element_type=jnp.float32).astype(jnp.bfloat16)
    out_a = scattered_sum(spread(part_a), groups)
    sent_a = lax.ppermute(
        (out_a * weight_a.astype(jnp.float32)[:, None]).astype(jnp.bfloat16), "pipe", ahead(pipe)
    )
    section_out_a = (
        relayed_a.astype(jnp.float32)
        + lax.dot_general(away_a, sent_a, contract_first, preferred_element_type=jnp.float32)
    ).astype(jnp.bfloat16)

    factors = jnp.concatenate([d_gate, d_up, weighed], axis=1)
    twin_factors = lax.ppermute(factors, "pipe", twins(pipe))
    twin_logits_grad = lax.ppermute(logits_grad, "pipe", twins(pipe))
    both_rows = jnp.concatenate([packed_rows, flat(twin_rows[:, 0])])
    both_grads = jnp.concatenate([packed_grads, flat(twin_rows[:, 1])])
    both_factors = jnp.concatenate([factors, twin_factors])
    grad_gate_up = jnp.stack(
        [
            lax.dot_general(
                both_rows,
                both_factors[:, k * hidden_width : (k + 1) * hidden_width],
                contract_first,
                preferred_element_type=jnp.float32,
            ).astype(jnp.bfloat16)
            for k in range(2)
        ]
    )
    grad_down = lax.dot_general(
        both_factors[:, 2 * hidden_width :],
        both_grads,
        contract_first,
        preferred_element_type=jnp.float32,
    ).astype(jnp.bfloat16)
    share = model_width // groups
    all_rows = jnp.concatenate([everywhere[:, 0], twin_rows[:, 0]]).reshape(-1, model_width)
    grad_router = lax.dot_general(
        lax.dynamic_slice_in_dim(all_rows, me * share, share, axis=1),
        jnp.concatenate([logits_grad, twin_logits_grad]),
        contract_first,
        preferred_element_type=jnp.float32,
    ).astype(jnp.bfloat16)
    return (
        section_out_a[None],
        grad_in_b[None],
        grad_gate_up[None],
        grad_down[None],
        grad_router[None],
    )


def solution(mesh):
    return jax.shard_map(
        on_device,
        mesh=mesh,
        in_specs=(
            P("pipe", "expert", None),
            P("pipe", "expert", None),
            P("pipe", None, None),
            P("pipe", None, None, "expert"),
            P("pipe", "expert", None),
            P("pipe", "expert", None),
            P("pipe", "expert", None),
            P("pipe", "expert", None),
        ),
        out_specs=(
            P("pipe", "expert", None),
            P("pipe", "expert", None),
            P("pipe", None, None, "expert"),
            P("pipe", "expert", None),
            P("pipe", "expert", None),
        ),
        check_vma=False,
    )
```

time: 753 us -> 128 us (0.17)
  the two profiles are of different devices: /device:TPU:17 before, /device:TPU:0 now
where the time goes in v1:
time: 128 us; the launch traced here: 127 us
  waiting for transfers between devices  33.5 us (26%)
  matrix products  31 us (24%)
  starting transfers between devices  29.5 us (23%)
  other arithmetic  24 us (19%)
  local copies, waits for them, and re-layouts  7.77 us (6%)
    ppermute x1, waiting for transfers between devices, on_device(): twin_packed = lax.ppermute(packed[:2 * slots], 'pipe', twins(pipe))  12.4 us
    ppermute x4, waiting for transfers between devices, scattered_sum(): lax.ppermute(jnp.where(low, second, first), 'expert', across(groups, bit))  8.24 us
    ppermute x8, waiting for transfers between devices, gathered_all(): other = lax.ppermute(held, 'expert', across(groups, bit))  6.29 us
    ppermute x8, starting transfers between devices, gathered_all(): other = lax.ppermute(held, 'expert', across(groups, bit))  5.26 us
    ppermute x1, starting transfers between devices, on_device(): lax.ppermute((slot_back + router_back).astype(jnp.bfloat16), 'pipe', behi...  4.72 us
    ppermute x1, starting transfers between devices, on_device(): twin_packed = lax.ppermute(packed[:2 * slots], 'pipe', twins(pipe))  4.7 us
    ppermute x1, starting transfers between devices, on_device(): relayed_g = lax.ppermute(grad_out_b, 'pipe', behind(pipe))[0]  4.56 us
    dot_general x3, matrix products, take(): jnp.dot(select, values, preferred_element_type=jnp.float32)  4.44 us
  transfers between devices with their start and end apart: 21, of which 9 were waited for; matrix products, arithmetic and copies ran while one was open for 39% of the time, Pallas kernels for 0%

profile of v1, /device:TPU:0, one launch (start us, length us, event | category | flops | bytes accessed | tf_op | source)
XLA Modules:
  0.0 126.9 jit_solution(14842191069513801355)
XLA Ops:
  0.7 0.9 compare_reduce_fusion
  1.7 0.8 fusion.72
  2.6 1.5 %convolution_convert_fusion.6 = bf16[16,4096]{1,0:T(8,128)(2,1)S(1)} fusion(bf16[1,128,4096]{2,1,0:T(8,128)(2,1)} %param.13, bf16[128]{0:T(256)(128)(2,1)S(1)} %convert_element_type.221, f32[128]{0:T(128)S(1)} %convolution_bitcast_fusion), kind=kOutput, calls=%fused_computation.13 | convolution fusion | flops 16846848 | bytes 1180416 | tf_op jit(solution)/shard_map/dot_general | solution.py:75
  4.1 1.5 %fusion.44 = f32[16,128]{1,0:T(8,128)S(1)} fusion(bf16[16,4096]{1,0:T(8,128)(2,1)S(1)} %convolution_convert_fusion.6, bf16[1,4096,128]{2,1,0:T(8,128)(2,1)} %param.10), kind=kOutput, calls=%fused_computation.56 | convolution fusion | flops 16777216 | bytes 1187840 | tf_op jit(solution)/shard_map/dot_general | solution.py:84
  6.9 2.9 %collective-permute-start.9 = (f32[1,16,256]{2,1,0:T(8,128)}, f32[1,16,256]{2,1,0:T(8,128)}, u32[]{:S(2)}, u32[]{:S(2)}) collective-permute-start(f32[1,16,256]{2,1,0:T(8,128)} %maximum_bitcast_fusion.8), channel_id=1, source_target_pairs={{0,2},{1,3},{2,0},{3,1},{4,6},{5,7},{6,4},{7,5},{8,10},{9,11},{10,... | collective-permute-start | bytes 49160 | tf_op jit(solution)/shard_map/ppermute | solution.py:34
  9.9 4.6 %collective-permute-start.7 = (bf16[1,128,4096]{2,1,0:T(8,128)(2,1)}, bf16[1,128,4096]{2,1,0:T(8,128)(2,1)}, u32[]{:S(2)}, u32[]{:S(2)}) collective-permute-start(bf16[1,128,4096]{2,1,0:T(8,128)(2,1)} %param.15), channel_id=1, source_target_pairs={{4,0},{8,4},{12,8},{16,12},{20,16},{24,20},{28,24},{0,28},{5,1},{9... | collective-permute-start | bytes 3145736 | tf_op jit(solution)/shard_map/ppermute | solution.py:113
  14.4 1.5 %convolution_convert_fusion.5 = bf16[16,4096]{1,0:T(8,128)(2,1)S(1)} fusion(bf16[1,128,4096]{2,1,0:T(8,128)(2,1)} %param.15, bf16[128]{0:T(256)(128)(2,1)S(1)} %convert_element_type.221, f32[128]{0:T(128)S(1)} %convolution_bitcast_fusion), kind=kOutput, calls=%fused_computation.12 | convolution fusion | flops 16846848 | bytes 1180416 | tf_op jit(solution)/shard_map/dot_general | solution.py:75
  16.1 1.5 %convolution_convert_fusion.4 = bf16[16,4096]{1,0:T(8,128)(2,1)S(1)} fusion(bf16[1,128,4096]{2,1,0:T(8,128)(2,1)} %param.8, bf16[128]{0:T(256)(128)(2,1)S(1)} %convert_element_type.218, f32[128]{0:T(128)S(1)} %convolution_bitcast_fusion.1), kind=kOutput, calls=%fused_computation.11 | convolution fusion | flops 16846848 | bytes 1180416 | tf_op jit(solution)/shard_map/dot_general | solution.py:75
  17.6 0.8 maximum_bitcast_fusion.5
  19.6 4.7 %collective-permute-start.16 = (bf16[32,4096]{1,0:T(8,128)(2,1)}, bf16[32,4096]{1,0:T(8,128)(2,1)}, u32[]{:S(2)}, u32[]{:S(2)}) collective-permute-start(bf16[32,4096]{1,0:T(8,128)(2,1)} %pad_maximum_fusion.4), channel_id=1, source_target_pairs={{0,28},{4,24},{8,20},{12,16},{16,12},{20,8},{24,4},{28,0},{1,29},{... | collective-permute-start | bytes 786440 | tf_op jit(solution)/shard_map/ppermute | solution.py:127
  26.6 0.9 select_reduce_fusion.2
  27.6 1.3 %convert_reduce_fusion.1 = f32[16]{0:T(128)} fusion(bf16[128]{0:T(256)(128)(2,1)} %copy-done.24, f32[128]{0:T(128)} %copy-done.25), kind=kLoop, calls=%fused_computation.133 | loop fusion | flops 8176 | bytes 832 | tf_op jit(solution)/shard_map/reduce_sum | solution.py:82
  29.0 1.3 select_convert_fusion.1
  32.8 1.2 multiply_reduce_fusion.1
  34.0 1.2 convert_element_type.364
  35.2 12.4 %collective-permute-done.16 = bf16[32,4096]{1,0:T(8,128)(2,1)} collective-permute-done((bf16[32,4096]{1,0:T(8,128)(2,1)}, bf16[32,4096]{1,0:T(8,128)(2,1)}, u32[]{:S(2)}, u32[]{:S(2)}) %collective-permute-start.16) | collective-permute-done | bytes 262176 | tf_op jit(solution)/shard_map/ppermute | solution.py:127
  48.1 0.8 select_bitcast_fusion.13
  49.7 4.6 %collective-permute-done.17 = bf16[1,32,4096]{2,1,0:T(8,128)(2,1)} collective-permute-done((bf16[1,32,4096]{2,1,0:T(8,128)(2,1)}, bf16[1,32,4096]{2,1,0:T(8,128)(2,1)}, u32[]{:S(2)}, u32[]{:S(2)}) %collective-permute-start.17) | collective-permute-done | bytes 262176 | tf_op jit(solution)/shard_map/ppermute | solution.py:34
  54.3 1.1 select_bitcast_fusion.7
  55.5 1.1 select_bitcast_fusion.5
  57.7 1.5 %collective-permute-done.3 = bf16[2,48,4096]{2,1,0:T(8,128)(2,1)S(1)} collective-permute-done((bf16[2,48,4096]{2,1,0:T(8,128)(2,1)S(1)}, bf16[2,48,4096]{2,1,0:T(8,128)(2,1)S(1)}, u32[]{:S(2)}, u32[]{:S(2)}) %collective-permute-start.3) | collective-permute-done | bytes 786464 | tf_op jit(solution)/shard_map/ppermute | solution.py:34
  59.6 1.6 %slice_bitcast_fusion.4 = (bf16[4,1,16,4096]{3,2,0,1:T(8,128)(2,1)}, bf16[4,1,1,16,4096]{4,3,1,0,2:T(8,128)(2,1)}, bf16[4,1,1,16,4096]{4,3,1,0,2:T(8,128)(2,1)},...) fusion(bf16[4,2,1,16,4096]{4,3,1,0,2:T(8,128)(2,1)S(1)} %bitcas, ...), kind=kLoop, calls=%fused_computation.195 | loop fusion | bytes 6291456 | tf_op jit(solution)/shard_map/squeeze | solution.py:206
  61.2 1.9 %copy-done.1 = bf16[1,2,4096,256]{3,2,1,0:T(8,128)(2,1)S(1)} copy-done((bf16[1,2,4096,256]{3,2,1,0:T(8,128)(2,1)S(1)}, bf16[1,2,4096,256]{3,2,1,0:T(8,128)(2,1)}, u32[]{:S(2)}) %copy-start.1) | copy-done | bytes 4194328
  64.1 0.9 multiply_reduce_fusion
  65.6 2.4 %fusion.16 = f32[64,4096]{1,0:T(8,128)S(1)} fusion(bf16[64,256]{1,0:T(8,128)(2,1)S(1)} %get-tuple-element.25, bf16[1,2,4096,256]{3,2,1,0:T(8,128)(2,1)} %param.11), kind=kOutput, calls=%fused_computation.27 | convolution fusion | flops 134217728 | bytes 3178496 | tf_op jit(solution)/shard_map/dot_general | solution.py:173
  69.2 2.6 %fusion.4 = bf16[64,4096]{1,0:T(8,128)(2,1)S(1)} fusion(f32[64,4096]{1,0:T(8,128)S(1)} %fusion.16, bf16[64,256]{1,0:T(8,128)(2,1)S(1)} %get-tuple-element.27, bf16[1,2,4096,256]{3,2,1,0:T(8,128)(2,1)} %param.11, pred[]{:T(512)S(6)} %eq.108), kind=kOutput, calls=%fused_computation.9 | convolution fusion | flops 135004160 | bytes 3702785 | tf_op jit(solution)/shard_map/dot_general | solution.py:174
  71.9 0.8 copy-done.9
  72.7 0.8 select_bitcast_fusion.8
  73.9 4.0 %fusion.5 = bf16[64,4096]{1,0:T(8,128)(2,1)} fusion(bf16[1,256,4096]{2,1,0:T(8,128)(2,1)S(1)} %copy-done, bf16[64,4096]{1,0:T(8,128)(2,1)} %bitcast.253, bf16[1,2,4096,256]{3,2,1,0:T(8,128)(2,1)} %param.11, pred[]{:T(512)S(6)} %eq.108, f32[64,256]{1,0:T(8,128)S(1)} %fusion.20), kind=kOutput, calls=%fused_computation.10 | convolution fusion | flops 269058048 | bytes 5308417 | tf_op jit(solution)/shard_map/dot_general | solution.py:193
  77.9 1.1 select_bitcast_fusion.9
  79.1 2.3 %pad_maximum_fusion.1 = bf16[8,1,16,4096]{3,2,0,1:T(8,128)(2,1)} fusion(bf16[4,1,16,4096]{3,2,0,1:T(8,128)(2,1)} %get-tuple-element.15, bf16[4,1,16,4096]{3,2,0,1:T(8,128)(2,1)} %get-tuple-element.37), kind=kLoop, calls=%fused_computation.53 | loop fusion | flops 524288 | bytes 2097152 | tf_op jit(solution)/shard_map/concatenate | solution.py:227
  81.5 3.9 %collective-permute-start.20 = (bf16[64,128]{1,0:T(8,128)(2,1)S(1)}, bf16[64,128]{1,0:T(8,128)(2,1)S(1)}, u32[]{:S(2)}, u32[]{:S(2)}) collective-permute-start(bf16[64,128]{1,0:T(8,128)(2,1)S(1)} %fusion.69), channel_id=1, source_target_pairs={{0,28},{4,24},{8,20},{12,16},{16,12},{20,8},{24,4},{28,0},{1,29},{... | collective-permute-start | bytes 49160 | tf_op jit(solution)/shard_map/ppermute | solution.py:205
  85.5 2.6 %collective-permute-done.20 = bf16[64,128]{1,0:T(8,128)(2,1)S(1)} collective-permute-done((bf16[64,128]{1,0:T(8,128)(2,1)S(1)}, bf16[64,128]{1,0:T(8,128)(2,1)S(1)}, u32[]{:S(2)}, u32[]{:S(2)}) %collective-permute-start.20) | collective-permute-done | bytes 16416 | tf_op jit(solution)/shard_map/ppermute | solution.py:205
  88.0 1.9 %fusion.28 = bf16[1,1024,128]{2,1,0:T(8,128)(2,1)} fusion(bf16[128,4096]{1,0:T(8,128)(2,1)} %bitcast.255, s32[]{:T(128)S(6)} %select_n.253, bf16[64,128]{1,0:T(8,128)(2,1)S(1)} %collective-permute-done.20, bf16[64,128]{1,0:T(8,128)(2,1)S(1)} %fusion.69), kind=kOutput, calls=%fused_computation.41 | convolution fusion | flops 33751040 | bytes 557060 | tf_op jit(solution)/shard_map/dot_general | solution.py:228
  89.9 0.9 pad_maximum_fusion.5
  90.9 1.9 %fusion = bf16[1,4096,256]{2,1,0:T(8,128)(2,1)S(1)} fusion(bf16[64,4096]{1,0:T(8,128)(2,1)} %bitcast.239, bf16[64,4096]{1,0:T(8,128)(2,1)} %bitcast.243, bf16[128,768]{1,0:T(8,128)(2,1)S(1)} %pad_maximum_fusion.5), kind=kOutput, calls=%fused_computation.3 | convolution fusion | flops 271581184 | bytes 3211264 | tf_op jit(solution)/shard_map/dot_general | solution.py:211
  93.6 2.4 %maximum_bitcast_fusion = bf16[1,2,4096,256]{3,2,1,0:T(8,128)(2,1)} fusion(bf16[1,4096,256]{2,1,0:T(8,128)(2,1)S(1)} %fusion.1, bf16[1,4096,256]{2,1,0:T(8,128)(2,1)S(1)} %fusion), kind=kLoop, calls=%fused_computation.14 | loop fusion | flops 2097152 | bytes 8388608 | tf_op jit(solution)/shard_map/broadcast_in_dim | solution.py:237
  96.0 2.0 %fusion.2 = bf16[1,256,4096]{2,1,0:T(8,128)(2,1)} fusion(bf16[64,4096]{1,0:T(8,128)(2,1)S(1)} %bitcast.252, bf16[64,4096]{1,0:T(8,128)(2,1)S(1)} %bitcast.246, bf16[128,768]{1,0:T(8,128)(2,1)S(1)} %pad_maximum_fusion.5), kind=kOutput, calls=%fused_computation.5 | convolution fusion | flops 271581184 | bytes 3211264 | tf_op jit(solution)/shard_map/dot_general | solution.py:220
  98.7 1.0 collective-permute-done.4
  99.7 1.5 %collective-permute-start.12 = (bf16[16,4096]{1,0:T(8,128)(2,1)S(1)}, bf16[16,4096]{1,0:T(8,128)(2,1)S(1)}, u32[]{:S(2)}, u32[]{:S(2)}) collective-permute-start(bf16[16,4096]{1,0:T(8,128)(2,1)S(1)} %select_bitcast_fusion.10), channel_id=1, source_target_pairs={{0,2},{1,3},{2,0},{3,1},{4,6},{5,7},{6,4},{7,5},{8,10},{9,11},{10,... | collective-permute-start | bytes 393224 | tf_op jit(solution)/shard_map/ppermute | solution.py:54
  101.3 4.1 %collective-permute-done.12 = bf16[16,4096]{1,0:T(8,128)(2,1)S(1)} collective-permute-done((bf16[16,4096]{1,0:T(8,128)(2,1)S(1)}, bf16[16,4096]{1,0:T(8,128)(2,1)S(1)}, u32[]{:S(2)}, u32[]{:S(2)}) %collective-permute-start.12) | collective-permute-done | bytes 131104 | tf_op jit(solution)/shard_map/ppermute | solution.py:54
  105.5 1.5 %collective-permute-start.5 = (bf16[16,4096]{1,0:T(8,128)(2,1)S(1)}, bf16[16,4096]{1,0:T(8,128)(2,1)S(1)}, u32[]{:S(2)}, u32[]{:S(2)}) collective-permute-start(bf16[16,4096]{1,0:T(8,128)(2,1)S(1)} %select_bitcast_fusion.11), channel_id=1, source_target_pairs={{0,2},{1,3},{2,0},{3,1},{4,6},{5,7},{6,4},{7,5},{8,10},{9,11},{10,... | collective-permute-start | bytes 393224 | tf_op jit(solution)/shard_map/ppermute | solution.py:54
  107.4 3.1 %collective-permute-done.5 = bf16[16,4096]{1,0:T(8,128)(2,1)S(1)} collective-permute-done((bf16[16,4096]{1,0:T(8,128)(2,1)S(1)}, bf16[16,4096]{1,0:T(8,128)(2,1)S(1)}, u32[]{:S(2)}, u32[]{:S(2)}) %collective-permute-start.5) | collective-permute-done | bytes 131104 | tf_op jit(solution)/shard_map/ppermute | solution.py:54
  110.4 4.7 %collective-permute-start.15 = (bf16[16,4096]{1,0:T(8,128)(2,1)S(1)}, bf16[16,4096]{1,0:T(8,128)(2,1)S(1)}, u32[]{:S(2)}, u32[]{:S(2)}) collective-permute-start(bf16[16,4096]{1,0:T(8,128)(2,1)S(1)} %fusion.54), channel_id=1, source_target_pairs={{4,0},{8,4},{12,8},{16,12},{20,16},{24,20},{28,24},{0,28},{5,1},{9... | collective-permute-start | bytes 393224 | tf_op jit(solution)/shard_map/ppermute | solution.py:183
  115.3 2.2 %collective-permute-start.6 = (bf16[16,4096]{1,0:T(8,128)(2,1)S(1)}, bf16[16,4096]{1,0:T(8,128)(2,1)S(1)}, u32[]{:S(2)}, u32[]{:S(2)}) collective-permute-start(bf16[16,4096]{1,0:T(8,128)(2,1)S(1)} %fusion.56), channel_id=1, source_target_pairs={{0,4},{4,8},{8,12},{12,16},{16,20},{20,24},{24,28},{28,0},{1,5},{5... | collective-permute-start | bytes 393224 | tf_op jit(solution)/shard_map/ppermute | solution.py:195
  117.5 4.1 %collective-permute-done.15 = bf16[16,4096]{1,0:T(8,128)(2,1)S(1)} collective-permute-done((bf16[16,4096]{1,0:T(8,128)(2,1)S(1)}, bf16[16,4096]{1,0:T(8,128)(2,1)S(1)}, u32[]{:S(2)}, u32[]{:S(2)}) %collective-permute-start.15) | collective-permute-done | bytes 131104 | tf_op jit(solution)/shard_map/ppermute | solution.py:183
  121.5 2.7 %fusion.38 = bf16[1,128,4096]{2,1,0:T(8,128)(2,1)} fusion(bf16[1,128,4096]{2,1,0:T(8,128)(2,1)} %collective-permute-done.7, bf16[16,128]{1,0:T(8,128)(2,1)} %collective-permute-done.8, bf16[16,4096]{1,0:T(8,128)(2,1)S(1)} %collective-permute-done.15), kind=kOutput, calls=%fused_computation.47 | convolution fusion | flops 18350080 | bytes 2232320 | tf_op jit(solution)/shard_map/dot_general | solution.py:188
  124.2 2.6 %fusion.37 = bf16[1,128,4096]{2,1,0:T(8,128)(2,1)} fusion(bf16[1,128,4096]{2,1,0:T(8,128)(2,1)} %collective-permute-done, bf16[16,128]{1,0:T(8,128)(2,1)S(1)} %collective-permute-done.1, bf16[16,4096]{1,0:T(8,128)(2,1)S(1)} %collective-permute-done.6), kind=kOutput, calls=%fused_computation.46 | convolution fusion | flops 18350080 | bytes 2232320 | tf_op jit(solution)/shard_map/dot_general | solution.py:200
  (139 shorter events, 16.4 us)
Async XLA Ops:
  0.6 63.5 %copy-start = (bf16[1,256,4096]{2,1,0:T(8,128)(2,1)S(1)}, bf16[1,256,4096]{2,1,0:T(8,128)(2,1)}, u32[]{:S(2)}) copy-start(bf16[1,256,4096]{2,1,0:T(8,128)(2,1)} %param.12) | copy-start | bytes 6291460
  0.6 15.3 %copy-start.22 = (s32[1,128,8]{1,2,0:T(8,128)S(1)}, s32[1,128,8]{1,2,0:T(8,128)}, u32[]{:S(2)}) copy-start(s32[1,128,8]{1,2,0:T(8,128)} %param.9) | copy-start | bytes 12292
  5.6 19.3 %copy-start.3 = (bf16[1,4096,128]{2,1,0:T(8,128)(2,1)S(1)}, bf16[1,4096,128]{2,1,0:T(8,128)(2,1)}, u32[]{:S(2)}) copy-start(bf16[1,4096,128]{2,1,0:T(8,128)(2,1)} %param.10) | copy-start | bytes 3145732
  6.2 8.2 %copy-start.16 = (f32[16,128]{1,0:T(8,128)}, f32[16,128]{1,0:T(8,128)S(1)}, u32[]{:S(2)}) copy-start(f32[16,128]{1,0:T(8,128)S(1)} %select_reduce_fusion) | copy-start | bytes 24580
  6.3 8.1 %copy-start.17 = (f32[16,128]{1,0:T(8,128)}, f32[16,128]{1,0:T(8,128)S(1)}, u32[]{:S(2)}) copy-start(f32[16,128]{1,0:T(8,128)S(1)} %mul.165) | copy-start | bytes 24580
  6.9 23.8 %collective-permute-start.9 = (f32[1,16,256]{2,1,0:T(8,128)}, f32[1,16,256]{2,1,0:T(8,128)}, u32[]{:S(2)}, u32[]{:S(2)}) collective-permute-start(f32[1,16,256]{2,1,0:T(8,128)} %maximum_bitcast_fusion.8), channel_id=1, source_target_pairs={{0,2},{1,3},{2,0},{3,1},{4,6},{5,7},{6,4},{7,5},{8,10},{9,11},{10,... | collective-permute-start | bytes 49160 | tf_op jit(solution)/shard_map/ppermute | solution.py:34
  9.9 107.6 %collective-permute-start.7 = (bf16[1,128,4096]{2,1,0:T(8,128)(2,1)}, bf16[1,128,4096]{2,1,0:T(8,128)(2,1)}, u32[]{:S(2)}, u32[]{:S(2)}) collective-permute-start(bf16[1,128,4096]{2,1,0:T(8,128)(2,1)} %param.15), channel_id=1, source_target_pairs={{4,0},{8,4},{12,8},{16,12},{20,16},{24,20},{28,24},{0,28},{5,1},{9... | collective-permute-start | bytes 3145736 | tf_op jit(solution)/shard_map/ppermute | solution.py:113
  14.4 109.8 %collective-permute-start = (bf16[1,128,4096]{2,1,0:T(8,128)(2,1)}, bf16[1,128,4096]{2,1,0:T(8,128)(2,1)}, u32[]{:S(2)}, u32[]{:S(2)}) collective-permute-start(bf16[1,128,4096]{2,1,0:T(8,128)(2,1)} %param.8), channel_id=1, source_target_pairs={{0,4},{4,8},{8,12},{12,16},{16,20},{20,24},{24,28},{28,0},{1,5},{5... | collective-permute-start | bytes 3145736 | tf_op jit(solution)/shard_map/ppermute | solution.py:112
  15.9 9.3 %copy-start.23 = (s32[1,128,8]{1,2,0:T(8,128)S(1)}, s32[1,128,8]{1,2,0:T(8,128)}, u32[]{:S(2)}) copy-start(s32[1,128,8]{1,2,0:T(8,128)} %param.9) | copy-start | bytes 12292
  16.0 9.2 %copy-start.24 = (bf16[128]{0:T(256)(128)(2,1)}, bf16[128]{0:T(256)(128)(2,1)S(1)}, u32[]{:S(2)}) copy-start(bf16[128]{0:T(256)(128)(2,1)S(1)} %convert_element_type.218) | copy-start | bytes 772
  16.1 9.1 %copy-start.25 = (f32[128]{0:T(128)}, f32[128]{0:T(128)S(1)}, u32[]{:S(2)}) copy-start(f32[128]{0:T(128)S(1)} %convolution_bitcast_fusion.1) | copy-start | bytes 1540
  18.4 37.2 %collective-permute-start.2 = (bf16[1,48,4096]{2,1,0:T(8,128)(2,1)}, bf16[1,48,4096]{2,1,0:T(8,128)(2,1)}, u32[]{:S(2)}, u32[]{:S(2)}) collective-permute-start(bf16[1,48,4096]{2,1,0:T(8,128)(2,1)} %maximum_bitcast_fusion.5), channel_id=1, source_target_pairs={{0,2},{1,3},{2,0},{3,1},{4,6},{5,7},{6,4},{7,5},{8,10},{9,11},{10,... | collective-permute-start | bytes 1179656 | tf_op jit(solution)/shard_map/ppermute | solution.py:34
  19.6 27.9 %collective-permute-start.16 = (bf16[32,4096]{1,0:T(8,128)(2,1)}, bf16[32,4096]{1,0:T(8,128)(2,1)}, u32[]{:S(2)}, u32[]{:S(2)}) collective-permute-start(bf16[32,4096]{1,0:T(8,128)(2,1)} %pad_maximum_fusion.4), channel_id=1, source_target_pairs={{0,28},{4,24},{8,20},{12,16},{16,12},{20,8},{24,4},{28,0},{1,29},{... | collective-permute-start | bytes 786440 | tf_op jit(solution)/shard_map/ppermute | solution.py:127
  25.3 0.6 copy-start.19
  27.5 3.3 %copy-start.18 = (f32[16,8]{0,1:T(8,128)}, f32[16,8]{0,1:T(8,128)S(1)}, u32[]{:S(2)}) copy-start(f32[16,8]{0,1:T(8,128)S(1)} %copy.66) | copy-start | bytes 1540
  27.6 3.1 %copy-start.20 = (f32[16]{0:T(128)}, f32[16]{0:T(128)S(1)}, u32[]{:S(2)}) copy-start(f32[16]{0:T(128)S(1)} %reduce_max.18) | copy-start | bytes 196
  31.5 0.6 copy-start.15
  32.7 2.4 %collective-permute-start.10 = (f32[2,16,256]{2,1,0:T(8,128)}, f32[2,16,256]{2,1,0:T(8,128)}, u32[]{:S(2)}, u32[]{:S(2)}) collective-permute-start(f32[2,16,256]{2,1,0:T(8,128)} %maximum_bitcast_fusion.7), channel_id=1, source_target_pairs={{0,1},{1,0},{2,3},{3,2},{4,5},{5,4},{6,7},{7,6},{8,9},{9,8},{10,11... | collective-permute-start | bytes 98312 | tf_op jit(solution)/shard_map/ppermute | solution.py:34
  35.2 80.1 %collective-permute-start.8 = (bf16[16,128]{1,0:T(8,128)(2,1)}, bf16[16,128]{1,0:T(8,128)(2,1)}, u32[]{:S(2)}, u32[]{:S(2)}) collective-permute-start(bf16[16,128]{1,0:T(8,128)(2,1)} %select_convert_fusion), channel_id=1, source_target_pairs={{4,0},{8,4},{12,8},{16,12},{20,16},{24,20},{28,24},{0,28},{5,1},{9... | collective-permute-start | bytes 12296 | tf_op jit(solution)/shard_map/ppermute | solution.py:123
  47.6 6.8 %collective-permute-start.17 = (bf16[1,32,4096]{2,1,0:T(8,128)(2,1)}, bf16[1,32,4096]{2,1,0:T(8,128)(2,1)}, u32[]{:S(2)}, u32[]{:S(2)}) collective-permute-start(bf16[1,32,4096]{2,1,0:T(8,128)(2,1)} %bitcast.50), channel_id=1, source_target_pairs={{0,2},{1,3},{2,0},{3,1},{4,6},{5,7},{6,4},{7,5},{8,10},{9,11},{10,... | collective-permute-start | bytes 786440 | tf_op jit(solution)/shard_map/ppermute | solution.py:34
  55.5 2.0 %collective-permute-start.18 = (bf16[2,32,4096]{2,1,0:T(8,128)(2,1)S(1)}, bf16[2,32,4096]{2,1,0:T(8,128)(2,1)S(1)}, u32[]{:S(2)}, u32[]{:S(2)}) collective-permute-start(bf16[2,32,4096]{2,1,0:T(8,128)(2,1)S(1)} %maximum_bitcast_fusion.4), channel_id=1, source_target_pairs={{0,1},{1,0},{2,3},{3,2},{4,5},{5,4},{6,7},{7,6},{8,9},{9,8},{10,11... | collective-permute-start | bytes 1572872 | tf_op jit(solution)/shard_map/ppermute | solution.py:34
  56.8 2.5 %collective-permute-start.3 = (bf16[2,48,4096]{2,1,0:T(8,128)(2,1)S(1)}, bf16[2,48,4096]{2,1,0:T(8,128)(2,1)S(1)}, u32[]{:S(2)}, u32[]{:S(2)}) collective-permute-start(bf16[2,48,4096]{2,1,0:T(8,128)(2,1)S(1)} %maximum_bitcast_fusion.3), channel_id=1, source_target_pairs={{0,1},{1,0},{2,3},{3,2},{4,5},{5,4},{6,7},{7,6},{8,9},{9,8},{10,11... | collective-permute-start | bytes 2359304 | tf_op jit(solution)/shard_map/ppermute | solution.py:34
  59.6 3.5 %copy-start.1 = (bf16[1,2,4096,256]{3,2,1,0:T(8,128)(2,1)S(1)}, bf16[1,2,4096,256]{3,2,1,0:T(8,128)(2,1)}, u32[]{:S(2)}) copy-start(bf16[1,2,4096,256]{3,2,1,0:T(8,128)(2,1)} %param.11) | copy-start | bytes 12582916
  61.2 2.8 %copy-start.5 = (bf16[4,1,1,16,4096]{4,3,1,0,2:T(8,128)(2,1)}, bf16[4,1,1,16,4096]{4,3,1,0,2:T(8,128)(2,1)S(1)}, u32[]{:S(2)}) copy-start(bf16[4,1,1,16,4096]{4,3,1,0,2:T(8,128)(2,1)S(1)} %get-tuple-element.36) | copy-start | bytes 1572868
  61.2 2.8 %copy-start.7 = (bf16[4,1,1,16,4096]{4,3,1,0,2:T(8,128)(2,1)}, bf16[4,1,1,16,4096]{4,3,1,0,2:T(8,128)(2,1)S(1)}, u32[]{:S(2)}) copy-start(bf16[4,1,1,16,4096]{4,3,1,0,2:T(8,128)(2,1)S(1)} %get-tuple-element.35) | copy-start | bytes 1572868
  65.1 13.9 %collective-permute-start.13 = (f32[1,4,16]{2,1,0:T(4,128)S(1)}, f32[1,4,16]{2,1,0:T(4,128)S(1)}, u32[]{:S(2)}, u32[]{:S(2)}) collective-permute-start(f32[1,4,16]{2,1,0:T(4,128)S(1)} %select_n.241), channel_id=1, source_target_pairs={{0,2},{1,3},{2,0},{3,1},{4,6},{5,7},{6,4},{7,5},{8,10},{9,11},{10,... | collective-permute-start | bytes 776 | tf_op jit(solution)/shard_map/ppermute | solution.py:34
  65.6 7.8 %copy-start.13 = (bf16[4,1,1,16,4096]{4,3,1,0,2:T(8,128)(2,1)S(1)}, bf16[4,1,1,16,4096]{4,3,1,0,2:T(8,128)(2,1)}, u32[]{:S(2)}) copy-start(bf16[4,1,1,16,4096]{4,3,1,0,2:T(8,128)(2,1)} %get-tuple-element.34) | copy-start | bytes 1572868
  68.7 4.8 %copy-start.2 = (bf16[1,2,4096,256]{3,2,1,0:T(8,128)(2,1)S(1)}, bf16[1,2,4096,256]{3,2,1,0:T(8,128)(2,1)}, u32[]{:S(2)}) copy-start(bf16[1,2,4096,256]{3,2,1,0:T(8,128)(2,1)} %param.11) | copy-start | bytes 12582916
  68.7 21.3 %collective-permute-start.19 = (bf16[64,768]{1,0:T(8,128)(2,1)}, bf16[64,768]{1,0:T(8,128)(2,1)}, u32[]{:S(2)}, u32[]{:S(2)}) collective-permute-start(bf16[64,768]{1,0:T(8,128)(2,1)} %pad_maximum_fusion.6), channel_id=1, source_target_pairs={{0,28},{4,24},{8,20},{12,16},{16,12},{20,8},{24,4},{28,0},{1,29},{... | collective-permute-start | bytes 294920 | tf_op jit(solution)/shard_map/ppermute | solution.py:204
  71.9 0.8 copy-start.9
  77.9 3.6 %copy-start.14 = (f32[4,16,128]{2,1,0:T(8,128)S(1)}, f32[4,16,128]{2,1,0:T(8,128)}, u32[]{:S(2)}) copy-start(f32[4,16,128]{2,1,0:T(8,128)} %slice.56) | copy-start | bytes 98308
  77.9 10.2 %copy-start.21 = (bf16[16,128]{1,0:T(8,128)(2,1)S(1)}, bf16[16,128]{1,0:T(8,128)(2,1)}, u32[]{:S(2)}) copy-start(bf16[16,128]{1,0:T(8,128)(2,1)} %select_convert_fusion.1) | copy-start | bytes 12292
  79.0 2.3 %collective-permute-start.14 = (f32[2,4,16]{2,1,0:T(4,128)S(1)}, f32[2,4,16]{2,1,0:T(4,128)S(1)}, u32[]{:S(2)}, u32[]{:S(2)}) collective-permute-start(f32[2,4,16]{2,1,0:T(4,128)S(1)} %maximum_bitcast_fusion.9), channel_id=1, source_target_pairs={{0,1},{1,0},{2,3},{3,2},{4,5},{5,4},{6,7},{7,6},{8,9},{9,8},{10,11... | collective-permute-start | bytes 1544 | tf_op jit(solution)/shard_map/ppermute | solution.py:34
  81.5 11.3 %copy-start.4 = (bf16[4,1,1,16,4096]{4,3,1,0,2:T(8,128)(2,1)S(1)}, bf16[4,1,1,16,4096]{4,3,1,0,2:T(8,128)(2,1)}, u32[]{:S(2)}) copy-start(bf16[4,1,1,16,4096]{4,3,1,0,2:T(8,128)(2,1)} %get-tuple-element.17) | copy-start | bytes 1572868
  81.5 11.3 %copy-start.6 = (bf16[4,1,1,16,4096]{4,3,1,0,2:T(8,128)(2,1)S(1)}, bf16[4,1,1,16,4096]{4,3,1,0,2:T(8,128)(2,1)}, u32[]{:S(2)}) copy-start(bf16[4,1,1,16,4096]{4,3,1,0,2:T(8,128)(2,1)} %copy-done.5) | copy-start | bytes 1572868
  81.5 6.5 %collective-permute-start.20 = (bf16[64,128]{1,0:T(8,128)(2,1)S(1)}, bf16[64,128]{1,0:T(8,128)(2,1)S(1)}, u32[]{:S(2)}, u32[]{:S(2)}) collective-permute-start(bf16[64,128]{1,0:T(8,128)(2,1)S(1)} %fusion.69), channel_id=1, source_target_pairs={{0,28},{4,24},{8,20},{12,16},{16,12},{20,8},{24,4},{28,0},{1,29},{... | collective-permute-start | bytes 49160 | tf_op jit(solution)/shard_map/ppermute | solution.py:205
  88.0 36.2 %collective-permute-start.1 = (bf16[16,128]{1,0:T(8,128)(2,1)S(1)}, bf16[16,128]{1,0:T(8,128)(2,1)S(1)}, u32[]{:S(2)}, u32[]{:S(2)}) collective-permute-start(bf16[16,128]{1,0:T(8,128)(2,1)S(1)} %copy-done.21), channel_id=1, source_target_pairs={{0,4},{4,8},{8,12},{12,16},{16,20},{20,24},{24,28},{28,0},{1,5},{5... | collective-permute-start | bytes 12296 | tf_op jit(solution)/shard_map/ppermute | solution.py:122
  89.9 8.1 %collective-permute-start.11 = (bf16[2,16,4096]{2,1,0:T(8,128)(2,1)}, bf16[2,16,4096]{2,1,0:T(8,128)(2,1)S(1)}, u32[]{:S(2)}, u32[]{:S(2)}) collective-permute-start(bf16[2,16,4096]{2,1,0:T(8,128)(2,1)} %select_bitcast_fusion.8), channel_id=1, source_target_pairs={{0,1},{1,0},{2,3},{3,2},{4,5},{5,4},{6,7},{7,6},{8,9},{9,8},{10,11... | collective-permute-start | bytes 786440 | tf_op jit(solution)/shard_map/ppermute | solution.py:54
  93.6 2.4 %copy-start.8 = (bf16[4,1,1,16,4096]{4,3,1,0,2:T(8,128)(2,1)S(1)}, bf16[4,1,1,16,4096]{4,3,1,0,2:T(8,128)(2,1)}, u32[]{:S(2)}) copy-start(bf16[4,1,1,16,4096]{4,3,1,0,2:T(8,128)(2,1)} %copy-done.7) | copy-start | bytes 1572868
  93.6 2.4 %copy-start.12 = (bf16[4,1,1,16,4096]{4,3,1,0,2:T(8,128)(2,1)S(1)}, bf16[4,1,1,16,4096]{4,3,1,0,2:T(8,128)(2,1)}, u32[]{:S(2)}) copy-start(bf16[4,1,1,16,4096]{4,3,1,0,2:T(8,128)(2,1)} %get-tuple-element.16) | copy-start | bytes 1572868
  96.0 2.6 %copy-start.10 = (bf16[64,4096]{1,0:T(8,128)(2,1)S(1)}, bf16[64,4096]{1,0:T(8,128)(2,1)}, u32[]{:S(2)}) copy-start(bf16[64,4096]{1,0:T(8,128)(2,1)} %copy-done.9) | copy-start | bytes 1572868
  96.0 5.2 %copy-start.11 = (bf16[64,4096]{1,0:T(8,128)(2,1)S(1)}, bf16[64,4096]{1,0:T(8,128)(2,1)}, u32[]{:S(2)}) copy-start(bf16[64,4096]{1,0:T(8,128)(2,1)} %fusion.5) | copy-start | bytes 1572868
  98.0 17.1 %copy-start.26 = (f32[16]{0:T(128)S(1)}, f32[16]{0:T(128)}, u32[]{:S(2)}) copy-start(f32[16]{0:T(128)} %convert_element_type.364) | copy-start | bytes 196
  98.0 1.7 %collective-permute-start.4 = (bf16[2,16,4096]{2,1,0:T(8,128)(2,1)S(1)}, bf16[2,16,4096]{2,1,0:T(8,128)(2,1)S(1)}, u32[]{:S(2)}, u32[]{:S(2)}) collective-permute-start(bf16[2,16,4096]{2,1,0:T(8,128)(2,1)S(1)} %select_bitcast_fusion.9), channel_id=1, source_target_pairs={{0,1},{1,0},{2,3},{3,2},{4,5},{5,4},{6,7},{7,6},{8,9},{9,8},{10,11... | collective-permute-start | bytes 786440 | tf_op jit(solution)/shard_map/ppermute | solution.py:54
  99.7 5.8 %collective-permute-start.12 = (bf16[16,4096]{1,0:T(8,128)(2,1)S(1)}, bf16[16,4096]{1,0:T(8,128)(2,1)S(1)}, u32[]{:S(2)}, u32[]{:S(2)}) collective-permute-start(bf16[16,4096]{1,0:T(8,128)(2,1)S(1)} %select_bitcast_fusion.10), channel_id=1, source_target_pairs={{0,2},{1,3},{2,0},{3,1},{4,6},{5,7},{6,4},{7,5},{8,10},{9,11},{10,... | collective-permute-start | bytes 393224 | tf_op jit(solution)/shard_map/ppermute | solution.py:54
  105.5 5.0 %collective-permute-start.5 = (bf16[16,4096]{1,0:T(8,128)(2,1)S(1)}, bf16[16,4096]{1,0:T(8,128)(2,1)S(1)}, u32[]{:S(2)}, u32[]{:S(2)}) collective-permute-start(bf16[16,4096]{1,0:T(8,128)(2,1)S(1)} %select_bitcast_fusion.11), channel_id=1, source_target_pairs={{0,2},{1,3},{2,0},{3,1},{4,6},{5,7},{6,4},{7,5},{8,10},{9,11},{10,... | collective-permute-start | bytes 393224 | tf_op jit(solution)/shard_map/ppermute | solution.py:54
  110.4 11.1 %collective-permute-start.15 = (bf16[16,4096]{1,0:T(8,128)(2,1)S(1)}, bf16[16,4096]{1,0:T(8,128)(2,1)S(1)}, u32[]{:S(2)}, u32[]{:S(2)}) collective-permute-start(bf16[16,4096]{1,0:T(8,128)(2,1)S(1)} %fusion.54), channel_id=1, source_target_pairs={{4,0},{8,4},{12,8},{16,12},{20,16},{24,20},{28,24},{0,28},{5,1},{9... | collective-permute-start | bytes 393224 | tf_op jit(solution)/shard_map/ppermute | solution.py:183
  115.3 8.9 %collective-permute-start.6 = (bf16[16,4096]{1,0:T(8,128)(2,1)S(1)}, bf16[16,4096]{1,0:T(8,128)(2,1)S(1)}, u32[]{:S(2)}, u32[]{:S(2)}) collective-permute-start(bf16[16,4096]{1,0:T(8,128)(2,1)S(1)} %fusion.56), channel_id=1, source_target_pairs={{0,4},{4,8},{8,12},{12,16},{16,20},{20,24},{24,28},{28,0},{1,5},{5... | collective-permute-start | bytes 393224 | tf_op jit(solution)/shard_map/ppermute | solution.py:195

commit v2 on v1

v2 whole, which is shorter than its diff:
```python
import functools

import jax
import jax.numpy as jnp
from jax import lax
from jax.experimental import pallas as pl
from jax.experimental.pallas import tpu as pltpu
from jax.sharding import PartitionSpec as P

F32, BF16 = jnp.float32, jnp.bfloat16
whole = pl.BlockSpec(memory_space=pltpu.VMEM)
scalar = pl.BlockSpec(memory_space=pltpu.SMEM)
last_last = (((1,), (1,)), ((), ()))
first_first = (((0,), (0,)), ((), ()))
MIB = 1 << 20


def dot(a, b, dims=(((1,), (0,)), ((), ()))):
    return lax.dot_general(a, b, dims, preferred_element_type=F32)


def ahead(count):
    return [(i, (i + 1) % count) for i in range(count)]


def behind(count):
    return [((i + 1) % count, i) for i in range(count)]


def twins(count):
    return [(i, count - 1 - i) for i in range(count)]


def exchanged(block, bit):
    count = lax.axis_size("expert")
    return lax.ppermute(block, "expert", [(i, i ^ bit) for i in range(count)])


def call(kernel, outs, args, limit=32, cost=None, **more):
    return pl.pallas_call(
        kernel,
        out_shape=[jax.ShapeDtypeStruct(shape, dtype) for shape, dtype in outs],
        compiler_params=pltpu.CompilerParams(vmem_limit_bytes=limit * MIB),
        cost_estimate=pl.CostEstimate(flops=cost[0], bytes_accessed=cost[1], transcendentals=0),
        **more,
    )(*args)


def slot_select(ids, flight, slot_count):
    tokens = ids.shape[1]
    earlier = (
        lax.broadcasted_iota(jnp.int32, (tokens, tokens), 0)
        < lax.broadcasted_iota(jnp.int32, (tokens, tokens), 1)
    ).astype(F32).astype(BF16)
    slot_ids = lax.broadcasted_iota(jnp.int32, (slot_count, tokens), 0).astype(F32)
    picked = []
    for f in range(flight):
        named = jnp.max((ids == f).astype(F32), axis=0, keepdims=True)
        named = jnp.broadcast_to(named, (slot_count, tokens))
        rank = dot(named.astype(BF16), earlier)
        picked.append(jnp.where(rank == slot_ids, named, 0.0))
    return jnp.concatenate(picked, axis=0).astype(BF16)


def pick_kernel(flight, slot_count, ids_a, ids_b, x_a, x_b, grad, packed, twin, sel_a, sel_b):
    width = x_a.shape[1]
    tokens = x_a.shape[0]
    for ids_ref, select_ref, sources in ((ids_b, sel_b, ((0, x_b), (1, grad))), (ids_a, sel_a, ((2, x_a),))):
        ids = ids_ref[...]
        select = slot_select(ids, flight, slot_count)
        select_ref[...] = select
        spare = jnp.zeros((packed.shape[2] - width - ids.shape[0], tokens), F32)
        lanes = jnp.concatenate([ids.astype(F32), spare], axis=0).astype(BF16)
        slot_ids = dot(select, lanes, last_last).astype(BF16)
        for place, source in sources:
            rows = dot(select, source[...]).astype(BF16)
            packed[place, :, :width] = rows
            packed[place, :, width:] = slot_ids
            if place < 2:
                twin[place] = rows


def gates(ids, logits, topk, expert):
    lanes = lax.broadcasted_iota(jnp.int32, logits.shape, 1).astype(F32)
    picks = [ids[:, k : k + 1] for k in range(topk)]
    chosen = [
        jnp.sum(jnp.where(lanes == pick, logits, 0.0), axis=1, keepdims=True) for pick in picks
    ]
    top = functools.reduce(jnp.maximum, chosen)
    powers = [jnp.exp(value - top) for value in chosen]
    scale = 1.0 / functools.reduce(jnp.add, powers)
    probs = [power * scale for power in powers]
    named = [(pick == expert).astype(F32) for pick in picks]
    weight = functools.reduce(jnp.add, [p * n for p, n in zip(probs, named)])
    basis = functools.reduce(
        jnp.add,
        [jnp.where(lanes == pick, p * (n - weight), 0.0) for pick, p, n in zip(picks, probs, named)],
    )
    return weight, basis


def expert_kernel(counts, topk, mine, *refs):
    pieces, refs = refs[: len(counts)], refs[len(counts) :]
    router, gate_up, down, keep, send, lg_part, factors, rows, grads, ids = refs
    slot_count = pieces[0].shape[2]
    width, hidden_width = gate_up.shape[1], gate_up.shape[2]
    blocks = sum(counts)
    half = blocks * slot_count
    place = 0
    for piece, count in zip(pieces, counts):
        for j in range(count):
            here = pl.ds(place * slot_count, slot_count)
            there = pl.ds(half + place * slot_count, slot_count)
            rows[here, :] = piece[j, 0, :, :width]
            rows[there, :] = piece[j, 2, :, :width]
            grads[here, :] = piece[j, 1, :, :width]
            ids[here, :] = piece[j, 0, :, width:].astype(F32)
            ids[there, :] = piece[j, 2, :, width:].astype(F32)
            place += 1
    expert = mine[0].astype(F32)
    logits = dot(rows[...], router[...])
    act_gate = dot(rows[...], gate_up[0])
    act_up = dot(rows[...], gate_up[1])
    back = dot(grads[...], down[...], last_last)
    weight, basis = gates(ids[...], logits, topk, expert)
    logistic = jax.nn.sigmoid(act_gate)
    hidden = act_gate * logistic * act_up
    weight_b = weight[:half]
    hidden_b, gate_b, up_b, log_b = hidden[:half], act_gate[:half], act_up[:half], logistic[:half]
    lg_part[...] = (
        jnp.sum(hidden_b * back, axis=1, keepdims=True) * basis[:half]
    ).reshape(lg_part.shape)
    d_hidden = weight_b * back
    d_gate = (d_hidden * up_b * log_b * (1.0 + gate_b * (1.0 - log_b))).astype(BF16)
    d_up = (d_hidden * gate_b * log_b).astype(BF16)
    factors[:, :hidden_width] = d_gate
    factors[:, hidden_width : 2 * hidden_width] = d_up
    factors[:, 2 * hidden_width :] = (weight_b * hidden_b).astype(BF16)
    hidden_a = (weight[half:] * hidden[half:]).astype(BF16)
    step = min(width, 512)
    for first in range(0, width, step):
        cols = slice(first, first + step)
        part_a = dot(hidden_a, down[:, cols]).astype(BF16)
        part_b = (
            dot(d_gate, gate_up[0, cols, :], last_last) + dot(d_up, gate_up[1, cols, :], last_last)
        ).astype(BF16)
        for j in range(blocks):
            out, k = (keep, j) if j < blocks // 2 else (send, j - blocks // 2)
            here = slice(j * slot_count, (j + 1) * slot_count)
            out[k, :, cols] = part_a[here]
            out[k, :, first + width : first + width + step] = part_b[here]


def flipped_sum(lg, lg_in, blocks, span):
    return [lg[j] + lg_in[j ^ span] for j in range(blocks)]


def middle_kernel(span, keep, recv, lg, lg_in, keep_out, send_out, lg_out):
    count = keep.shape[0] // 2
    for j in range(keep.shape[0]):
        total = (keep[j].astype(F32) + recv[j].astype(F32)).astype(BF16)
        if j < count:
            keep_out[j] = total
        else:
            send_out[j - count] = total
    for j, value in enumerate(flipped_sum(lg, lg_in, lg.shape[0], span)):
        lg_out[j] = value


def last_kernel(span, keep, recv, lg, lg_in, router, factors, sel_a, sel_b, out_a, out_b, wide):
    width = router.shape[0]
    total = keep[0].astype(F32) + recv[0].astype(F32)
    sums = [value.astype(BF16) for value in flipped_sum(lg, lg_in, lg.shape[0], span)]
    out_a[:, :width] = total[:, :width].astype(BF16)
    out_a[:, width:] = sel_a[...]
    out_b[:, :width] = (total[:, width:] + dot(sums[0], router[...], last_last)).astype(BF16)
    out_b[:, width:] = sel_b[...]
    slot_count = factors.shape[0] // lg.shape[0]
    core = factors.shape[1]
    experts = router.shape[1]
    for j, value in enumerate(sums):
        wide[j, :, :core] = factors[j * slot_count : (j + 1) * slot_count, :]
        for f in range(value.shape[0] // slot_count):
            wide[j, :, core + f * experts : core + (f + 1) * experts] = value[
                f * slot_count : (f + 1) * slot_count
            ]


def grads_kernel(own_counts, width, hidden_width, experts, same, me, *refs):
    count = len(own_counts)
    own, twin, refs = refs[:count], refs[count : 2 * count], refs[2 * count :]
    own_all, twin_all = own, twin
    if not same:
        own_all, twin_all, refs = refs[:count], refs[count : 2 * count], refs[2 * count :]
    own_wide, twin_wide, gate_up, down, router = refs
    i = pl.program_id(0)
    tile, share_tile = down.shape[1], router.shape[0]
    share = share_tile * pl.num_programs(0)
    cols = pl.ds(pl.multiple_of(i * tile, tile), tile)
    mine = pl.ds(pl.multiple_of(me[0] * share + i * share_tile, 128), share_tile)

    def stacked(groups, which, where):
        return jnp.concatenate(
            [p[j, which, :, where] for pieces in groups for p, n in zip(pieces, own_counts) for j in range(n)]
        )

    def column(first, size):
        return jnp.concatenate(
            [w[j, :, first : first + size] for w in (own_wide, twin_wide) for j in range(w.shape[0])]
        )

    core = 3 * hidden_width
    rows = stacked((own, twin), 0, cols)
    both = dot(rows, column(0, 2 * hidden_width), first_first).astype(BF16)
    gate_up[0] = both[:, :hidden_width]
    gate_up[1] = both[:, hidden_width:]
    down[...] = dot(
        column(2 * hidden_width, hidden_width), stacked((own, twin), 1, cols), first_first
    ).astype(BF16)
    flight = (own_wide.shape[2] - core) // experts
    lg = jnp.concatenate(
        [
            w[j, :, core + f * experts : core + (f + 1) * experts]
            for w in (own_wide, twin_wide)
            for j in range(w.shape[0])
            for f in range(flight)
        ]
    )
    router[...] = dot(stacked((own_all, twin_all), 0, mine), lg, first_first).astype(BF16)


def place_kernel(base, sent, select, out):
    out[...] = (base[...].astype(F32) + dot(select[...], sent[...], first_first)).astype(BF16)


def placed(base, sent):
    tokens, width = base.shape
    slots = sent.shape[0]
    tile = width // 4
    return call(
        place_kernel,
        [((tokens, width), BF16)],
        (base, sent, sent),
        cost=(2 * tokens * slots * width, 4 * tokens * width),
        grid=(width // tile,),
        in_specs=[
            pl.BlockSpec((tokens, tile), lambda i: (0, i)),
            pl.BlockSpec((slots, tile), lambda i: (0, i)),
            pl.BlockSpec((slots, tokens), lambda i: (0, width // tokens)),
        ],
        out_specs=[pl.BlockSpec((tokens, tile), lambda i: (0, i))],
    )[0]


def on_device(section_in_a, route_a, router, gate_up, down_proj, section_in_b, route_b, grad_out_b):
    groups = lax.axis_size("expert")
    pipe = lax.axis_size("pipe")
    me = lax.axis_index("expert")
    wsplit = min(8, groups)
    flight = groups // wsplit
    mine = me // wsplit
    tok_rows, width = section_in_a.shape[1:]
    topk = route_a.shape[2]
    slot_count = tok_rows // 8
    slots = flight * slot_count
    router_table = router[0]
    experts = router_table.shape[1]
    hidden_width = gate_up.shape[3]
    bits = [1 << k for k in reversed(range(groups.bit_length() - 1))]

    relayed_a = lax.ppermute(section_in_a, "pipe", ahead(pipe))[0]
    packed, twin_rows, sel_a, sel_b = call(
        functools.partial(pick_kernel, flight, slot_count),
        [
            ((3, slots, width + experts), BF16),
            ((2, slots, width), BF16),
            ((slots, tok_rows), BF16),
            ((slots, tok_rows), BF16),
        ],
        (route_a[0].T, route_b[0].T, section_in_a[0], section_in_b[0], grad_out_b[0]),
        cost=(6 * slots * tok_rows * width, 8 * tok_rows * width),
        in_specs=[whole] * 5,
        out_specs=[whole] * 4,
    )

    def everywhere(block):
        pieces = [block[None]]
        for bit in bits:
            held = pieces[0] if len(pieces) == 1 else jnp.concatenate(pieces)
            pieces.append(exchanged(held, bit))
        return pieces

    def of_mine(piece):
        if flight == 1:
            return piece
        split = piece.reshape(piece.shape[:2] + (flight, slot_count) + piece.shape[3:])
        return lax.dynamic_index_in_dim(split, mine, axis=2, keepdims=False)

    def spread(values):
        if flight == 1:
            return values
        here = (jnp.arange(flight) == mine)[None, :, None, None]
        full = jnp.where(here, values[:, None], jnp.zeros((), values.dtype))
        return full.reshape(values.shape[0], slots, values.shape[2])

    own_all = everywhere(packed)
    relayed_g = lax.ppermute(grad_out_b, "pipe", behind(pipe))[0]
    twin_all = everywhere(lax.ppermute(twin_rows, "pipe", twins(pipe)))
    own = [of_mine(p) for p in own_all]
    twin = [of_mine(p) for p in twin_all]
    counts = [p.shape[0] for p in own]
    rows_all = groups * slot_count

    keep, send, lg, factors = call(
        functools.partial(expert_kernel, counts, topk),
        [
            ((groups // 2, slot_count, 2 * width), BF16),
            ((groups // 2, slot_count, 2 * width), BF16),
            ((groups, slot_count, experts), F32),
            ((rows_all, 3 * hidden_width), BF16),
        ],
        (mine.reshape(1), *own, router_table, gate_up[0], down_proj[0]),
        cost=(20 * rows_all * width * hidden_width, 6 * width * hidden_width),
        in_specs=[scalar] + [whole] * (len(own) + 3),
        out_specs=[whole] * 4,
        scratch_shapes=[
            pltpu.VMEM((2 * rows_all, width), BF16),
            pltpu.VMEM((rows_all, width), BF16),
            pltpu.VMEM((2 * rows_all, experts), F32),
        ],
    )
    keep, send, lg = spread(keep), spread(send), spread(lg)
    for step, bit in enumerate(reversed(bits)):
        recv, lg_in = exchanged(send, bit), exchanged(lg, bit)
        span = groups >> (step + 1)
        if step < len(bits) - 1:
            half = (keep.shape[0] // 2,) + keep.shape[1:]
            keep, send, lg = call(
                functools.partial(middle_kernel, span),
                [(half, BF16), (half, BF16), (lg.shape, F32)],
                (keep, recv, lg, lg_in),
                cost=(keep.size, 6 * keep.size),
                in_specs=[whole] * 4,
                out_specs=[whole] * 3,
            )
    sent_a, sent_b, wide = call(
        functools.partial(last_kernel, span),
        [
            ((slots, width + tok_rows), BF16),
            ((slots, width + tok_rows), BF16),
            ((groups, slot_count, 3 * hidden_width + flight * experts), BF16),
        ],
        (keep, recv, lg, lg_in, router_table, factors, sel_a, sel_b),
        cost=(2 * slots * width * experts, 2 * width * experts),
        in_specs=[whole] * 8,
        out_specs=[whole] * 3,
    )
    last_b = lax.ppermute(sent_b, "pipe", behind(pipe))
    twin_wide = lax.ppermute(wide, "pipe", twins(pipe))
    last_a = lax.ppermute(sent_a, "pipe", ahead(pipe))

    share = width // groups
    tiles = min(8, share // 128)
    tile = width // tiles
    same = flight == 1
    held = (*own, *twin) if same else (*own, *twin, *own_all, *twin_all)
    grad_gate_up, grad_down, grad_router = call(
        functools.partial(grads_kernel, counts, width, hidden_width, experts, same),
        [
            ((2, width, hidden_width), BF16),
            ((hidden_width, width), BF16),
            ((share, experts), BF16),
        ],
        (me.reshape(1), *held, wide, twin_wide),
        cost=(12 * rows_all * width * hidden_width, 6 * width * hidden_width),
        grid=(tiles,),
        in_specs=[scalar] + [whole] * (len(held) + 2),
        out_specs=[
            pl.BlockSpec((2, tile, hidden_width), lambda i: (0, i, 0)),
            pl.BlockSpec((hidden_width, tile), lambda i: (0, i)),
            pl.BlockSpec((share // tiles, experts), lambda i: (i, 0)),
        ],
    )
    grad_in_b = placed(relayed_g, last_b)
    section_out_a = placed(relayed_a, last_a)
    return (
        section_out_a[None],
        grad_in_b[None],
        grad_gate_up[None],
        grad_down[None],
        grad_router[None],
    )


def solution(mesh):
    return jax.shard_map(
        on_device,
        mesh=mesh,
        in_specs=(
            P("pipe", "expert", None),
            P("pipe", "expert", None),
            P("pipe", None, None),
            P("pipe", None, None, "expert"),
            P("pipe", "expert", None),
            P("pipe", "expert", None),
            P("pipe", "expert", None),
            P("pipe", "expert", None),
        ),
        out_specs=(
            P("pipe", "expert", None),
            P("pipe", "expert", None),
            P("pipe", None, None, "expert"),
            P("pipe", "expert", None),
            P("pipe", "expert", None),
        ),
        check_vma=False,
    )
```

time: 128 us -> 99 us (0.77)
  the two profiles are of different devices: /device:TPU:0 before, /device:TPU:16 now
where the time goes in v2:
time: 99 us; the launch traced here: 98.6 us
  waiting for transfers between devices  52.7 us (53%)
  Pallas kernels  22.7 us (23%)
  starting transfers between devices  13.7 us (14%)
  local copies, waits for them, and re-layouts  6.69 us (7%)
  other arithmetic  2.05 us (2%)
    pallas_call x7, Pallas kernels, call(): pl.pallas_call(kernel, out_shape=[jax.ShapeDtypeStruct(shape, dtype) for...  22.7 us
    ppermute x8, waiting for transfers between devices, exchanged(): return lax.ppermute(block, 'expert', [(i, i ^ bit) for i in range(count)])  18.4 us
    ppermute x1, waiting for transfers between devices, on_device(): relayed_g = lax.ppermute(grad_out_b, 'pipe', behind(pipe))[0]  14 us
    ppermute x1, waiting for transfers between devices, on_device(): twin_all = everywhere(lax.ppermute(twin_rows, 'pipe', twins(pipe)))  13.9 us
    unnamed x22, local copies, waits for them, and re-layouts  6.69 us
    ppermute x8, starting transfers between devices, exchanged(): return lax.ppermute(block, 'expert', [(i, i ^ bit) for i in range(count)])  5.86 us
    ppermute x1, waiting for transfers between devices, on_device(): twin_wide = lax.ppermute(wide, 'pipe', twins(pipe))  5.04 us
    ppermute x1, starting transfers between devices, on_device(): twin_wide = lax.ppermute(wide, 'pipe', twins(pipe))  2.35 us
  transfers between devices with their start and end apart: 14, of which 7 were waited for; matrix products, arithmetic and copies ran while one was open for 1% of the time, Pallas kernels for 17%

profile of v2, /device:TPU:16, one launch (start us, length us, event | category | flops | bytes accessed | tf_op | source)
XLA Modules:
  0.0 98.6 jit_solution(9690637093190893864)
XLA Ops:
  0.6 0.0 copy-start
  0.6 0.0 copy-start.2
  0.7 1.4 %copy-done.6 = bf16[1,128,4096]{2,1,0:T(8,128)(2,1)S(1)} copy-done((bf16[1,128,4096]{2,1,0:T(8,128)(2,1)S(1)}, bf16[1,128,4096]{2,1,0:T(8,128)(2,1)}, u32[]{:S(2)}) %copy-start.6) | copy-done | bytes 1048600
  2.0 0.7 copy-done.7
  2.7 0.7 copy-done.8
  3.4 2.3 %shard_map.119 = (bf16[3,16,4224]{2,1,0:T(8,128)(2,1)S(1)}, bf16[2,16,4096]{2,1,0:T(8,128)(2,1)S(1)}, bf16[16,128]{1,0:T(8,128)(2,1)S(1)}, bf16[16,128]{1,0:T(8,128)(2,1)S(1)}) custom-call(s32[8,128]{1,0:T(8,128)S(1)} %bitcast.32, s32[8,128]{1,0:T(8,128)S(1)} %bitcast.33, bf16[128,4096]{1,0:T(8,128)(2,1)} %bitcast.6.x_a, bf16[128,4096]{1,0:T(8,128)(2,1)S(1)} %bitcast.31, ...), custom_call_target="tpu_custom_call" | custom-call | flops 50331648 | bytes 4194304 | tf_op jit(solution)/shard_map/pallas_call | solution.py:40
  5.7 1.6 %collective-permute-start.1 = (bf16[1,3,16,4224]{3,2,1,0:T(8,128)(2,1)S(1)}, bf16[1,3,16,4224]{3,2,1,0:T(8,128)(2,1)S(1)}, u32[]{:S(2)}, u32[]{:S(2)}) collective-permute-start(bf16[1,3,16,4224]{3,2,1,0:T(8,128)(2,1)S(1)} %bitcast.27), channel_id=1, source_target_pairs={{0,2},{1,3},{2,0},{3,1},{4,6},{5,7},{6,4},{7,5},{8,10},{9,11},{10,... | collective-permute-start | bytes 1216520 | tf_op jit(solution)/shard_map/ppermute | solution.py:36
  7.3 9.6 %collective-permute-done.1.refs_1_ = bf16[1,3,16,4224]{3,2,1,0:T(8,128)(2,1)S(1)} collective-permute-done((bf16[1,3,16,4224]{3,2,1,0:T(8,128)(2,1)S(1)}, bf16[1,3,16,4224]{3,2,1,0:T(8,128)(2,1)S(1)}, u32[]{:S(2)}, u32[]{:S(2)}) %collective-permute-start.1) | collective-permute-done | bytes 405536 | tf_op jit(solution)/shard_map/ppermute | solution.py:36
  16.9 1.0 pad_maximum_fusion
  17.9 0.0 copy-done.9
  17.9 0.7 copy-done.3
  18.6 0.0 collective-permute-start.2
  18.6 1.4 %collective-permute-start.10 = (bf16[2,16,4096]{2,1,0:T(8,128)(2,1)S(1)}, bf16[2,16,4096]{2,1,0:T(8,128)(2,1)}, u32[]{:S(2)}, u32[]{:S(2)}) collective-permute-start(bf16[2,16,4096]{2,1,0:T(8,128)(2,1)S(1)} %get-tuple-element.34), channel_id=1, source_target_pairs={{0,28},{4,24},{8,20},{12,16},{16,12},{20,8},{24,4},{28,0},{1,29},{... | collective-permute-start | bytes 786440 | tf_op jit(solution)/shard_map/ppermute | solution.py:308
  20.0 13.9 %collective-permute-done.10 = bf16[2,16,4096]{2,1,0:T(8,128)(2,1)} collective-permute-done((bf16[2,16,4096]{2,1,0:T(8,128)(2,1)S(1)}, bf16[2,16,4096]{2,1,0:T(8,128)(2,1)}, u32[]{:S(2)}, u32[]{:S(2)}) %collective-permute-start.10) | collective-permute-done | bytes 262176 | tf_op jit(solution)/shard_map/ppermute | solution.py:308
  34.0 1.5 %collective-permute-start.11 = (bf16[1,2,16,4096]{3,2,1,0:T(8,128)(2,1)}, bf16[1,2,16,4096]{3,2,1,0:T(8,128)(2,1)}, u32[]{:S(2)}, u32[]{:S(2)}) collective-permute-start(bf16[1,2,16,4096]{3,2,1,0:T(8,128)(2,1)} %bitcast.17.refs_3_), channel_id=1, source_target_pairs={{0,2},{1,3},{2,0},{3,1},{4,6},{5,7},{6,4},{7,5},{8,10},{9,11},{10,... | collective-permute-start | bytes 786440 | tf_op jit(solution)/shard_map/ppermute | solution.py:36
  35.5 1.4 %collective-permute-start.8 = (bf16[1,128,4096]{2,1,0:T(8,128)(2,1)}, bf16[1,128,4096]{2,1,0:T(8,128)(2,1)}, u32[]{:S(2)}, u32[]{:S(2)}) collective-permute-start(bf16[1,128,4096]{2,1,0:T(8,128)(2,1)} %param.15), channel_id=1, source_target_pairs={{4,0},{8,4},{12,8},{16,12},{20,16},{24,20},{28,24},{0,28},{5,1},{9... | collective-permute-start | bytes 3145736 | tf_op jit(solution)/shard_map/ppermute | solution.py:307
  36.9 0.6 collective-permute-start
  37.5 0.0 collective-permute-done.2.refs_2_
  37.5 0.0 copy-done.2
  37.5 0.0 copy-start.1
  37.5 2.2 %copy-done.1 = bf16[1,2,4096,256]{3,2,1,0:T(8,128)(2,1)S(1)} copy-done((bf16[1,2,4096,256]{3,2,1,0:T(8,128)(2,1)S(1)}, bf16[1,2,4096,256]{3,2,1,0:T(8,128)(2,1)}, u32[]{:S(2)}) %copy-start.1) | copy-done | bytes 4194328
  39.7 1.0 %copy-done.4 = bf16[1,3,16,4224]{3,2,1,0:T(8,128)(2,1)S(1)} copy-done((bf16[1,3,16,4224]{3,2,1,0:T(8,128)(2,1)S(1)}, bf16[1,3,16,4224]{3,2,1,0:T(8,128)(2,1)}, u32[]{:S(2)}) %copy-start.4) | copy-done | bytes 405528
  40.7 5.4 %shard_map.120 = (bf16[2,16,8192]{2,1,0:T(8,128)(2,1)S(1)}, bf16[2,16,8192]{2,1,0:T(8,128)(2,1)S(1)}, f32[4,16,128]{2,1,0:T(8,128)S(1)}, bf16[64,768]{1,0:T(8,128)(2,1)S(1)}) custom-call(s32[1]{0:T(128)} %bitcast.1.mine, bf16[1,3,16,4224]{3,2,1,0:T(8,128)(2,1)S(1)} %bitcast.29, bf16[1,3,16,4224]{3,2,1,0:T(8,128)(2,1)S(1)} %copy-done.4, ...), custom_call_target="tpu_custom_call" | custom-call | flops 1342177280 | bytes 6291456 | tf_op jit(solution)/shard_map/pallas_call | solution.py:40
  46.1 0.1 collective-permute-start.3
  46.2 0.0 collective-permute-done.11.refs_4_
  46.2 1.1 %pad_maximum_fusion.1 = bf16[2,2,16,4096]{3,2,1,0:T(8,128)(2,1)S(1)} fusion(bf16[1,2,16,4096]{3,2,1,0:T(8,128)(2,1)} %collective-permute-done.11.refs_4_, bf16[1,2,16,4096]{3,2,1,0:T(8,128)(2,1)} %bitcast.17.refs_3_), kind=kLoop, calls=%fused_computation.1 | loop fusion | flops 262144 | bytes 1048576 | tf_op jit(solution)/shard_map/concatenate | solution.py:289
  47.3 0.6 collective-permute-start.12
  47.9 0.1 collective-permute-start.4
  47.9 1.5 %collective-permute-done.4.lg_in = f32[4,16,128]{2,1,0:T(8,128)S(1)} collective-permute-done((f32[4,16,128]{2,1,0:T(8,128)S(1)}, f32[4,16,128]{2,1,0:T(8,128)S(1)}, u32[]{:S(2)}, u32[]{:S(2)}) %collective-permute-start.4) | collective-permute-done | bytes 32800 | tf_op jit(solution)/shard_map/ppermute | solution.py:36
  49.4 0.0 collective-permute-done.3.recv
  49.4 0.1 shard_map.121
  49.6 0.6 collective-permute-start.5
  50.2 1.5 %collective-permute-start.6 = (f32[4,16,128]{2,1,0:T(8,128)S(1)}, f32[4,16,128]{2,1,0:T(8,128)S(1)}, u32[]{:S(2)}, u32[]{:S(2)}) collective-permute-start(f32[4,16,128]{2,1,0:T(8,128)S(1)} %get-tuple-element.28.lg), channel_id=1, source_target_pairs={{0,2},{1,3},{2,0},{3,1},{4,6},{5,7},{6,4},{7,5},{8,10},{9,11},{10,... | collective-permute-start | bytes 98312 | tf_op jit(solution)/shard_map/ppermute | solution.py:36
  51.7 7.2 %collective-permute-done.6.lg_in = f32[4,16,128]{2,1,0:T(8,128)S(1)} collective-permute-done((f32[4,16,128]{2,1,0:T(8,128)S(1)}, f32[4,16,128]{2,1,0:T(8,128)S(1)}, u32[]{:S(2)}, u32[]{:S(2)}) %collective-permute-start.6) | collective-permute-done | bytes 32800 | tf_op jit(solution)/shard_map/ppermute | solution.py:36
  58.9 0.0 collective-permute-done.5.recv
  58.9 0.4 shard_map.122
  59.3 2.4 %collective-permute-start.13 = (bf16[4,16,896]{2,1,0:T(8,128)(2,1)S(1)}, bf16[4,16,896]{2,1,0:T(8,128)(2,1)S(1)}, u32[]{:S(2)}, u32[]{:S(2)}) collective-permute-start(bf16[4,16,896]{2,1,0:T(8,128)(2,1)S(1)} %get-tuple-element.35.refs_6_), channel_id=1, source_target_pairs={{0,28},{4,24},{8,20},{12,16},{16,12},{20,8},{24,4},{28,0},{1,29},{... | collective-permute-start | bytes 344072 | tf_op jit(solution)/shard_map/ppermute | solution.py:359
  61.7 0.6 collective-permute-start.9
  62.3 0.0 collective-permute-done.12.refs_5_
  62.3 1.4 %collective-permute-start.7 = (bf16[16,4224]{1,0:T(8,128)(2,1)S(1)}, bf16[16,4224]{1,0:T(8,128)(2,1)S(1)}, u32[]{:S(2)}, u32[]{:S(2)}) collective-permute-start(bf16[16,4224]{1,0:T(8,128)(2,1)S(1)} %get-tuple-element.32), channel_id=1, source_target_pairs={{0,4},{4,8},{8,12},{12,16},{16,20},{20,24},{24,28},{28,0},{1,5},{5... | collective-permute-start | bytes 405512 | tf_op jit(solution)/shard_map/ppermute | solution.py:360
  63.7 5.0 %collective-permute-done.13.refs_7_ = bf16[4,16,896]{2,1,0:T(8,128)(2,1)S(1)} collective-permute-done((bf16[4,16,896]{2,1,0:T(8,128)(2,1)S(1)}, bf16[4,16,896]{2,1,0:T(8,128)(2,1)S(1)}, u32[]{:S(2)}, u32[]{:S(2)}) %collective-permute-start.13) | collective-permute-done | bytes 114720 | tf_op jit(solution)/shard_map/ppermute | solution.py:359
  68.7 6.8 %shard_map.125 = (bf16[2,4096,256]{2,1,0:T(8,128)(2,1)}, bf16[256,4096]{1,0:T(8,128)(2,1)}, bf16[1024,128]{1,0:T(8,128)(2,1)}) custom-call(s32[1]{0:T(128)} %bitcast.16.me, bf16[1,3,16,4224]{3,2,1,0:T(8,128)(2,1)S(1)} %bitcast.30, bf16[1,3,16,4224]{3,2,1,0:T(8,128)(2,1)S(1)} %copy-done.5, bf16[2,3,16,4224]{3,2,1,0:T(8,128)(2,1)} %collective-permute-done.2.refs_2_, ...), custom_call_target="tpu_custom_call" | custom-call | flops 805306368 | bytes 6291456 | tf_op jit(solution)/shard_map/pallas_call | solution.py:40
  75.6 14.0 %collective-permute-done.8 = bf16[1,128,4096]{2,1,0:T(8,128)(2,1)} collective-permute-done((bf16[1,128,4096]{2,1,0:T(8,128)(2,1)}, bf16[1,128,4096]{2,1,0:T(8,128)(2,1)}, u32[]{:S(2)}, u32[]{:S(2)}) %collective-permute-start.8) | collective-permute-done | bytes 1048608 | tf_op jit(solution)/shard_map/ppermute | solution.py:307
  89.6 1.3 %collective-permute-done.9.sent.select = bf16[16,4224]{1,0:T(8,128)(2,1)S(1)} collective-permute-done((bf16[16,4224]{1,0:T(8,128)(2,1)S(1)}, bf16[16,4224]{1,0:T(8,128)(2,1)S(1)}, u32[]{:S(2)}, u32[]{:S(2)}) %collective-permute-start.9) | collective-permute-done | bytes 135200 | tf_op jit(solution)/shard_map/ppermute | solution.py:358
  90.9 3.8 %shard_map.124 = bf16[128,4096]{1,0:T(8,128)(2,1)} custom-call(bf16[128,4096]{1,0:T(8,128)(2,1)} %bitcast.14.base, bf16[16,4224]{1,0:T(8,128)(2,1)S(1)} %collective-permute-done.9.sent.select, bf16[16,4224]{1,0:T(8,128)(2,1)S(1)} %collective-permute-done.9.sent.select), custom_call_target="tpu_custom_call" | custom-call | flops 16777216 | bytes 2097152 | tf_op jit(solution)/shard_map/pallas_call | solution.py:40
  94.7 0.0 collective-permute-done
  94.7 0.0 collective-permute-done.7.sent.select
  94.7 3.8 %shard_map.123 = bf16[128,4096]{1,0:T(8,128)(2,1)} custom-call(bf16[128,4096]{1,0:T(8,128)(2,1)} %bitcast.base, bf16[16,4224]{1,0:T(8,128)(2,1)S(1)} %collective-permute-done.7.sent.select, bf16[16,4224]{1,0:T(8,128)(2,1)S(1)} %collective-permute-done.7.sent.select), custom_call_target="tpu_custom_call" | custom-call | flops 16777216 | bytes 2097152 | tf_op jit(solution)/shard_map/pallas_call | solution.py:40
  (11 shorter events, 0.0 us)
Async XLA Ops:
  0.6 36.9 %copy-start = (bf16[1,4096,128]{2,1,0:T(8,128)(2,1)S(1)}, bf16[1,4096,128]{2,1,0:T(8,128)(2,1)}, u32[]{:S(2)}) copy-start(bf16[1,4096,128]{2,1,0:T(8,128)(2,1)} %param.10) | copy-start | bytes 3145732
  0.6 36.9 %copy-start.2 = (bf16[1,256,4096]{2,1,0:T(8,128)(2,1)S(1)}, bf16[1,256,4096]{2,1,0:T(8,128)(2,1)}, u32[]{:S(2)}) copy-start(bf16[1,256,4096]{2,1,0:T(8,128)(2,1)} %param.12) | copy-start | bytes 6291460
  0.7 1.4 %copy-start.6 = (bf16[1,128,4096]{2,1,0:T(8,128)(2,1)S(1)}, bf16[1,128,4096]{2,1,0:T(8,128)(2,1)}, u32[]{:S(2)}) copy-start(bf16[1,128,4096]{2,1,0:T(8,128)(2,1)} %param.13) | copy-start | bytes 3145732
  2.0 0.7 copy-start.7
  2.7 0.7 copy-start.8
  5.7 12.2 %copy-start.9 = (bf16[16,128]{1,0:T(8,128)(2,1)}, bf16[16,128]{1,0:T(8,128)(2,1)S(1)}, u32[]{:S(2)}) copy-start(bf16[16,128]{1,0:T(8,128)(2,1)S(1)} %get-tuple-element.31.sel_b) | copy-start | bytes 12292
  5.7 11.2 %collective-permute-start.1 = (bf16[1,3,16,4224]{3,2,1,0:T(8,128)(2,1)S(1)}, bf16[1,3,16,4224]{3,2,1,0:T(8,128)(2,1)S(1)}, u32[]{:S(2)}, u32[]{:S(2)}) collective-permute-start(bf16[1,3,16,4224]{3,2,1,0:T(8,128)(2,1)S(1)} %bitcast.27), channel_id=1, source_target_pairs={{0,2},{1,3},{2,0},{3,1},{4,6},{5,7},{6,4},{7,5},{8,10},{9,11},{10,... | collective-permute-start | bytes 1216520 | tf_op jit(solution)/shard_map/ppermute | solution.py:36
  17.9 0.8 copy-start.3
  18.6 18.9 %collective-permute-start.2 = (bf16[2,3,16,4224]{3,2,1,0:T(8,128)(2,1)}, bf16[2,3,16,4224]{3,2,1,0:T(8,128)(2,1)}, u32[]{:S(2)}, u32[]{:S(2)}) collective-permute-start(bf16[2,3,16,4224]{3,2,1,0:T(8,128)(2,1)} %pad_maximum_fusion), channel_id=1, source_target_pairs={{0,1},{1,0},{2,3},{3,2},{4,5},{5,4},{6,7},{7,6},{8,9},{9,8},{10,11... | collective-permute-start | bytes 2433032 | tf_op jit(solution)/shard_map/ppermute | solution.py:36
  18.6 15.3 %collective-permute-start.10 = (bf16[2,16,4096]{2,1,0:T(8,128)(2,1)S(1)}, bf16[2,16,4096]{2,1,0:T(8,128)(2,1)}, u32[]{:S(2)}, u32[]{:S(2)}) collective-permute-start(bf16[2,16,4096]{2,1,0:T(8,128)(2,1)S(1)} %get-tuple-element.34), channel_id=1, source_target_pairs={{0,28},{4,24},{8,20},{12,16},{16,12},{20,8},{24,4},{28,0},{1,29},{... | collective-permute-start | bytes 786440 | tf_op jit(solution)/shard_map/ppermute | solution.py:308
  34.0 12.2 %collective-permute-start.11 = (bf16[1,2,16,4096]{3,2,1,0:T(8,128)(2,1)}, bf16[1,2,16,4096]{3,2,1,0:T(8,128)(2,1)}, u32[]{:S(2)}, u32[]{:S(2)}) collective-permute-start(bf16[1,2,16,4096]{3,2,1,0:T(8,128)(2,1)} %bitcast.17.refs_3_), channel_id=1, source_target_pairs={{0,2},{1,3},{2,0},{3,1},{4,6},{5,7},{6,4},{7,5},{8,10},{9,11},{10,... | collective-permute-start | bytes 786440 | tf_op jit(solution)/shard_map/ppermute | solution.py:36
  35.5 54.1 %collective-permute-start.8 = (bf16[1,128,4096]{2,1,0:T(8,128)(2,1)}, bf16[1,128,4096]{2,1,0:T(8,128)(2,1)}, u32[]{:S(2)}, u32[]{:S(2)}) collective-permute-start(bf16[1,128,4096]{2,1,0:T(8,128)(2,1)} %param.15), channel_id=1, source_target_pairs={{4,0},{8,4},{12,8},{16,12},{20,16},{24,20},{28,24},{0,28},{5,1},{9... | collective-permute-start | bytes 3145736 | tf_op jit(solution)/shard_map/ppermute | solution.py:307
  36.9 57.9 %collective-permute-start = (bf16[1,128,4096]{2,1,0:T(8,128)(2,1)}, bf16[1,128,4096]{2,1,0:T(8,128)(2,1)}, u32[]{:S(2)}, u32[]{:S(2)}) collective-permute-start(bf16[1,128,4096]{2,1,0:T(8,128)(2,1)} %param.8), channel_id=1, source_target_pairs={{0,4},{4,8},{8,12},{12,16},{16,20},{20,24},{24,28},{28,0},{1,5},{5... | collective-permute-start | bytes 3145736 | tf_op jit(solution)/shard_map/ppermute | solution.py:271
  37.5 2.2 %copy-start.1 = (bf16[1,2,4096,256]{3,2,1,0:T(8,128)(2,1)S(1)}, bf16[1,2,4096,256]{3,2,1,0:T(8,128)(2,1)}, u32[]{:S(2)}) copy-start(bf16[1,2,4096,256]{3,2,1,0:T(8,128)(2,1)} %param.11) | copy-start | bytes 12582916
  39.7 1.0 %copy-start.4 = (bf16[1,3,16,4224]{3,2,1,0:T(8,128)(2,1)S(1)}, bf16[1,3,16,4224]{3,2,1,0:T(8,128)(2,1)}, u32[]{:S(2)}) copy-start(bf16[1,3,16,4224]{3,2,1,0:T(8,128)(2,1)} %copy-done.3) | copy-start | bytes 1216516
  40.7 18.2 %copy-start.10 = (bf16[16,128]{1,0:T(8,128)(2,1)S(1)}, bf16[16,128]{1,0:T(8,128)(2,1)}, u32[]{:S(2)}) copy-start(bf16[16,128]{1,0:T(8,128)(2,1)} %copy-done.9) | copy-start | bytes 12292
  40.7 28.0 %copy-start.5 = (bf16[1,3,16,4224]{3,2,1,0:T(8,128)(2,1)S(1)}, bf16[1,3,16,4224]{3,2,1,0:T(8,128)(2,1)}, u32[]{:S(2)}) copy-start(bf16[1,3,16,4224]{3,2,1,0:T(8,128)(2,1)} %copy-done.3) | copy-start | bytes 1216516
  46.1 3.3 %collective-permute-start.3 = (bf16[2,16,8192]{2,1,0:T(8,128)(2,1)S(1)}, bf16[2,16,8192]{2,1,0:T(8,128)(2,1)S(1)}, u32[]{:S(2)}, u32[]{:S(2)}) collective-permute-start(bf16[2,16,8192]{2,1,0:T(8,128)(2,1)S(1)} %get-tuple-element.24), channel_id=1, source_target_pairs={{0,1},{1,0},{2,3},{3,2},{4,5},{5,4},{6,7},{7,6},{8,9},{9,8},{10,11... | collective-permute-start | bytes 1572872 | tf_op jit(solution)/shard_map/ppermute | solution.py:36
  47.3 15.0 %collective-permute-start.12 = (bf16[2,2,16,4096]{3,2,1,0:T(8,128)(2,1)S(1)}, bf16[2,2,16,4096]{3,2,1,0:T(8,128)(2,1)S(1)}, u32[]{:S(2)}, u32[]{:S(2)}) collective-permute-start(bf16[2,2,16,4096]{3,2,1,0:T(8,128)(2,1)S(1)} %pad_maximum_fusion.1), channel_id=1, source_target_pairs={{0,1},{1,0},{2,3},{3,2},{4,5},{5,4},{6,7},{7,6},{8,9},{9,8},{10,11... | collective-permute-start | bytes 1572872 | tf_op jit(solution)/shard_map/ppermute | solution.py:36
  47.9 1.6 %collective-permute-start.4 = (f32[4,16,128]{2,1,0:T(8,128)S(1)}, f32[4,16,128]{2,1,0:T(8,128)S(1)}, u32[]{:S(2)}, u32[]{:S(2)}) collective-permute-start(f32[4,16,128]{2,1,0:T(8,128)S(1)} %get-tuple-element.25.lg), channel_id=1, source_target_pairs={{0,1},{1,0},{2,3},{3,2},{4,5},{5,4},{6,7},{7,6},{8,9},{9,8},{10,11... | collective-permute-start | bytes 98312 | tf_op jit(solution)/shard_map/ppermute | solution.py:36
  49.6 9.4 %collective-permute-start.5 = (bf16[1,16,8192]{2,1,0:T(8,128)(2,1)S(1)}, bf16[1,16,8192]{2,1,0:T(8,128)(2,1)S(1)}, u32[]{:S(2)}, u32[]{:S(2)}) collective-permute-start(bf16[1,16,8192]{2,1,0:T(8,128)(2,1)S(1)} %get-tuple-element.27), channel_id=1, source_target_pairs={{0,2},{1,3},{2,0},{3,1},{4,6},{5,7},{6,4},{7,5},{8,10},{9,11},{10,... | collective-permute-start | bytes 786440 | tf_op jit(solution)/shard_map/ppermute | solution.py:36
  50.2 8.7 %collective-permute-start.6 = (f32[4,16,128]{2,1,0:T(8,128)S(1)}, f32[4,16,128]{2,1,0:T(8,128)S(1)}, u32[]{:S(2)}, u32[]{:S(2)}) collective-permute-start(f32[4,16,128]{2,1,0:T(8,128)S(1)} %get-tuple-element.28.lg), channel_id=1, source_target_pairs={{0,2},{1,3},{2,0},{3,1},{4,6},{5,7},{6,4},{7,5},{8,10},{9,11},{10,... | collective-permute-start | bytes 98312 | tf_op jit(solution)/shard_map/ppermute | solution.py:36
  59.3 9.4 %collective-permute-start.13 = (bf16[4,16,896]{2,1,0:T(8,128)(2,1)S(1)}, bf16[4,16,896]{2,1,0:T(8,128)(2,1)S(1)}, u32[]{:S(2)}, u32[]{:S(2)}) collective-permute-start(bf16[4,16,896]{2,1,0:T(8,128)(2,1)S(1)} %get-tuple-element.35.refs_6_), channel_id=1, source_target_pairs={{0,28},{4,24},{8,20},{12,16},{16,12},{20,8},{24,4},{28,0},{1,29},{... | collective-permute-start | bytes 344072 | tf_op jit(solution)/shard_map/ppermute | solution.py:359
  61.7 29.2 %collective-permute-start.9 = (bf16[16,4224]{1,0:T(8,128)(2,1)S(1)}, bf16[16,4224]{1,0:T(8,128)(2,1)S(1)}, u32[]{:S(2)}, u32[]{:S(2)}) collective-permute-start(bf16[16,4224]{1,0:T(8,128)(2,1)S(1)} %get-tuple-element.33), channel_id=1, source_target_pairs={{4,0},{8,4},{12,8},{16,12},{20,16},{24,20},{28,24},{0,28},{5,1},{9... | collective-permute-start | bytes 405512 | tf_op jit(solution)/shard_map/ppermute | solution.py:358
  62.3 32.4 %collective-permute-start.7 = (bf16[16,4224]{1,0:T(8,128)(2,1)S(1)}, bf16[16,4224]{1,0:T(8,128)(2,1)S(1)}, u32[]{:S(2)}, u32[]{:S(2)}) collective-permute-start(bf16[16,4224]{1,0:T(8,128)(2,1)S(1)} %get-tuple-element.32), channel_id=1, source_target_pairs={{0,4},{4,8},{8,12},{12,16},{16,20},{20,24},{24,28},{28,0},{1,5},{5... | collective-permute-start | bytes 405512 | tf_op jit(solution)/shard_map/ppermute | solution.py:360

commit v3 on v2

v3 whole, which is shorter than its diff:
```python
import functools

import jax
import jax.numpy as jnp
from jax import lax
from jax.experimental import pallas as pl
from jax.experimental.pallas import tpu as pltpu
from jax.sharding import PartitionSpec as P

F32, BF16 = jnp.float32, jnp.bfloat16
whole = pl.BlockSpec(memory_space=pltpu.VMEM)
anywhere = pl.BlockSpec(memory_space=pl.ANY)
outside = pl.BlockSpec(memory_space=pltpu.HBM)
scalar = pl.BlockSpec(memory_space=pltpu.SMEM)
last_last = (((1,), (1,)), ((), ()))
first_first = (((0,), (0,)), ((), ()))
MIB = 1 << 20


def dot(a, b, dims=(((1,), (0,)), ((), ()))):
    return lax.dot_general(a, b, dims, preferred_element_type=F32)


def near(count):
    return [(i, i ^ 1) for i in range(count)]


def far(count):
    return [(i, (i + 1 if i % 2 else i - 1) % count) for i in range(count)]


def twins(count):
    return [(i, count - 1 - i) for i in range(count)]


def exchanged(block, bit):
    count = lax.axis_size("expert")
    return lax.ppermute(block, "expert", [(i, i ^ bit) for i in range(count)])


def call(kernel, outs, args, limit=24, **more):
    return pl.pallas_call(
        kernel,
        out_shape=[jax.ShapeDtypeStruct(shape, dtype) for shape, dtype in outs],
        compiler_params=pltpu.CompilerParams(vmem_limit_bytes=limit * MIB),
        cost_estimate=pl.CostEstimate(flops=0, bytes_accessed=0, transcendentals=0),
        **more,
    )(*args)


def slot_select(ids, flight, slot_count):
    tokens = ids.shape[1]
    earlier = (
        lax.broadcasted_iota(jnp.int32, (tokens, tokens), 0)
        < lax.broadcasted_iota(jnp.int32, (tokens, tokens), 1)
    ).astype(F32).astype(BF16)
    slot_ids = lax.broadcasted_iota(jnp.int32, (slot_count, tokens), 0).astype(F32)
    picked = []
    for f in range(flight):
        named = jnp.max((ids == f).astype(F32), axis=0, keepdims=True)
        named = jnp.broadcast_to(named, (slot_count, tokens))
        rank = dot(named.astype(BF16), earlier)
        picked.append(jnp.where(rank == slot_ids, named, 0.0))
    return jnp.concatenate(picked, axis=0).astype(BF16)


def pick_kernel(flight, slot_count, topk, odd, *refs):
    sources, refs = refs[:5], refs[5:]
    packed, twin, sel_a, sel_b, to_near = refs[:5]
    held, sems = refs[5:10], refs[10]
    copies = [
        pltpu.make_async_copy(source, here, sems.at[k])
        for k, (source, here) in enumerate(zip(sources, held))
    ]
    for copy in copies:
        copy.start()
    ids_b, ids_a, x_b, grad, x_a = held
    tokens, width = x_b.shape
    lanes = packed.shape[2] - width
    for k, (ids_ref, select_ref) in enumerate(((ids_b, sel_b), (ids_a, sel_a))):
        copies[k].wait()
        ids = ids_ref[...]
        select = slot_select(ids, flight, slot_count)
        select_ref[...] = select
        spare = jnp.zeros((lanes - topk, tokens), F32)
        numbers = jnp.concatenate([ids.astype(F32), spare], axis=0).astype(BF16)
        slot_ids = dot(select, numbers, last_last).astype(BF16)
        for place, source in ((0, 2), (1, 3)) if k == 0 else ((2, 4),):
            copies[source].wait()
            if place > 0:
                @pl.when(odd[0] == (1 if place == 1 else 0))
                def _(onward=held[source]):
                    pltpu.make_async_copy(onward, to_near.at[0], sems.at[5]).start()

            rows = dot(select, held[source][...]).astype(BF16)
            packed[place, :, :width] = rows
            packed[place, :, width:] = slot_ids
            if place < 2:
                twin[place] = rows
    pltpu.make_async_copy(x_a, to_near.at[0], sems.at[5]).wait()


def order_kernel(flight, slots, odd, ids_a, ids_b, x_a, grad, first, at, far, ids, block, sems):
    for mine, ids_ref, block_ref in ((1, ids_a, x_a), (0, ids_b, grad)):

        @pl.when(odd[0] == mine)
        def _(ids_ref=ids_ref, block_ref=block_ref):
            pltpu.make_async_copy(ids_ref, ids, sems.at[0]).start()
            pltpu.make_async_copy(block_ref, block, sems.at[1]).start()

    tokens = block.shape[0]
    earlier = (
        lax.broadcasted_iota(jnp.int32, (tokens, tokens), 0)
        < lax.broadcasted_iota(jnp.int32, (tokens, tokens), 1)
    ).astype(F32).astype(BF16)
    place = lax.broadcasted_iota(jnp.int32, (tokens, tokens), 0).astype(F32)
    token = lax.broadcasted_iota(jnp.int32, (8, tokens), 1).astype(F32)
    pltpu.make_async_copy(ids_a, ids, sems.at[0]).wait()
    named = jnp.max((ids[...] < flight).astype(F32), axis=0, keepdims=True)
    named = jnp.broadcast_to(named, (8, tokens))
    rank = dot(named.astype(BF16), earlier)
    count = jnp.sum(named, axis=1, keepdims=True)
    where = jnp.where(named > 0.0, rank, count + token - rank)[:1]
    at[...] = jnp.broadcast_to(where, at.shape).astype(BF16)
    order = (place == where).astype(F32).astype(BF16)
    pltpu.make_async_copy(x_a, block, sems.at[1]).wait()
    rows = dot(order, block[...]).astype(BF16)
    first[...] = rows[:slots, :]
    far[...] = rows[slots:, :]


def gates(ids, logits, topk, expert):
    lanes = lax.broadcasted_iota(jnp.int32, logits.shape, 1).astype(F32)
    picks = [ids[:, k : k + 1] for k in range(topk)]
    chosen = [
        jnp.sum(jnp.where(lanes == pick, logits, 0.0), axis=1, keepdims=True) for pick in picks
    ]
    top = functools.reduce(jnp.maximum, chosen)
    powers = [jnp.exp(value - top) for value in chosen]
    scale = 1.0 / functools.reduce(jnp.add, powers)
    probs = [power * scale for power in powers]
    named = [(pick == expert).astype(F32) for pick in picks]
    weight = functools.reduce(jnp.add, [p * n for p, n in zip(probs, named)])
    basis = functools.reduce(
        jnp.add,
        [jnp.where(lanes == pick, p * (n - weight), 0.0) for pick, p, n in zip(picks, probs, named)],
    )
    return weight, basis


def coded(columns, lanes):
    rows = columns[0].shape[0]
    lane = lax.broadcasted_iota(jnp.int32, (rows, lanes), 1)
    out = jnp.zeros((rows, lanes), F32)
    for j, rest in enumerate(columns):
        for k in range(3):
            term = rest.astype(BF16).astype(F32)
            out = jnp.where(lane == 3 * j + k, term, out)
            rest = rest - term
    return out.astype(BF16)


def decoded(code, count):
    code = code.astype(F32)
    return [
        code[:, 3 * j : 3 * j + 1] + code[:, 3 * j + 1 : 3 * j + 2] + code[:, 3 * j + 2 : 3 * j + 3]
        for j in range(count)
    ]


def summed_scores(own, other, blocks, span, width):
    mine, theirs = decoded(own[:, width:], blocks), decoded(other[:, width:], blocks)
    return [mine[j] + theirs[j ^ span] for j in range(blocks)]


def expert_kernel(blocks, topk, mine, *refs):
    pieces, refs = refs[:blocks], refs[blocks:]
    (router, gate_up, down), refs = refs[:3], refs[3:]
    parts, refs = refs[:blocks], refs[blocks:]
    basis_out, factors, rows, grads, ids = refs
    slot_count = pieces[0].shape[1]
    width, hidden_width = gate_up.shape[1], gate_up.shape[2]
    half = blocks * slot_count
    for place in range(blocks):
        piece = pieces[place]
        here = pl.ds(place * slot_count, slot_count)
        there = pl.ds(half + place * slot_count, slot_count)
        rows[here, :] = piece[0, :, :width]
        rows[there, :] = piece[2, :, :width]
        grads[here, :] = piece[1, :, :width]
        ids[here, :] = piece[0, :, width:].astype(F32)
        ids[there, :] = piece[2, :, width:].astype(F32)
    weight, basis = gates(ids[...], dot(rows[...], router[...]), topk, mine[0].astype(F32))
    act_gate = dot(rows[...], gate_up[0])
    act_up = dot(rows[...], gate_up[1])
    back = dot(grads[...], down[...], last_last)
    logistic = jax.nn.sigmoid(act_gate)
    hidden = act_gate * logistic * act_up
    weight_b = weight[:half]
    hidden_b, gate_b, up_b, log_b = hidden[:half], act_gate[:half], act_up[:half], logistic[:half]
    basis_out[...] = basis[:half].reshape(basis_out.shape)
    scores = jnp.sum(hidden_b * back, axis=1, keepdims=True)
    code = coded(
        [scores[j * slot_count : (j + 1) * slot_count] for j in range(blocks)],
        parts[0].shape[1] - 2 * width,
    )
    d_hidden = weight_b * back
    d_gate = (d_hidden * up_b * log_b * (1.0 + gate_b * (1.0 - log_b))).astype(BF16)
    d_up = (d_hidden * gate_b * log_b).astype(BF16)
    factors[:, :hidden_width] = d_gate
    factors[:, hidden_width : 2 * hidden_width] = d_up
    factors[:, 2 * hidden_width :] = (weight_b * hidden_b).astype(BF16)
    hidden_a = (weight[half:] * hidden[half:]).astype(BF16)
    step = min(width, 512)
    for first in range(0, width, step):
        cols = slice(first, first + step)
        part_a = dot(hidden_a, down[:, cols]).astype(BF16)
        part_b = (
            dot(d_gate, gate_up[0, cols, :], last_last) + dot(d_up, gate_up[1, cols, :], last_last)
        ).astype(BF16)
        for j, part in enumerate(parts):
            here = slice(j * slot_count, (j + 1) * slot_count)
            part[:, cols] = part_a[here]
            part[:, first + width : first + width + step] = part_b[here]
    for part in parts:
        part[:, 2 * width :] = code


def added(terms, width):
    return functools.reduce(jnp.add, [term[:, :width].astype(F32) for term in terms])


def middle_kernel(blocks, span, sizes, split, own, other, *refs):
    terms, outs = refs[: sum(sizes)], refs[sum(sizes) + blocks :]
    lanes = own.shape[1] - 128
    code = coded(summed_scores(own, other, blocks, span, lanes), 128)
    for size in sizes:
        total = added(terms[:size], lanes).astype(BF16)
        if split:
            outs[0][...] = total[:, : lanes // 2]
            outs[1][:, : lanes // 2] = total[:, lanes // 2 :]
            outs[1][:, lanes // 2 :] = code
        else:
            outs[0][:, :lanes] = total
            outs[0][:, lanes:] = code
            outs = outs[1:]
        terms = terms[size:]


def last_kernel(blocks, span, count, odd, own, *refs):
    terms, refs = refs[: count - 2], refs[count - 2 :]
    last_a, last_b, basis, router, factors, sel_a, sel_b, first, at, to_near, to_far, wide = refs
    width, experts = router.shape
    slots = first.shape[0]
    total = added(terms, 2 * width)
    scores = summed_scores(own, last_b, blocks, span, width)
    sums = [(score * basis[j]).astype(BF16) for j, score in enumerate(scores)]
    more_a = total[:, :width] + last_a[...].astype(F32)
    more_b = (
        total[:, width:] + last_b[:, :width].astype(F32) + dot(sums[0], router[...], last_last)
    )
    even = odd[0] == 0
    to_near[:, :width] = jnp.where(even, more_a, more_b).astype(BF16)
    to_near[:, width:] = jnp.where(even, sel_a[...], sel_b[...])
    more = jnp.where(even, more_b, more_a)
    if slots * blocks != factors.shape[0]:
        place = lax.broadcasted_iota(jnp.int32, at.shape, 0).astype(F32)
        row = (place == at[...].astype(F32)).astype(F32).astype(BF16)
        slot = jnp.where(even, sel_b[...].astype(F32), sel_a[...].astype(F32)).astype(BF16)
        more = jnp.dot(dot(row, slot, last_last), more, precision=lax.Precision.HIGHEST)
    to_far[:, :width] = (first[...].astype(F32) + more).astype(BF16)
    to_far[:, width:] = at[...]
    slot_count = factors.shape[0] // blocks
    core = factors.shape[1]
    for j, value in enumerate(sums):
        wide[j, :, :core] = factors[j * slot_count : (j + 1) * slot_count, :]
        for f in range(value.shape[0] // slot_count):
            wide[j, :, core + f * experts : core + (f + 1) * experts] = value[
                f * slot_count : (f + 1) * slot_count
            ]


def grads_kernel(blocks, hidden_width, experts, same, me, *refs):
    pieces, refs = refs[: 2 * blocks], refs[2 * blocks :]
    pieces_all = pieces
    if not same:
        pieces_all, refs = refs[: 2 * blocks], refs[2 * blocks :]
    own_wide, twin_wide, gate_up, down, router = refs
    i = pl.program_id(0)
    tile, share_tile = down.shape[1], router.shape[0]
    share = share_tile * pl.num_programs(0)
    cols = pl.ds(pl.multiple_of(i * tile, tile), tile)
    mine = pl.ds(pl.multiple_of(me[0] * share + i * share_tile, 128), share_tile)

    def stacked(held, which, where):
        return jnp.concatenate([piece[which, :, where] for piece in held])

    def column(first, size):
        return jnp.concatenate(
            [w[j, :, first : first + size] for w in (own_wide, twin_wide) for j in range(blocks)]
        )

    core = 3 * hidden_width
    both = dot(stacked(pieces, 0, cols), column(0, 2 * hidden_width), first_first).astype(BF16)
    gate_up[0] = both[:, :hidden_width]
    gate_up[1] = both[:, hidden_width:]
    down[...] = dot(
        column(2 * hidden_width, hidden_width), stacked(pieces, 1, cols), first_first
    ).astype(BF16)
    flight = (own_wide.shape[2] - core) // experts
    lg = jnp.concatenate(
        [
            w[j, :, core + f * experts : core + (f + 1) * experts]
            for w in (own_wide, twin_wide)
            for j in range(blocks)
            for f in range(flight)
        ]
    )
    router[...] = dot(stacked(pieces_all, 0, mine), lg, first_first).astype(BF16)


def place_kernel(odd, near, last_near, last_far, far, *refs):
    outs, held, sems = refs[:2], refs[2:4], refs[4]
    tokens, width = held[0].shape
    step = width // 4
    place = lax.broadcasted_iota(jnp.int32, (tokens, tokens), 0).astype(F32)
    order = (place == last_far[:1, width:].astype(F32)).astype(F32).astype(BF16)
    select = last_near[:, width:]
    for c in range(4):
        cols = slice(c * step, (c + 1) * step)
        held[0][:, cols] = (
            near[:, cols].astype(F32) + dot(select, last_near[:, cols], first_first)
        ).astype(BF16)
        rows = jnp.concatenate([last_far[:, cols], far[:, cols]])
        held[1][:, cols] = dot(order, rows, first_first).astype(BF16)
        for k, block in enumerate(held):
            for out, from_odd in ((outs[0], k == 0), (outs[1], k == 1)):

                @pl.when((odd[0] == 1) == from_odd)
                def _(out=out, block=block, k=k, cols=cols):
                    pltpu.make_async_copy(block.at[:, cols], out.at[:, cols], sems.at[k]).start()

    for k, block in enumerate(held):
        pltpu.make_async_copy(block, outs[k], sems.at[k]).wait()


def placed(odd, near, last_near, last_far, far):
    tokens, width = near.shape
    return call(
        place_kernel,
        [((tokens, width), BF16)] * 2,
        (odd, near, last_near, last_far, far),
        in_specs=[scalar] + [whole] * 4,
        out_specs=[outside] * 2,
        scratch_shapes=[pltpu.VMEM((tokens, width), BF16)] * 2 + [pltpu.SemaphoreType.DMA((2,))],
    )


def on_device(section_in_a, route_a, router, gate_up, down_proj, section_in_b, route_b, grad_out_b):
    groups = lax.axis_size("expert")
    pipe = lax.axis_size("pipe")
    me = lax.axis_index("expert")
    wsplit = min(8, groups)
    flight = groups // wsplit
    mine = me // wsplit
    tok_rows, width = section_in_a.shape[1:]
    topk = route_a.shape[2]
    slot_count = tok_rows // 8
    slots = flight * slot_count
    router_table = router[0]
    experts = router_table.shape[1]
    hidden_width = gate_up.shape[3]
    bits = [1 << k for k in reversed(range(groups.bit_length() - 1))]

    odd = lax.axis_index("pipe") % 2
    packed, twin_rows, sel_a, sel_b, to_near = call(
        functools.partial(pick_kernel, flight, slot_count, topk),
        [
            ((3, slots, width + experts), BF16),
            ((2, slots, width), BF16),
            ((slots, tok_rows), BF16),
            ((slots, tok_rows), BF16),
            (section_in_a.shape, BF16),
        ],
        (odd.reshape(1), route_b[0].T, route_a[0].T, section_in_b[0], grad_out_b[0], section_in_a[0]),
        limit=61,
        in_specs=[scalar] + [outside] * 5,
        out_specs=[whole] * 4 + [outside],
        scratch_shapes=[pltpu.VMEM((topk, tok_rows), jnp.int32)] * 2
        + [pltpu.VMEM((tok_rows, width), BF16)] * 3
        + [pltpu.SemaphoreType.DMA((6,))],
    )

    first, at, to_far = call(
        functools.partial(order_kernel, flight, slots),
        [
            ((slots, width), BF16),
            ((slots, tok_rows), BF16),
            ((tok_rows - slots, width), BF16),
        ],
        (odd.reshape(1), route_a[0].T, route_b[0].T, section_in_a[0], grad_out_b[0]),
        limit=61,
        in_specs=[scalar] + [outside] * 4,
        out_specs=[whole] * 3,
        scratch_shapes=[
            pltpu.VMEM((topk, tok_rows), jnp.int32),
            pltpu.VMEM((tok_rows, width), BF16),
            pltpu.SemaphoreType.DMA((2,)),
        ],
    )

    def everywhere(block):
        pieces = [block]
        for bit in bits:
            pieces += [exchanged(piece, bit) for piece in pieces]
        return pieces

    def of_mine(piece):
        if flight == 1:
            return piece
        split = piece.reshape(piece.shape[0], flight, slot_count, piece.shape[2])
        return lax.dynamic_index_in_dim(split, mine, axis=1, keepdims=False)

    def spread(values):
        if flight == 1:
            return values
        here = (jnp.arange(flight) == mine)[:, None, None]
        full = jnp.where(here, values[..., None, :, :], jnp.zeros((), values.dtype))
        return full.reshape(values.shape[:-2] + (slots, values.shape[-1]))

    own_all = everywhere(packed)
    from_near = lax.ppermute(to_near, "pipe", near(pipe))[0]
    from_far = lax.ppermute(to_far, "pipe", far(pipe))
    twin_all = everywhere(lax.ppermute(twin_rows, "pipe", twins(pipe)))
    twin = [of_mine(p) for p in twin_all]
    own = [of_mine(p) for p in own_all]
    rows_all = groups * slot_count
    lanes = 2 * width + 128

    *parts, basis, factors = call(
        functools.partial(expert_kernel, groups, topk),
        [((slot_count, lanes), BF16)] * groups
        + [((groups, slot_count, experts), F32), ((rows_all, 3 * hidden_width), BF16)],
        (mine.reshape(1), *own, router_table, gate_up[0], down_proj[0]),
        in_specs=[scalar] + [whole] * (groups + 3),
        out_specs=[whole] * (groups + 2),
        scratch_shapes=[
            pltpu.VMEM((2 * rows_all, width), BF16),
            pltpu.VMEM((rows_all, width), BF16),
            pltpu.VMEM((2 * rows_all, experts), F32),
        ],
    )
    if flight > 1:
        held = jnp.concatenate([piece[0] for piece in own_all]).reshape(groups * slots, -1)
        named = jnp.tile(jnp.repeat(jnp.arange(flight), slot_count), groups)
        basis = gates(
            held[:, width:].astype(F32),
            dot(held[:, :width], router_table),
            topk,
            named.astype(F32)[:, None],
        )[1].reshape(groups, slots, experts)
    terms = [[spread(part)] for part in parts]
    span, carrier = groups, terms[0][0]
    for bit in reversed(bits):
        sums = [terms[j][0] for j in range(span // 2, span)]
        split = span == 2
        if span < groups:
            sizes = [len(terms[j]) for j in range(span // 2, span)]
            given = [term for j in range(span // 2, span) for term in terms[j]]
            sums = call(
                functools.partial(middle_kernel, groups, span, sizes, split),
                [((slots, width), BF16), ((slots, width + 128), BF16)]
                if split
                else [((slots, lanes), BF16)] * len(sizes),
                (carrier, terms[span - 1][-1], *given, *twin_all),
                in_specs=[whole] * (2 + len(given)) + [anywhere] * groups,
                out_specs=[whole] * (2 if split else len(sizes)),
            )
            carrier = sums[-1]
        span //= 2
        if split:
            terms[0] += [exchanged(value, bit) for value in sums]
        else:
            for j in reversed(range(span)):
                terms[j].append(exchanged(sums[j], bit))
    last_near, last_far, wide = call(
        functools.partial(last_kernel, groups, span, len(terms[0])),
        [
            ((slots, width + tok_rows), BF16),
            ((slots, width + tok_rows), BF16),
            ((groups, slot_count, 3 * hidden_width + flight * experts), BF16),
        ],
        (
            odd.reshape(1),
            carrier,
            *terms[0],
            basis,
            router_table,
            factors,
            sel_a,
            sel_b,
            first,
            at,
        ),
        in_specs=[scalar] + [whole] * (len(terms[0]) + 8),
        out_specs=[whole] * 3,
    )
    twin_wide = lax.ppermute(wide, "pipe", twins(pipe))
    last_near = lax.ppermute(last_near, "pipe", near(pipe))
    last_far = lax.ppermute(last_far, "pipe", far(pipe))

    share = width // groups
    tiles = min(8, share // 128)
    tile = width // tiles
    same = flight == 1
    held = (*own, *twin) if same else (*own, *twin, *own_all, *twin_all)
    grad_gate_up, grad_down, grad_router = call(
        functools.partial(grads_kernel, groups, hidden_width, experts, same),
        [
            ((2, width, hidden_width), BF16),
            ((hidden_width, width), BF16),
            ((share, experts), BF16),
        ],
        (me.reshape(1), *held, wide, twin_wide),
        grid=(tiles,),
        in_specs=[scalar] + [whole] * (len(held) + 2),
        out_specs=[
            pl.BlockSpec((2, tile, hidden_width), lambda i: (0, i, 0)),
            pl.BlockSpec((hidden_width, tile), lambda i: (0, i)),
            pl.BlockSpec((share // tiles, experts), lambda i: (i, 0)),
        ],
    )
    section_out_a, grad_in_b = placed(odd.reshape(1), from_near, last_near, last_far, from_far)
    return (
        section_out_a[None],
        grad_in_b[None],
        grad_gate_up[None],
        grad_down[None],
        grad_router[None],
    )


def solution(mesh):
    return jax.shard_map(
        on_device,
        mesh=mesh,
        in_specs=(
            P("pipe", "expert", None),
            P("pipe", "expert", None),
            P("pipe", None, None),
            P("pipe", None, None, "expert"),
            P("pipe", "expert", None),
            P("pipe", "expert", None),
            P("pipe", "expert", None),
            P("pipe", "expert", None),
        ),
        out_specs=(
            P("pipe", "expert", None),
            P("pipe", "expert", None),
            P("pipe", None, None, "expert"),
            P("pipe", "expert", None),
            P("pipe", "expert", None),
        ),
        check_vma=False,
    )
```

time: 99 us -> 73.2 us (0.74)
  the two profiles are of different devices: /device:TPU:16 before, /device:TPU:0 now
where the time goes in v3:
time: 73.2 us; the launch traced here: 72.9 us
  waiting for transfers between devices  25 us (34%)
  starting transfers between devices  22 us (30%)
  Pallas kernels  20.4 us (28%)
  local copies, waits for them, and re-layouts  4.8 us (7%)
  between operations  0.76 us (1%)
    pallas_call x7, Pallas kernels, call(): pl.pallas_call(kernel, out_shape=[jax.ShapeDtypeStruct(shape, dtype) for...  20.4 us
    ppermute x10, waiting for transfers between devices, exchanged(): return lax.ppermute(block, 'expert', [(i, i ^ bit) for i in range(count)])  12.2 us
    ppermute x10, starting transfers between devices, exchanged(): return lax.ppermute(block, 'expert', [(i, i ^ bit) for i in range(count)])  7.68 us
    ppermute x1, waiting for transfers between devices, on_device(): twin_wide = lax.ppermute(wide, 'pipe', twins(pipe))  5.74 us
    unnamed x18, local copies, waits for them, and re-layouts  4.8 us
    ppermute x1, starting transfers between devices, on_device(): from_far = lax.ppermute(to_far, 'pipe', far(pipe))  4.37 us
    ppermute x1, waiting for transfers between devices, on_device(): from_near = lax.ppermute(to_near, 'pipe', near(pipe))[0]  4.34 us
    ppermute x1, starting transfers between devices, on_device(): twin_all = everywhere(lax.ppermute(twin_rows, 'pipe', twins(pipe)))  4.05 us
  transfers between devices with their start and end apart: 16, of which 6 were waited for; matrix products, arithmetic and copies ran while one was open for 0% of the time, Pallas kernels for 18%

profile of v3, /device:TPU:0, one launch (start us, length us, event | category | flops | bytes accessed | tf_op | source)
XLA Modules:
  0.0 72.9 jit_solution(13723720556238317806)
XLA Ops:
  0.6 0.0 copy-start
  0.7 4.0 %shard_map.119 = (bf16[3,16,4224]{2,1,0:T(8,128)(2,1)}, bf16[2,16,4096]{2,1,0:T(8,128)(2,1)}, bf16[16,128]{1,0:T(8,128)(2,1)}, bf16[16,128]{1,0:T(8,128)(2,1)}, bf16[1,128,4096]{2,1,0:T(8,128)(2,1)}) custom-call(s32[1]{0:T(128)} %bitcast.odd, s32[8,128]{1,0:T(8,128)} %bitcast.30, s32[8,128]{1,0:T(8,128)} %bitcast.32, bf16[128,4096]{1,0:T(8,128)(2,1)} %bitcast.29, ...), custom_call_target="tpu_custom_call" | custom-call | tf_op jit(solution)/shard_map/pallas_call | solution.py:42
  4.7 3.0 %collective-permute-start.1 = (bf16[3,16,4224]{2,1,0:T(8,128)(2,1)}, bf16[3,16,4224]{2,1,0:T(8,128)(2,1)S(1)}, u32[]{:S(2)}, u32[]{:S(2)}) collective-permute-start(bf16[3,16,4224]{2,1,0:T(8,128)(2,1)} %get-tuple-element.30.refs_0_), channel_id=1, source_target_pairs={{0,2},{1,3},{2,0},{3,1},{4,6},{5,7},{6,4},{7,5},{8,10},{9,11},{10,... | collective-permute-start | bytes 1216520 | tf_op jit(solution)/shard_map/ppermute | solution.py:38
  7.7 0.0 collective-permute-start.2
  7.7 4.1 %collective-permute-start.5 = (bf16[2,16,4096]{2,1,0:T(8,128)(2,1)}, bf16[2,16,4096]{2,1,0:T(8,128)(2,1)S(1)}, u32[]{:S(2)}, u32[]{:S(2)}) collective-permute-start(bf16[2,16,4096]{2,1,0:T(8,128)(2,1)} %get-tuple-element.34), channel_id=1, source_target_pairs={{0,28},{4,24},{8,20},{12,16},{16,12},{20,8},{24,4},{28,0},{1,29},{... | collective-permute-start | bytes 786440 | tf_op jit(solution)/shard_map/ppermute | solution.py:434
  11.8 1.0 %collective-permute-start = (bf16[1,128,4096]{2,1,0:T(8,128)(2,1)}, bf16[1,128,4096]{2,1,0:T(8,128)(2,1)}, u32[]{:S(2)}, u32[]{:S(2)}) collective-permute-start(bf16[1,128,4096]{2,1,0:T(8,128)(2,1)} %get-tuple-element.29), channel_id=1, source_target_pairs={{0,4},{4,0},{8,12},{12,8},{16,20},{20,16},{24,28},{28,24},{1,5},{5... | collective-permute-start | bytes 3145736 | tf_op jit(solution)/shard_map/ppermute | solution.py:432
  12.8 4.5 %collective-permute-done.1.refs_1_ = bf16[3,16,4224]{2,1,0:T(8,128)(2,1)S(1)} collective-permute-done((bf16[3,16,4224]{2,1,0:T(8,128)(2,1)}, bf16[3,16,4224]{2,1,0:T(8,128)(2,1)S(1)}, u32[]{:S(2)}, u32[]{:S(2)}) %collective-permute-start.1) | collective-permute-done | bytes 405536 | tf_op jit(solution)/shard_map/ppermute | solution.py:38
  17.3 0.0 collective-permute-start.3
  17.3 2.6 %shard_map.122 = (bf16[16,4096]{1,0:T(8,128)(2,1)}, bf16[16,128]{1,0:T(8,128)(2,1)}, bf16[112,4096]{1,0:T(8,128)(2,1)}) custom-call(s32[1]{0:T(128)} %bitcast.odd, s32[8,128]{1,0:T(8,128)} %bitcast.33, s32[8,128]{1,0:T(8,128)} %bitcast.31, bf16[128,4096]{1,0:T(8,128)(2,1)} %bitcast.28, bf16[128,4096]{1,0:T(8,128)(2,1)} %bitcast.26), custom_call_target="tpu_custom_call" | custom-call | tf_op jit(solution)/shard_map/pallas_call | solution.py:42
  19.9 4.4 %collective-permute-start.14 = (bf16[112,4096]{1,0:T(8,128)(2,1)}, bf16[112,4096]{1,0:T(8,128)(2,1)}, u32[]{:S(2)}, u32[]{:S(2)}) collective-permute-start(bf16[112,4096]{1,0:T(8,128)(2,1)} %get-tuple-element.46), channel_id=1, source_target_pairs={{0,28},{4,8},{8,4},{12,16},{16,12},{20,24},{24,20},{28,0},{1,29},{... | collective-permute-start | bytes 2752520 | tf_op jit(solution)/shard_map/ppermute | solution.py:433
  24.3 0.0 collective-permute-done.5.refs_2_.refs_4_
  24.3 1.5 %collective-permute-start.6 = (bf16[2,16,4096]{2,1,0:T(8,128)(2,1)S(1)}, bf16[2,16,4096]{2,1,0:T(8,128)(2,1)S(1)}, u32[]{:S(2)}, u32[]{:S(2)}) collective-permute-start(bf16[2,16,4096]{2,1,0:T(8,128)(2,1)S(1)} %collective-permute-done.5.refs_2_.refs_4_), channel_id=1, source_target_pairs={{0,2},{1,3},{2,0},{3,1},{4,6},{5,7},{6,4},{7,5},{8,10},{9,11},{10,... | collective-permute-start | bytes 786440 | tf_op jit(solution)/shard_map/ppermute | solution.py:38
  25.8 0.0 collective-permute-done.2.refs_2_
  25.8 0.0 collective-permute-start.7
  25.8 0.0 collective-permute-done.3.refs_3_
  25.8 0.0 copy-done
  25.8 0.0 copy-start.1
  25.8 2.2 %copy-done.1 = bf16[1,2,4096,256]{3,2,1,0:T(8,128)(2,1)S(1)} copy-done((bf16[1,2,4096,256]{3,2,1,0:T(8,128)(2,1)S(1)}, bf16[1,2,4096,256]{3,2,1,0:T(8,128)(2,1)}, u32[]{:S(2)}) %copy-start.1) | copy-done | bytes 4194328
  28.0 1.6 %copy-done.2 = bf16[1,256,4096]{2,1,0:T(8,128)(2,1)S(1)} copy-done((bf16[1,256,4096]{2,1,0:T(8,128)(2,1)S(1)}, bf16[1,256,4096]{2,1,0:T(8,128)(2,1)}, u32[]{:S(2)}) %copy-start.2) | copy-done | bytes 2097176
  29.6 1.0 %copy-done.3 = bf16[3,16,4224]{2,1,0:T(8,128)(2,1)S(1)} copy-done((bf16[3,16,4224]{2,1,0:T(8,128)(2,1)S(1)}, bf16[3,16,4224]{2,1,0:T(8,128)(2,1)}, u32[]{:S(2)}) %copy-start.3) | copy-done | bytes 405528
  30.6 4.2 %shard_map.120 = (bf16[16,8320]{1,0:T(8,128)(2,1)S(1)}, bf16[16,8320]{1,0:T(8,128)(2,1)S(1)}, bf16[16,8320]{1,0:T(8,128)(2,1)S(1)}, bf16[16,8320]{1,0:T(8,128)(2...) custom-call(s32[1]{0:T(128)} %bitcast.9.mine, bf16[3,16,4224]{2,1,0:T(8,128)(2,1)S(1)} %copy-done.3, ...), custom_call_target="tpu_custom_call" | custom-call | tf_op jit(solution)/shard_map/pallas_call | solution.py:42
  34.8 0.0 copy-start.4
  34.9 0.6 collective-permute-start.4
  35.4 0.0 collective-permute-done.6.refs_3_.refs_5_
  35.4 0.1 collective-permute-start.8
  35.5 0.0 collective-permute-done.7.refs_4_.refs_6_
  35.5 0.4 collective-permute-start.9
  35.9 1.0 %collective-permute-done.8.refs_5_.refs_7_ = bf16[2,16,4096]{2,1,0:T(8,128)(2,1)S(1)} collective-permute-done((bf16[2,16,4096]{2,1,0:T(8,128)(2,1)S(1)}, bf16[2,16,4096]{2,1,0:T(8,128)(2,1)S(1)}, u32[]{:S(2)}, u32[]{:S(2)}) %collective-permute-start.8) | collective-permute-done | bytes 262176 | tf_op jit(solution)/shard_map/ppermute | solution.py:38
  37.0 0.0 collective-permute-done.4.other.refs_1_
  37.0 0.3 shard_map.121
  37.2 0.6 collective-permute-start.11
  37.8 1.5 %collective-permute-start.10 = (bf16[16,4096]{1,0:T(8,128)(2,1)S(1)}, bf16[16,4096]{1,0:T(8,128)(2,1)S(1)}, u32[]{:S(2)}, u32[]{:S(2)}) collective-permute-start(bf16[16,4096]{1,0:T(8,128)(2,1)S(1)} %get-tuple-element.37), channel_id=1, source_target_pairs={{0,2},{1,3},{2,0},{3,1},{4,6},{5,7},{6,4},{7,5},{8,10},{9,11},{10,... | collective-permute-start | bytes 393224 | tf_op jit(solution)/shard_map/ppermute | solution.py:38
  39.3 0.0 collective-permute-done.9.refs_1_
  39.3 6.6 %collective-permute-done.10.refs_2_ = bf16[16,4096]{1,0:T(8,128)(2,1)S(1)} collective-permute-done((bf16[16,4096]{1,0:T(8,128)(2,1)S(1)}, bf16[16,4096]{1,0:T(8,128)(2,1)S(1)}, u32[]{:S(2)}, u32[]{:S(2)}) %collective-permute-start.10) | collective-permute-done | bytes 131104 | tf_op jit(solution)/shard_map/ppermute | solution.py:38
  46.0 0.0 collective-permute-done.11.refs_3_
  46.0 0.0 copy-done.5
  46.0 0.0 copy-done.6
  46.0 0.6 shard_map.123
  46.6 0.1 collective-permute-start.12
  46.6 1.9 %collective-permute-start.13 = (bf16[16,4224]{1,0:T(8,128)(2,1)S(1)}, bf16[16,4224]{1,0:T(8,128)(2,1)S(1)}, u32[]{:S(2)}, u32[]{:S(2)}) collective-permute-start(bf16[16,4224]{1,0:T(8,128)(2,1)S(1)} %get-tuple-element.45), channel_id=1, source_target_pairs={{0,28},{4,8},{8,4},{12,16},{16,12},{20,24},{24,20},{28,0},{1,29},{... | collective-permute-start | bytes 405512 | tf_op jit(solution)/shard_map/ppermute | solution.py:510
  48.5 2.9 %collective-permute-start.15 = (bf16[4,16,896]{2,1,0:T(8,128)(2,1)S(1)}, bf16[4,16,896]{2,1,0:T(8,128)(2,1)S(1)}, u32[]{:S(2)}, u32[]{:S(2)}) collective-permute-start(bf16[4,16,896]{2,1,0:T(8,128)(2,1)S(1)} %get-tuple-element.49.refs_8_), channel_id=1, source_target_pairs={{0,28},{4,24},{8,20},{12,16},{16,12},{20,8},{24,4},{28,0},{1,29},{... | collective-permute-start | bytes 344072 | tf_op jit(solution)/shard_map/ppermute | solution.py:508
  51.4 5.7 %collective-permute-done.15.refs_9_ = bf16[4,16,896]{2,1,0:T(8,128)(2,1)S(1)} collective-permute-done((bf16[4,16,896]{2,1,0:T(8,128)(2,1)S(1)}, bf16[4,16,896]{2,1,0:T(8,128)(2,1)S(1)}, u32[]{:S(2)}, u32[]{:S(2)}) %collective-permute-start.15) | collective-permute-done | bytes 114720 | tf_op jit(solution)/shard_map/ppermute | solution.py:508
  57.2 5.6 %shard_map.125 = (bf16[2,4096,256]{2,1,0:T(8,128)(2,1)}, bf16[256,4096]{1,0:T(8,128)(2,1)}, bf16[1024,128]{1,0:T(8,128)(2,1)}) custom-call(s32[1]{0:T(128)} %bitcast.17.me, bf16[3,16,4224]{2,1,0:T(8,128)(2,1)S(1)} %copy-done.4, bf16[3,16,4224]{2,1,0:T(8,128)(2,1)S(1)} %collective-permute-done.1.refs_1_, ...), custom_call_target="tpu_custom_call" | custom-call | tf_op jit(solution)/shard_map/pallas_call | solution.py:42
  62.7 0.0 collective-permute-done.14.far
  62.7 4.3 %collective-permute-done = bf16[1,128,4096]{2,1,0:T(8,128)(2,1)} collective-permute-done((bf16[1,128,4096]{2,1,0:T(8,128)(2,1)}, bf16[1,128,4096]{2,1,0:T(8,128)(2,1)}, u32[]{:S(2)}, u32[]{:S(2)}) %collective-permute-start) | collective-permute-done | bytes 1048608 | tf_op jit(solution)/shard_map/ppermute | solution.py:432
  67.1 2.7 %collective-permute-done.12.last_near = bf16[16,4224]{1,0:T(8,128)(2,1)S(1)} collective-permute-done((bf16[16,4224]{1,0:T(8,128)(2,1)S(1)}, bf16[16,4224]{1,0:T(8,128)(2,1)S(1)}, u32[]{:S(2)}, u32[]{:S(2)}) %collective-permute-start.12) | collective-permute-done | bytes 135200 | tf_op jit(solution)/shard_map/ppermute | solution.py:509
  69.8 0.0 collective-permute-done.13.last_far
  69.8 3.1 %shard_map.124 = (bf16[128,4096]{1,0:T(8,128)(2,1)}, bf16[128,4096]{1,0:T(8,128)(2,1)}) custom-call(s32[1]{0:T(128)} %bitcast.odd, bf16[128,4096]{1,0:T(8,128)(2,1)} %bitcast.8.near, bf16[16,4224]{1,0:T(8,128)(2,1)S(1)} %collective-permute-done.12.last_near, bf16[16,4224]{1,0:T(8,128)(2,1)S(1)} %collective-permute-done.13.last_far, ...), custom_call_target="tpu_custom_call" | custom-call | tf_op jit(solution)/shard_map/pallas_call | solution.py:42
  (9 shorter events, 0.0 us)
Async XLA Ops:
  0.6 25.2 %copy-start = (bf16[1,4096,128]{2,1,0:T(8,128)(2,1)S(1)}, bf16[1,4096,128]{2,1,0:T(8,128)(2,1)}, u32[]{:S(2)}) copy-start(bf16[1,4096,128]{2,1,0:T(8,128)(2,1)} %param.10) | copy-start | bytes 3145732
  4.7 12.6 %collective-permute-start.1 = (bf16[3,16,4224]{2,1,0:T(8,128)(2,1)}, bf16[3,16,4224]{2,1,0:T(8,128)(2,1)S(1)}, u32[]{:S(2)}, u32[]{:S(2)}) collective-permute-start(bf16[3,16,4224]{2,1,0:T(8,128)(2,1)} %get-tuple-element.30.refs_0_), channel_id=1, source_target_pairs={{0,2},{1,3},{2,0},{3,1},{4,6},{5,7},{6,4},{7,5},{8,10},{9,11},{10,... | collective-permute-start | bytes 1216520 | tf_op jit(solution)/shard_map/ppermute | solution.py:38
  7.7 18.1 %collective-permute-start.2 = (bf16[3,16,4224]{2,1,0:T(8,128)(2,1)}, bf16[3,16,4224]{2,1,0:T(8,128)(2,1)S(1)}, u32[]{:S(2)}, u32[]{:S(2)}) collective-permute-start(bf16[3,16,4224]{2,1,0:T(8,128)(2,1)} %get-tuple-element.30.refs_0_), channel_id=1, source_target_pairs={{0,1},{1,0},{2,3},{3,2},{4,5},{5,4},{6,7},{7,6},{8,9},{9,8},{10,11... | collective-permute-start | bytes 1216520 | tf_op jit(solution)/shard_map/ppermute | solution.py:38
  7.7 16.6 %collective-permute-start.5 = (bf16[2,16,4096]{2,1,0:T(8,128)(2,1)}, bf16[2,16,4096]{2,1,0:T(8,128)(2,1)S(1)}, u32[]{:S(2)}, u32[]{:S(2)}) collective-permute-start(bf16[2,16,4096]{2,1,0:T(8,128)(2,1)} %get-tuple-element.34), channel_id=1, source_target_pairs={{0,28},{4,24},{8,20},{12,16},{16,12},{20,8},{24,4},{28,0},{1,29},{... | collective-permute-start | bytes 786440 | tf_op jit(solution)/shard_map/ppermute | solution.py:434
  11.8 55.3 %collective-permute-start = (bf16[1,128,4096]{2,1,0:T(8,128)(2,1)}, bf16[1,128,4096]{2,1,0:T(8,128)(2,1)}, u32[]{:S(2)}, u32[]{:S(2)}) collective-permute-start(bf16[1,128,4096]{2,1,0:T(8,128)(2,1)} %get-tuple-element.29), channel_id=1, source_target_pairs={{0,4},{4,0},{8,12},{12,8},{16,20},{20,16},{24,28},{28,24},{1,5},{5... | collective-permute-start | bytes 3145736 | tf_op jit(solution)/shard_map/ppermute | solution.py:432
  17.3 8.5 %collective-permute-start.3 = (bf16[3,16,4224]{2,1,0:T(8,128)(2,1)S(1)}, bf16[3,16,4224]{2,1,0:T(8,128)(2,1)S(1)}, u32[]{:S(2)}, u32[]{:S(2)}) collective-permute-start(bf16[3,16,4224]{2,1,0:T(8,128)(2,1)S(1)} %collective-permute-done.1.refs_1_), channel_id=1, source_target_pairs={{0,1},{1,0},{2,3},{3,2},{4,5},{5,4},{6,7},{7,6},{8,9},{9,8},{10,11... | collective-permute-start | bytes 1216520 | tf_op jit(solution)/shard_map/ppermute | solution.py:38
  19.9 42.8 %collective-permute-start.14 = (bf16[112,4096]{1,0:T(8,128)(2,1)}, bf16[112,4096]{1,0:T(8,128)(2,1)}, u32[]{:S(2)}, u32[]{:S(2)}) collective-permute-start(bf16[112,4096]{1,0:T(8,128)(2,1)} %get-tuple-element.46), channel_id=1, source_target_pairs={{0,28},{4,8},{8,4},{12,16},{16,12},{20,24},{24,20},{28,0},{1,29},{... | collective-permute-start | bytes 2752520 | tf_op jit(solution)/shard_map/ppermute | solution.py:433
  24.3 11.1 %collective-permute-start.6 = (bf16[2,16,4096]{2,1,0:T(8,128)(2,1)S(1)}, bf16[2,16,4096]{2,1,0:T(8,128)(2,1)S(1)}, u32[]{:S(2)}, u32[]{:S(2)}) collective-permute-start(bf16[2,16,4096]{2,1,0:T(8,128)(2,1)S(1)} %collective-permute-done.5.refs_2_.refs_4_), channel_id=1, source_target_pairs={{0,2},{1,3},{2,0},{3,1},{4,6},{5,7},{6,4},{7,5},{8,10},{9,11},{10,... | collective-permute-start | bytes 786440 | tf_op jit(solution)/shard_map/ppermute | solution.py:38
  25.8 9.7 %collective-permute-start.7 = (bf16[2,16,4096]{2,1,0:T(8,128)(2,1)S(1)}, bf16[2,16,4096]{2,1,0:T(8,128)(2,1)S(1)}, u32[]{:S(2)}, u32[]{:S(2)}) collective-permute-start(bf16[2,16,4096]{2,1,0:T(8,128)(2,1)S(1)} %collective-permute-done.5.refs_2_.refs_4_), channel_id=1, source_target_pairs={{0,1},{1,0},{2,3},{3,2},{4,5},{5,4},{6,7},{7,6},{8,9},{9,8},{10,11... | collective-permute-start | bytes 786440 | tf_op jit(solution)/shard_map/ppermute | solution.py:38
  25.8 2.2 %copy-start.1 = (bf16[1,2,4096,256]{3,2,1,0:T(8,128)(2,1)S(1)}, bf16[1,2,4096,256]{3,2,1,0:T(8,128)(2,1)}, u32[]{:S(2)}) copy-start(bf16[1,2,4096,256]{3,2,1,0:T(8,128)(2,1)} %param.11) | copy-start | bytes 12582916
  28.0 1.6 %copy-start.2 = (bf16[1,256,4096]{2,1,0:T(8,128)(2,1)S(1)}, bf16[1,256,4096]{2,1,0:T(8,128)(2,1)}, u32[]{:S(2)}) copy-start(bf16[1,256,4096]{2,1,0:T(8,128)(2,1)} %param.12) | copy-start | bytes 6291460
  29.6 1.0 %copy-start.3 = (bf16[3,16,4224]{2,1,0:T(8,128)(2,1)S(1)}, bf16[3,16,4224]{2,1,0:T(8,128)(2,1)}, u32[]{:S(2)}) copy-start(bf16[3,16,4224]{2,1,0:T(8,128)(2,1)} %get-tuple-element.30.refs_0_) | copy-start | bytes 1216516
  30.6 15.4 %copy-start.5 = (bf16[16,4096]{1,0:T(8,128)(2,1)S(1)}, bf16[16,4096]{1,0:T(8,128)(2,1)}, u32[]{:S(2)}) copy-start(bf16[16,4096]{1,0:T(8,128)(2,1)} %get-tuple-element.42.refs_9_) | copy-start | bytes 393220
  30.6 15.4 %copy-start.6 = (bf16[16,128]{1,0:T(8,128)(2,1)S(1)}, bf16[16,128]{1,0:T(8,128)(2,1)}, u32[]{:S(2)}) copy-start(bf16[16,128]{1,0:T(8,128)(2,1)} %get-tuple-element.40.refs_7_) | copy-start | bytes 12292
  30.6 15.4 %copy-start.7 = (bf16[16,128]{1,0:T(8,128)(2,1)S(1)}, bf16[16,128]{1,0:T(8,128)(2,1)}, u32[]{:S(2)}) copy-start(bf16[16,128]{1,0:T(8,128)(2,1)} %get-tuple-element.41.refs_8_) | copy-start | bytes 12292
  30.6 15.4 %copy-start.8 = (bf16[16,128]{1,0:T(8,128)(2,1)S(1)}, bf16[16,128]{1,0:T(8,128)(2,1)}, u32[]{:S(2)}) copy-start(bf16[16,128]{1,0:T(8,128)(2,1)} %get-tuple-element.43.refs_10_) | copy-start | bytes 12292
  34.8 22.3 %copy-start.4 = (bf16[3,16,4224]{2,1,0:T(8,128)(2,1)S(1)}, bf16[3,16,4224]{2,1,0:T(8,128)(2,1)}, u32[]{:S(2)}) copy-start(bf16[3,16,4224]{2,1,0:T(8,128)(2,1)} %get-tuple-element.30.refs_0_) | copy-start | bytes 1216516
  34.9 2.1 %collective-permute-start.4 = (bf16[16,8320]{1,0:T(8,128)(2,1)S(1)}, bf16[16,8320]{1,0:T(8,128)(2,1)S(1)}, u32[]{:S(2)}, u32[]{:S(2)}) collective-permute-start(bf16[16,8320]{1,0:T(8,128)(2,1)S(1)} %get-tuple-element.32), channel_id=1, source_target_pairs={{0,1},{1,0},{2,3},{3,2},{4,5},{5,4},{6,7},{7,6},{8,9},{9,8},{10,11... | collective-permute-start | bytes 798728 | tf_op jit(solution)/shard_map/ppermute | solution.py:38
  35.4 1.5 %collective-permute-start.8 = (bf16[2,16,4096]{2,1,0:T(8,128)(2,1)S(1)}, bf16[2,16,4096]{2,1,0:T(8,128)(2,1)S(1)}, u32[]{:S(2)}, u32[]{:S(2)}) collective-permute-start(bf16[2,16,4096]{2,1,0:T(8,128)(2,1)S(1)} %collective-permute-done.6.refs_3_.refs_5_), channel_id=1, source_target_pairs={{0,1},{1,0},{2,3},{3,2},{4,5},{5,4},{6,7},{7,6},{8,9},{9,8},{10,11... | collective-permute-start | bytes 786440 | tf_op jit(solution)/shard_map/ppermute | solution.py:38
  35.5 3.8 %collective-permute-start.9 = (bf16[16,8320]{1,0:T(8,128)(2,1)S(1)}, bf16[16,8320]{1,0:T(8,128)(2,1)S(1)}, u32[]{:S(2)}, u32[]{:S(2)}) collective-permute-start(bf16[16,8320]{1,0:T(8,128)(2,1)S(1)} %get-tuple-element.36), channel_id=1, source_target_pairs={{0,1},{1,0},{2,3},{3,2},{4,5},{5,4},{6,7},{7,6},{8,9},{9,8},{10,11... | collective-permute-start | bytes 798728 | tf_op jit(solution)/shard_map/ppermute | solution.py:38
  37.2 8.7 %collective-permute-start.11 = (bf16[16,4224]{1,0:T(8,128)(2,1)S(1)}, bf16[16,4224]{1,0:T(8,128)(2,1)S(1)}, u32[]{:S(2)}, u32[]{:S(2)}) collective-permute-start(bf16[16,4224]{1,0:T(8,128)(2,1)S(1)} %get-tuple-element.35.own), channel_id=1, source_target_pairs={{0,2},{1,3},{2,0},{3,1},{4,6},{5,7},{6,4},{7,5},{8,10},{9,11},{10,... | collective-permute-start | bytes 405512 | tf_op jit(solution)/shard_map/ppermute | solution.py:38
  37.8 8.1 %collective-permute-start.10 = (bf16[16,4096]{1,0:T(8,128)(2,1)S(1)}, bf16[16,4096]{1,0:T(8,128)(2,1)S(1)}, u32[]{:S(2)}, u32[]{:S(2)}) collective-permute-start(bf16[16,4096]{1,0:T(8,128)(2,1)S(1)} %get-tuple-element.37), channel_id=1, source_target_pairs={{0,2},{1,3},{2,0},{3,1},{4,6},{5,7},{6,4},{7,5},{8,10},{9,11},{10,... | collective-permute-start | bytes 393224 | tf_op jit(solution)/shard_map/ppermute | solution.py:38
  46.6 23.2 %collective-permute-start.12 = (bf16[16,4224]{1,0:T(8,128)(2,1)S(1)}, bf16[16,4224]{1,0:T(8,128)(2,1)S(1)}, u32[]{:S(2)}, u32[]{:S(2)}) collective-permute-start(bf16[16,4224]{1,0:T(8,128)(2,1)S(1)} %get-tuple-element.44), channel_id=1, source_target_pairs={{0,4},{4,0},{8,12},{12,8},{16,20},{20,16},{24,28},{28,24},{1,5},{5... | collective-permute-start | bytes 405512 | tf_op jit(solution)/shard_map/ppermute | solution.py:509
  46.6 23.2 %collective-permute-start.13 = (bf16[16,4224]{1,0:T(8,128)(2,1)S(1)}, bf16[16,4224]{1,0:T(8,128)(2,1)S(1)}, u32[]{:S(2)}, u32[]{:S(2)}) collective-permute-start(bf16[16,4224]{1,0:T(8,128)(2,1)S(1)} %get-tuple-element.45), channel_id=1, source_target_pairs={{0,28},{4,8},{8,4},{12,16},{16,12},{20,24},{24,20},{28,0},{1,29},{... | collective-permute-start | bytes 405512 | tf_op jit(solution)/shard_map/ppermute | solution.py:510
  48.5 8.6 %collective-permute-start.15 = (bf16[4,16,896]{2,1,0:T(8,128)(2,1)S(1)}, bf16[4,16,896]{2,1,0:T(8,128)(2,1)S(1)}, u32[]{:S(2)}, u32[]{:S(2)}) collective-permute-start(bf16[4,16,896]{2,1,0:T(8,128)(2,1)S(1)} %get-tuple-element.49.refs_8_), channel_id=1, source_target_pairs={{0,28},{4,24},{8,20},{12,16},{16,12},{20,8},{24,4},{28,0},{1,29},{... | collective-permute-start | bytes 344072 | tf_op jit(solution)/shard_map/ppermute | solution.py:508

commit v4 on v3

--- a/solution.py
+++ b/solution.py
@@ -64,10 +64,10 @@
     return jnp.concatenate(picked, axis=0).astype(BF16)
 
 
-def pick_kernel(flight, slot_count, topk, odd, *refs):
+def pick_kernel(flight, slot_count, topk, *refs):
     sources, refs = refs[:5], refs[5:]
-    packed, twin, sel_a, sel_b, to_near = refs[:5]
-    held, sems = refs[5:10], refs[10]
+    packed, twin, sel_a, sel_b = refs[:4]
+    held, sems = refs[4:9], refs[9]
     copies = [
         pltpu.make_async_copy(source, here, sems.at[k])
         for k, (source, here) in enumerate(zip(sources, held))
@@ -87,21 +87,16 @@
         slot_ids = dot(select, numbers, last_last).astype(BF16)
         for place, source in ((0, 2), (1, 3)) if k == 0 else ((2, 4),):
             copies[source].wait()
-            if place > 0:
-                @pl.when(odd[0] == (1 if place == 1 else 0))
-                def _(onward=held[source]):
-                    pltpu.make_async_copy(onward, to_near.at[0], sems.at[5]).start()
-
             rows = dot(select, held[source][...]).astype(BF16)
             packed[place, :, :width] = rows
             packed[place, :, width:] = slot_ids
             if place < 2:
                 twin[place] = rows
-    pltpu.make_async_copy(x_a, to_near.at[0], sems.at[5]).wait()
-
-
-def order_kernel(flight, slots, odd, ids_a, ids_b, x_a, grad, first, at, far, ids, block, sems):
-    for mine, ids_ref, block_ref in ((1, ids_a, x_a), (0, ids_b, grad)):
+
+
+def order_kernel(flight, slots, sends_a, odd, ids_a, ids_b, x_a, grad, *refs):
+    first, at, later, ids, block, sems = refs[-6:]
+    for mine, ids_ref, block_ref in ((sends_a, ids_a, x_a), (1 - sends_a, ids_b, grad)):
 
         @pl.when(odd[0] == mine)
         def _(ids_ref=ids_ref, block_ref=block_ref):
@@ -126,7 +121,10 @@
     pltpu.make_async_copy(x_a, block, sems.at[1]).wait()
     rows = dot(order, block[...]).astype(BF16)
     first[...] = rows[:slots, :]
-    far[...] = rows[slots:, :]
+    width = rows.shape[1]
+    later[:, :width] = rows[slots:, :]
+    if later.shape[1] > width:
+        later[:, width:] = jnp.broadcast_to(where, (later.shape[0], tokens)).astype(BF16)
 
 
 def gates(ids, logits, topk, expert):
@@ -249,9 +247,10 @@
 
 def last_kernel(blocks, span, count, odd, own, *refs):
     terms, refs = refs[: count - 2], refs[count - 2 :]
-    last_a, last_b, basis, router, factors, sel_a, sel_b, first, at, to_near, to_far, wide = refs
+    last_a, last_b, basis, router, factors, sel_a, sel_b = refs[:7]
+    first_near, first_far, at_near, at_far, to_near, to_far, wide = refs[7:]
     width, experts = router.shape
-    slots = first.shape[0]
+    slots = first_near.shape[0]
     total = added(terms, 2 * width)
     scores = summed_scores(own, last_b, blocks, span, width)
     sums = [(score * basis[j]).astype(BF16) for j, score in enumerate(scores)]
@@ -260,16 +259,19 @@
         total[:, width:] + last_b[:, :width].astype(F32) + dot(sums[0], router[...], last_last)
     )
     even = odd[0] == 0
-    to_near[:, :width] = jnp.where(even, more_a, more_b).astype(BF16)
-    to_near[:, width:] = jnp.where(even, sel_a[...], sel_b[...])
-    more = jnp.where(even, more_b, more_a)
-    if slots * blocks != factors.shape[0]:
-        place = lax.broadcasted_iota(jnp.int32, at.shape, 0).astype(F32)
-        row = (place == at[...].astype(F32)).astype(F32).astype(BF16)
-        slot = jnp.where(even, sel_b[...].astype(F32), sel_a[...].astype(F32)).astype(BF16)
-        more = jnp.dot(dot(row, slot, last_last), more, precision=lax.Precision.HIGHEST)
-    to_far[:, :width] = (first[...].astype(F32) + more).astype(BF16)
-    to_far[:, width:] = at[...]
+    for sends_a, first, at, out in (
+        (even, first_near, at_near, to_near),
+        (jnp.logical_not(even), first_far, at_far, to_far),
+    ):
+        more = jnp.where(sends_a, more_a, more_b)
+        if slots * blocks != factors.shape[0]:
+            place = lax.broadcasted_iota(jnp.int32, at.shape, 0).astype(F32)
+            row = (place == at[...].astype(F32)).astype(F32).astype(BF16)
+            slot = jnp.where(sends_a, sel_a[...].astype(F32), sel_b[...].astype(F32)).astype(BF16)
+            more = jnp.dot(dot(row, slot, last_last), more, precision=lax.Precision.HIGHEST)
+        out[:, :width] = (first[...].astype(F32) + more).astype(BF16)
+        if out.shape[1] > width:
+            out[:, width:] = at[...]
     slot_count = factors.shape[0] // blocks
     core = factors.shape[1]
     for j, value in enumerate(sums):
@@ -319,37 +321,37 @@
     router[...] = dot(stacked(pieces_all, 0, mine), lg, first_first).astype(BF16)
 
 
-def place_kernel(odd, near, last_near, last_far, far, *refs):
+def place_kernel(odd, last_near, near, last_far, far, *refs):
     outs, held, sems = refs[:2], refs[2:4], refs[4]
     tokens, width = held[0].shape
     step = width // 4
     place = lax.broadcasted_iota(jnp.int32, (tokens, tokens), 0).astype(F32)
-    order = (place == last_far[:1, width:].astype(F32)).astype(F32).astype(BF16)
-    select = last_near[:, width:]
+    orders = [
+        (place == at[:1, width:].astype(F32)).astype(F32).astype(BF16) for at in (near, last_far)
+    ]
     for c in range(4):
         cols = slice(c * step, (c + 1) * step)
-        held[0][:, cols] = (
-            near[:, cols].astype(F32) + dot(select, last_near[:, cols], first_first)
-        ).astype(BF16)
-        rows = jnp.concatenate([last_far[:, cols], far[:, cols]])
-        held[1][:, cols] = dot(order, rows, first_first).astype(BF16)
-        for k, block in enumerate(held):
+        for k, (last, later) in enumerate(((last_near, near), (last_far, far))):
+            rows = jnp.concatenate([last[:, cols], later[:, cols]])
+            held[k][:, cols] = dot(orders[k], rows, first_first).astype(BF16)
             for out, from_odd in ((outs[0], k == 0), (outs[1], k == 1)):
 
                 @pl.when((odd[0] == 1) == from_odd)
-                def _(out=out, block=block, k=k, cols=cols):
-                    pltpu.make_async_copy(block.at[:, cols], out.at[:, cols], sems.at[k]).start()
+                def _(out=out, k=k, cols=cols):
+                    pltpu.make_async_copy(
+                        held[k].at[:, cols], out.at[:, cols], sems.at[k]
+                    ).start()
 
     for k, block in enumerate(held):
         pltpu.make_async_copy(block, outs[k], sems.at[k]).wait()
 
 
-def placed(odd, near, last_near, last_far, far):
-    tokens, width = near.shape
+def placed(odd, last_near, near, last_far, far):
+    tokens, width = far.shape[0] + last_far.shape[0], far.shape[1]
     return call(
         place_kernel,
         [((tokens, width), BF16)] * 2,
-        (odd, near, last_near, last_far, far),
+        (odd, last_near, near, last_far, far),
         in_specs=[scalar] + [whole] * 4,
         out_specs=[outside] * 2,
         scratch_shapes=[pltpu.VMEM((tokens, width), BF16)] * 2 + [pltpu.SemaphoreType.DMA((2,))],
@@ -373,41 +375,41 @@
     bits = [1 << k for k in reversed(range(groups.bit_length() - 1))]
 
     odd = lax.axis_index("pipe") % 2
-    packed, twin_rows, sel_a, sel_b, to_near = call(
+    packed, twin_rows, sel_a, sel_b = call(
         functools.partial(pick_kernel, flight, slot_count, topk),
         [
             ((3, slots, width + experts), BF16),
             ((2, slots, width), BF16),
             ((slots, tok_rows), BF16),
             ((slots, tok_rows), BF16),
-            (section_in_a.shape, BF16),
         ],
-        (odd.reshape(1), route_b[0].T, route_a[0].T, section_in_b[0], grad_out_b[0], section_in_a[0]),
+        (route_b[0].T, route_a[0].T, section_in_b[0], grad_out_b[0], section_in_a[0]),
         limit=61,
-        in_specs=[scalar] + [outside] * 5,
-        out_specs=[whole] * 4 + [outside],
+        in_specs=[outside] * 5,
+        out_specs=[whole] * 4,
         scratch_shapes=[pltpu.VMEM((topk, tok_rows), jnp.int32)] * 2
         + [pltpu.VMEM((tok_rows, width), BF16)] * 3
-        + [pltpu.SemaphoreType.DMA((6,))],
-    )
-
-    first, at, to_far = call(
-        functools.partial(order_kernel, flight, slots),
-        [
-            ((slots, width), BF16),
-            ((slots, tok_rows), BF16),
-            ((tok_rows - slots, width), BF16),
-        ],
-        (odd.reshape(1), route_a[0].T, route_b[0].T, section_in_a[0], grad_out_b[0]),
-        limit=61,
-        in_specs=[scalar] + [outside] * 4,
-        out_specs=[whole] * 3,
-        scratch_shapes=[
-            pltpu.VMEM((topk, tok_rows), jnp.int32),
-            pltpu.VMEM((tok_rows, width), BF16),
-            pltpu.SemaphoreType.DMA((2,)),
-        ],
-    )
+        + [pltpu.SemaphoreType.DMA((5,))],
+    )
+
+    def ordered(sends_a, lanes, after):
+        return call(
+            functools.partial(order_kernel, flight, slots, sends_a),
+            [
+                ((slots, width), BF16),
+                ((slots, tok_rows), BF16),
+                ((tok_rows - slots, width + lanes), BF16),
+            ],
+            (odd.reshape(1), route_a[0].T, route_b[0].T, section_in_a[0], grad_out_b[0], *after),
+            limit=61,
+            in_specs=[scalar] + [outside] * 4 + [anywhere] * len(after),
+            out_specs=[whole] * 3,
+            scratch_shapes=[
+                pltpu.VMEM((topk, tok_rows), jnp.int32),
+                pltpu.VMEM((tok_rows, width), BF16),
+                pltpu.SemaphoreType.DMA((2,)),
+            ],
+        )
 
     def everywhere(block):
         pieces = [block]
@@ -429,7 +431,9 @@
         return full.reshape(values.shape[:-2] + (slots, values.shape[-1]))
 
     own_all = everywhere(packed)
-    from_near = lax.ppermute(to_near, "pipe", near(pipe))[0]
+    first_near, at_near, to_near = ordered(0, tok_rows, ())
+    from_near = lax.ppermute(to_near, "pipe", near(pipe))
+    first_far, at_far, to_far = ordered(1, 0, own_all[1:2])
     from_far = lax.ppermute(to_far, "pipe", far(pipe))
     twin_all = everywhere(lax.ppermute(twin_rows, "pipe", twins(pipe)))
     twin = [of_mine(p) for p in twin_all]
@@ -486,7 +490,7 @@
     last_near, last_far, wide = call(
         functools.partial(last_kernel, groups, span, len(terms[0])),
         [
-            ((slots, width + tok_rows), BF16),
+            ((slots, width), BF16),
             ((slots, width + tok_rows), BF16),
             ((groups, slot_count, 3 * hidden_width + flight * experts), BF16),
         ],
@@ -499,10 +503,12 @@
             factors,
             sel_a,
             sel_b,
-            first,
-            at,
+            first_near,
+            first_far,
+            at_near,
+            at_far,
         ),
-        in_specs=[scalar] + [whole] * (len(terms[0]) + 8),
+        in_specs=[scalar] + [whole] * (len(terms[0]) + 10),
         out_specs=[whole] * 3,
     )
     twin_wide = lax.ppermute(wide, "pipe", twins(pipe))
@@ -530,7 +536,7 @@
             pl.BlockSpec((share // tiles, experts), lambda i: (i, 0)),
         ],
     )
-    section_out_a, grad_in_b = placed(odd.reshape(1), from_near, last_near, last_far, from_far)
+    section_out_a, grad_in_b = placed(odd.reshape(1), last_near, from_near, last_far, from_far)
     return (
         section_out_a[None],
         grad_in_b[None],

time: 73.2 us -> 70.2 us (0.959)
  waiting for transfers between devices: 25 us -> 17.9 us
  Pallas kernels: 20.4 us -> 23.1 us
  local copies, waits for them, and re-layouts: 4.8 us -> 5.56 us
    ppermute x1, waiting for transfers between devices: 4.34 us -> 0.08 us  [on_device(): from_near = lax.ppermute(to_near, 'pipe', near(pipe))]
    pallas_call x7 -> x8, Pallas kernels: 20.4 us -> 23.1 us  [call(): pl.pallas_call(kernel, out_shape=[jax.ShapeDtypeStruct(shape, dtype) for...]
    ppermute x10, waiting for transfers between devices: 12.2 us -> 9.49 us  [exchanged(): return lax.ppermute(block, 'expert', [(i, i ^ bit) for i in range(count)])]
    ppermute x1, starting transfers between devices: 2.89 us -> 4.56 us  [on_device(): twin_wide = lax.ppermute(wide, 'pipe', twins(pipe))]
    ppermute x1, starting transfers between devices: 1.9 us -> 0.23 us  [on_device(): last_far = lax.ppermute(last_far, 'pipe', far(pipe))]
    unnamed x18 -> x26, local copies, waits for them, and re-layouts: 4.8 us -> 5.56 us
  transfers between devices with their start and end apart: 16 -> 16, of which waited for: 6 -> 6; matrix products, arithmetic and copies ran while one was open for 0% -> 0% of each run, Pallas kernels for 18% -> 24%
where the time goes in v4:
time: 70.2 us; the launch traced here: 69.9 us
  Pallas kernels  23.1 us (33%)
  starting transfers between devices  22.5 us (32%)
  waiting for transfers between devices  17.9 us (25%)
  local copies, waits for them, and re-layouts  5.56 us (8%)
  between operations  0.8 us (1%)
    pallas_call x8, Pallas kernels, call(): pl.pallas_call(kernel, out_shape=[jax.ShapeDtypeStruct(shape, dtype) for...  23.1 us
    ppermute x10, waiting for transfers between devices, exchanged(): return lax.ppermute(block, 'expert', [(i, i ^ bit) for i in range(count)])  9.49 us
    ppermute x10, starting transfers between devices, exchanged(): return lax.ppermute(block, 'expert', [(i, i ^ bit) for i in range(count)])  7.68 us
    ppermute x1, waiting for transfers between devices, on_device(): twin_wide = lax.ppermute(wide, 'pipe', twins(pipe))  5.73 us
    unnamed x26, local copies, waits for them, and re-layouts  5.56 us
    ppermute x1, starting transfers between devices, on_device(): from_far = lax.ppermute(to_far, 'pipe', far(pipe))  4.87 us
    ppermute x1, starting transfers between devices, on_device(): twin_wide = lax.ppermute(wide, 'pipe', twins(pipe))  4.56 us
    ppermute x1, starting transfers between devices, on_device(): twin_all = everywhere(lax.ppermute(twin_rows, 'pipe', twins(pipe)))  4.56 us
  transfers between devices with their start and end apart: 16, of which 6 were waited for; matrix products, arithmetic and copies ran while one was open for 0% of the time, Pallas kernels for 24%

profile of v4, /device:TPU:0, one launch (start us, length us, event | category | flops | bytes accessed | tf_op | source)
XLA Modules:
  0.0 69.9 jit_solution(3332753778117999018)
XLA Ops:
  0.6 3.2 %shard_map.119 = (bf16[3,16,4224]{2,1,0:T(8,128)(2,1)}, bf16[2,16,4096]{2,1,0:T(8,128)(2,1)}, bf16[16,128]{1,0:T(8,128)(2,1)}, bf16[16,128]{1,0:T(8,128)(2,1)}) custom-call(s32[8,128]{1,0:T(8,128)} %bitcast.31, s32[8,128]{1,0:T(8,128)} %bitcast.34, bf16[128,4096]{1,0:T(8,128)(2,1)} %bitcast.30, bf16[128,4096]{1,0:T(8,128)(2,1)} %bitcast.24, ...), custom_call_target="tpu_custom_call" | custom-call | tf_op jit(solution)/shard_map/pallas_call | solution.py:42
  3.9 0.0 copy-start.6
  3.9 3.0 %collective-permute-start = (bf16[3,16,4224]{2,1,0:T(8,128)(2,1)}, bf16[3,16,4224]{2,1,0:T(8,128)(2,1)S(1)}, u32[]{:S(2)}, u32[]{:S(2)}) collective-permute-start(bf16[3,16,4224]{2,1,0:T(8,128)(2,1)} %get-tuple-element.31.refs_0_), channel_id=1, source_target_pairs={{0,2},{1,3},{2,0},{3,1},{4,6},{5,7},{6,4},{7,5},{8,10},{9,11},{10,... | collective-permute-start | bytes 1216520 | tf_op jit(solution)/shard_map/ppermute | solution.py:38
  6.9 0.0 collective-permute-start.1
  6.9 4.6 %collective-permute-start.4 = (bf16[2,16,4096]{2,1,0:T(8,128)(2,1)}, bf16[2,16,4096]{2,1,0:T(8,128)(2,1)S(1)}, u32[]{:S(2)}, u32[]{:S(2)}) collective-permute-start(bf16[2,16,4096]{2,1,0:T(8,128)(2,1)} %get-tuple-element.35), channel_id=1, source_target_pairs={{0,28},{4,24},{8,20},{12,16},{16,12},{20,8},{24,4},{28,0},{1,29},{... | collective-permute-start | bytes 786440 | tf_op jit(solution)/shard_map/ppermute | solution.py:438
  11.4 2.6 %shard_map.122 = (bf16[16,4096]{1,0:T(8,128)(2,1)}, bf16[16,128]{1,0:T(8,128)(2,1)}, bf16[112,4224]{1,0:T(8,128)(2,1)}) custom-call(s32[1]{0:T(128)} %bitcast.odd, s32[8,128]{1,0:T(8,128)} %bitcast.35, s32[8,128]{1,0:T(8,128)} %bitcast.32, bf16[128,4096]{1,0:T(8,128)(2,1)} %bitcast.28, bf16[128,4096]{1,0:T(8,128)(2,1)} %bitcast.25), custom_call_target="tpu_custom_call" | custom-call | tf_op jit(solution)/shard_map/pallas_call | solution.py:42
  14.1 0.6 collective-permute-start.12
  14.7 1.8 %collective-permute-done.refs_1_.refs_0_ = bf16[3,16,4224]{2,1,0:T(8,128)(2,1)S(1)} collective-permute-done((bf16[3,16,4224]{2,1,0:T(8,128)(2,1)}, bf16[3,16,4224]{2,1,0:T(8,128)(2,1)S(1)}, u32[]{:S(2)}, u32[]{:S(2)}) %collective-permute-start) | collective-permute-done | bytes 405536 | tf_op jit(solution)/shard_map/ppermute | solution.py:38
  16.5 0.0 collective-permute-start.2
  16.5 0.7 %copy-done.2 = bf16[3,16,4224]{2,1,0:T(8,128)(2,1)} copy-done((bf16[3,16,4224]{2,1,0:T(8,128)(2,1)}, bf16[3,16,4224]{2,1,0:T(8,128)(2,1)S(1)}, u32[]{:S(2)}) %copy-start.2) | copy-done | bytes 405528
  17.2 2.6 %shard_map.123 = (bf16[16,4096]{1,0:T(8,128)(2,1)}, bf16[16,128]{1,0:T(8,128)(2,1)}, bf16[112,4096]{1,0:T(8,128)(2,1)}) custom-call(s32[1]{0:T(128)} %bitcast.odd, s32[8,128]{1,0:T(8,128)} %bitcast.36, s32[8,128]{1,0:T(8,128)} %bitcast.33, bf16[128,4096]{1,0:T(8,128)(2,1)} %bitcast.29, bf16[128,4096]{1,0:T(8,128)(2,1)} %bitcast.26, ...), custom_call_target="tpu_custom_call" | custom-call | tf_op jit(solution)/shard_map/pallas_call | solution.py:42
  19.9 4.9 %collective-permute-start.14 = (bf16[112,4096]{1,0:T(8,128)(2,1)}, bf16[112,4096]{1,0:T(8,128)(2,1)}, u32[]{:S(2)}, u32[]{:S(2)}) collective-permute-start(bf16[112,4096]{1,0:T(8,128)(2,1)} %get-tuple-element.50), channel_id=1, source_target_pairs={{0,28},{4,8},{8,4},{12,16},{16,12},{20,24},{24,20},{28,0},{1,29},{... | collective-permute-start | bytes 2752520 | tf_op jit(solution)/shard_map/ppermute | solution.py:437
  24.7 0.0 collective-permute-done.4.refs_2_.refs_4_
  24.7 1.5 %collective-permute-start.5 = (bf16[2,16,4096]{2,1,0:T(8,128)(2,1)S(1)}, bf16[2,16,4096]{2,1,0:T(8,128)(2,1)S(1)}, u32[]{:S(2)}, u32[]{:S(2)}) collective-permute-start(bf16[2,16,4096]{2,1,0:T(8,128)(2,1)S(1)} %collective-permute-done.4.refs_2_.refs_4_), channel_id=1, source_target_pairs={{0,2},{1,3},{2,0},{3,1},{4,6},{5,7},{6,4},{7,5},{8,10},{9,11},{10,... | collective-permute-start | bytes 786440 | tf_op jit(solution)/shard_map/ppermute | solution.py:38
  26.2 0.0 collective-permute-done.1.refs_2_
  26.2 0.0 collective-permute-start.6
  26.2 0.0 collective-permute-done.2.refs_3_
  26.2 0.0 copy-start.1
  26.3 2.2 %copy-done.1 = bf16[1,2,4096,256]{3,2,1,0:T(8,128)(2,1)S(1)} copy-done((bf16[1,2,4096,256]{3,2,1,0:T(8,128)(2,1)S(1)}, bf16[1,2,4096,256]{3,2,1,0:T(8,128)(2,1)}, u32[]{:S(2)}) %copy-start.1) | copy-done | bytes 4194328
  28.4 1.0 %copy-done.3 = bf16[3,16,4224]{2,1,0:T(8,128)(2,1)S(1)} copy-done((bf16[3,16,4224]{2,1,0:T(8,128)(2,1)S(1)}, bf16[3,16,4224]{2,1,0:T(8,128)(2,1)}, u32[]{:S(2)}) %copy-start.3) | copy-done | bytes 405528
  29.4 1.6 %copy-done.5 = bf16[1,256,4096]{2,1,0:T(8,128)(2,1)S(1)} copy-done((bf16[1,256,4096]{2,1,0:T(8,128)(2,1)S(1)}, bf16[1,256,4096]{2,1,0:T(8,128)(2,1)}, u32[]{:S(2)}) %copy-start.5) | copy-done | bytes 2097176
  31.0 0.0 copy-start.11
  31.1 4.2 %shard_map.120 = (bf16[16,8320]{1,0:T(8,128)(2,1)S(1)}, bf16[16,8320]{1,0:T(8,128)(2,1)S(1)}, bf16[16,8320]{1,0:T(8,128)(2,1)S(1)}, bf16[16,8320]{1,0:T(8,128)(2...) custom-call(s32[1]{0:T(128)} %bitcast.1.mine, bf16[3,16,4224]{2,1,0:T(8,128)(2,1)S(1)} %copy-done.6, ...), custom_call_target="tpu_custom_call" | custom-call | tf_op jit(solution)/shard_map/pallas_call | solution.py:42
  35.3 0.0 copy-start.4
  35.3 0.6 collective-permute-start.3
  35.9 0.0 collective-permute-done.5.refs_3_.refs_5_
  35.9 0.1 collective-permute-start.7
  36.0 0.0 collective-permute-done.6.refs_4_.refs_6_
  36.0 0.4 collective-permute-start.8
  36.4 1.0 %collective-permute-done.7.refs_5_.refs_7_ = bf16[2,16,4096]{2,1,0:T(8,128)(2,1)S(1)} collective-permute-done((bf16[2,16,4096]{2,1,0:T(8,128)(2,1)S(1)}, bf16[2,16,4096]{2,1,0:T(8,128)(2,1)S(1)}, u32[]{:S(2)}, u32[]{:S(2)}) %collective-permute-start.7) | collective-permute-done | bytes 262176 | tf_op jit(solution)/shard_map/ppermute | solution.py:38
  37.4 0.0 collective-permute-done.3.other.refs_1_
  37.4 0.3 shard_map.121
  37.7 0.6 collective-permute-start.10
  38.3 1.5 %collective-permute-start.9 = (bf16[16,4096]{1,0:T(8,128)(2,1)S(1)}, bf16[16,4096]{1,0:T(8,128)(2,1)S(1)}, u32[]{:S(2)}, u32[]{:S(2)}) collective-permute-start(bf16[16,4096]{1,0:T(8,128)(2,1)S(1)} %get-tuple-element.38), channel_id=1, source_target_pairs={{0,2},{1,3},{2,0},{3,1},{4,6},{5,7},{6,4},{7,5},{8,10},{9,11},{10,... | collective-permute-start | bytes 393224 | tf_op jit(solution)/shard_map/ppermute | solution.py:38
  39.8 0.0 collective-permute-done.8.refs_1_
  39.8 6.6 %collective-permute-done.9.refs_2_ = bf16[16,4096]{1,0:T(8,128)(2,1)S(1)} collective-permute-done((bf16[16,4096]{1,0:T(8,128)(2,1)S(1)}, bf16[16,4096]{1,0:T(8,128)(2,1)S(1)}, u32[]{:S(2)}, u32[]{:S(2)}) %collective-permute-start.9) | collective-permute-done | bytes 131104 | tf_op jit(solution)/shard_map/ppermute | solution.py:38
  46.4 0.0 collective-permute-done.10.refs_3_
  46.5 0.6 shard_map.124
  47.1 0.2 collective-permute-start.13
  47.3 0.0 collective-permute-start.11
  47.3 4.6 %collective-permute-start.15 = (bf16[4,16,896]{2,1,0:T(8,128)(2,1)S(1)}, bf16[4,16,896]{2,1,0:T(8,128)(2,1)S(1)}, u32[]{:S(2)}, u32[]{:S(2)}) collective-permute-start(bf16[4,16,896]{2,1,0:T(8,128)(2,1)S(1)} %get-tuple-element.53.refs_8_), channel_id=1, source_target_pairs={{0,28},{4,24},{8,20},{12,16},{16,12},{20,8},{24,4},{28,0},{1,29},{... | collective-permute-start | bytes 344072 | tf_op jit(solution)/shard_map/ppermute | solution.py:514
  51.9 5.7 %collective-permute-done.15.refs_9_ = bf16[4,16,896]{2,1,0:T(8,128)(2,1)S(1)} collective-permute-done((bf16[4,16,896]{2,1,0:T(8,128)(2,1)S(1)}, bf16[4,16,896]{2,1,0:T(8,128)(2,1)S(1)}, u32[]{:S(2)}, u32[]{:S(2)}) %collective-permute-start.15) | collective-permute-done | bytes 114720 | tf_op jit(solution)/shard_map/ppermute | solution.py:514
  57.6 6.5 %shard_map.126 = (bf16[2,4096,256]{2,1,0:T(8,128)(2,1)}, bf16[256,4096]{1,0:T(8,128)(2,1)}, bf16[1024,128]{1,0:T(8,128)(2,1)}) custom-call(s32[1]{0:T(128)} %bitcast.16.me, bf16[3,16,4224]{2,1,0:T(8,128)(2,1)S(1)} %copy-done.6, bf16[3,16,4224]{2,1,0:T(8,128)(2,1)S(1)} %copy-done.4, bf16[3,16,4224]{2,1,0:T(8,128)(2,1)S(1)} %collective-permute-done.1.refs_2_, ...), custom_call_target="tpu_custom_call" | custom-call | tf_op jit(solution)/shard_map/pallas_call | solution.py:42
  64.1 0.1 collective-permute-done.12.near
  64.2 0.0 collective-permute-done.14.far
  64.2 2.6 %collective-permute-done.11.last_near = bf16[16,4096]{1,0:T(8,128)(2,1)S(1)} collective-permute-done((bf16[16,4096]{1,0:T(8,128)(2,1)S(1)}, bf16[16,4096]{1,0:T(8,128)(2,1)S(1)}, u32[]{:S(2)}, u32[]{:S(2)}) %collective-permute-start.11) | collective-permute-done | bytes 131104 | tf_op jit(solution)/shard_map/ppermute | solution.py:515
  66.8 0.0 collective-permute-done.13.last_far
  66.8 3.0 %shard_map.125 = (bf16[128,4096]{1,0:T(8,128)(2,1)}, bf16[128,4096]{1,0:T(8,128)(2,1)}) custom-call(s32[1]{0:T(128)} %bitcast.odd, bf16[16,4096]{1,0:T(8,128)(2,1)S(1)} %collective-permute-done.11.last_near, bf16[112,4224]{1,0:T(8,128)(2,1)} %collective-permute-done.12.near, bf16[16,4224]{1,0:T(8,128)(2,1)S(1)} %collective-permute-done.13.last_far, ...), custom_call_target="tpu_custom_call" | custom-call | tf_op jit(solution)/shard_map/pallas_call | solution.py:42
  (18 shorter events, 0.0 us)
Async XLA Ops:
  0.6 25.6 %copy-start = (bf16[1,4096,128]{2,1,0:T(8,128)(2,1)S(1)}, bf16[1,4096,128]{2,1,0:T(8,128)(2,1)}, u32[]{:S(2)}) copy-start(bf16[1,4096,128]{2,1,0:T(8,128)(2,1)} %param.10) | copy-start | bytes 3145732
  3.9 22.4 %copy-start.6 = (bf16[3,16,4224]{2,1,0:T(8,128)(2,1)S(1)}, bf16[3,16,4224]{2,1,0:T(8,128)(2,1)}, u32[]{:S(2)}) copy-start(bf16[3,16,4224]{2,1,0:T(8,128)(2,1)} %get-tuple-element.31.refs_0_) | copy-start | bytes 1216516
  3.9 12.6 %collective-permute-start = (bf16[3,16,4224]{2,1,0:T(8,128)(2,1)}, bf16[3,16,4224]{2,1,0:T(8,128)(2,1)S(1)}, u32[]{:S(2)}, u32[]{:S(2)}) collective-permute-start(bf16[3,16,4224]{2,1,0:T(8,128)(2,1)} %get-tuple-element.31.refs_0_), channel_id=1, source_target_pairs={{0,2},{1,3},{2,0},{3,1},{4,6},{5,7},{6,4},{7,5},{8,10},{9,11},{10,... | collective-permute-start | bytes 1216520 | tf_op jit(solution)/shard_map/ppermute | solution.py:38
  6.9 19.3 %collective-permute-start.1 = (bf16[3,16,4224]{2,1,0:T(8,128)(2,1)}, bf16[3,16,4224]{2,1,0:T(8,128)(2,1)S(1)}, u32[]{:S(2)}, u32[]{:S(2)}) collective-permute-start(bf16[3,16,4224]{2,1,0:T(8,128)(2,1)} %get-tuple-element.31.refs_0_), channel_id=1, source_target_pairs={{0,1},{1,0},{2,3},{3,2},{4,5},{5,4},{6,7},{7,6},{8,9},{9,8},{10,11... | collective-permute-start | bytes 1216520 | tf_op jit(solution)/shard_map/ppermute | solution.py:38
  6.9 17.8 %collective-permute-start.4 = (bf16[2,16,4096]{2,1,0:T(8,128)(2,1)}, bf16[2,16,4096]{2,1,0:T(8,128)(2,1)S(1)}, u32[]{:S(2)}, u32[]{:S(2)}) collective-permute-start(bf16[2,16,4096]{2,1,0:T(8,128)(2,1)} %get-tuple-element.35), channel_id=1, source_target_pairs={{0,28},{4,24},{8,20},{12,16},{16,12},{20,8},{24,4},{28,0},{1,29},{... | collective-permute-start | bytes 786440 | tf_op jit(solution)/shard_map/ppermute | solution.py:438
  14.1 50.1 %collective-permute-start.12 = (bf16[112,4224]{1,0:T(8,128)(2,1)}, bf16[112,4224]{1,0:T(8,128)(2,1)}, u32[]{:S(2)}, u32[]{:S(2)}) collective-permute-start(bf16[112,4224]{1,0:T(8,128)(2,1)} %get-tuple-element.48), channel_id=1, source_target_pairs={{0,4},{4,0},{8,12},{12,8},{16,20},{20,16},{24,28},{28,24},{1,5},{5... | collective-permute-start | bytes 2838536 | tf_op jit(solution)/shard_map/ppermute | solution.py:435
  16.5 0.8 %copy-start.2 = (bf16[3,16,4224]{2,1,0:T(8,128)(2,1)}, bf16[3,16,4224]{2,1,0:T(8,128)(2,1)S(1)}, u32[]{:S(2)}) copy-start(bf16[3,16,4224]{2,1,0:T(8,128)(2,1)S(1)} %collective-permute-done.refs_1_.refs_0_) | copy-start | bytes 1216516
  16.5 9.8 %collective-permute-start.2 = (bf16[3,16,4224]{2,1,0:T(8,128)(2,1)S(1)}, bf16[3,16,4224]{2,1,0:T(8,128)(2,1)S(1)}, u32[]{:S(2)}, u32[]{:S(2)}) collective-permute-start(bf16[3,16,4224]{2,1,0:T(8,128)(2,1)S(1)} %collective-permute-done.refs_1_.refs_0_), channel_id=1, source_target_pairs={{0,1},{1,0},{2,3},{3,2},{4,5},{5,4},{6,7},{7,6},{8,9},{9,8},{10,11... | collective-permute-start | bytes 1216520 | tf_op jit(solution)/shard_map/ppermute | solution.py:38
  19.9 44.3 %collective-permute-start.14 = (bf16[112,4096]{1,0:T(8,128)(2,1)}, bf16[112,4096]{1,0:T(8,128)(2,1)}, u32[]{:S(2)}, u32[]{:S(2)}) collective-permute-start(bf16[112,4096]{1,0:T(8,128)(2,1)} %get-tuple-element.50), channel_id=1, source_target_pairs={{0,28},{4,8},{8,4},{12,16},{16,12},{20,24},{24,20},{28,0},{1,29},{... | collective-permute-start | bytes 2752520 | tf_op jit(solution)/shard_map/ppermute | solution.py:437
  24.7 11.2 %collective-permute-start.5 = (bf16[2,16,4096]{2,1,0:T(8,128)(2,1)S(1)}, bf16[2,16,4096]{2,1,0:T(8,128)(2,1)S(1)}, u32[]{:S(2)}, u32[]{:S(2)}) collective-permute-start(bf16[2,16,4096]{2,1,0:T(8,128)(2,1)S(1)} %collective-permute-done.4.refs_2_.refs_4_), channel_id=1, source_target_pairs={{0,2},{1,3},{2,0},{3,1},{4,6},{5,7},{6,4},{7,5},{8,10},{9,11},{10,... | collective-permute-start | bytes 786440 | tf_op jit(solution)/shard_map/ppermute | solution.py:38
  26.2 9.7 %collective-permute-start.6 = (bf16[2,16,4096]{2,1,0:T(8,128)(2,1)S(1)}, bf16[2,16,4096]{2,1,0:T(8,128)(2,1)}, u32[]{:S(2)}, u32[]{:S(2)}) collective-permute-start(bf16[2,16,4096]{2,1,0:T(8,128)(2,1)S(1)} %collective-permute-done.4.refs_2_.refs_4_), channel_id=1, source_target_pairs={{0,1},{1,0},{2,3},{3,2},{4,5},{5,4},{6,7},{7,6},{8,9},{9,8},{10,11... | collective-permute-start | bytes 786440 | tf_op jit(solution)/shard_map/ppermute | solution.py:38
  26.2 2.2 %copy-start.1 = (bf16[1,2,4096,256]{3,2,1,0:T(8,128)(2,1)S(1)}, bf16[1,2,4096,256]{3,2,1,0:T(8,128)(2,1)}, u32[]{:S(2)}) copy-start(bf16[1,2,4096,256]{3,2,1,0:T(8,128)(2,1)} %param.11) | copy-start | bytes 12582916
  28.4 1.0 %copy-start.3 = (bf16[3,16,4224]{2,1,0:T(8,128)(2,1)S(1)}, bf16[3,16,4224]{2,1,0:T(8,128)(2,1)}, u32[]{:S(2)}) copy-start(bf16[3,16,4224]{2,1,0:T(8,128)(2,1)} %copy-done.2) | copy-start | bytes 1216516
  29.4 1.6 %copy-start.5 = (bf16[1,256,4096]{2,1,0:T(8,128)(2,1)S(1)}, bf16[1,256,4096]{2,1,0:T(8,128)(2,1)}, u32[]{:S(2)}) copy-start(bf16[1,256,4096]{2,1,0:T(8,128)(2,1)} %param.12) | copy-start | bytes 6291460
  31.0 15.4 %copy-start.7 = (bf16[16,4096]{1,0:T(8,128)(2,1)S(1)}, bf16[16,4096]{1,0:T(8,128)(2,1)}, u32[]{:S(2)}) copy-start(bf16[16,4096]{1,0:T(8,128)(2,1)} %get-tuple-element.43.refs_9_) | copy-start | bytes 393220
  31.0 15.4 %copy-start.8 = (bf16[16,4096]{1,0:T(8,128)(2,1)S(1)}, bf16[16,4096]{1,0:T(8,128)(2,1)}, u32[]{:S(2)}) copy-start(bf16[16,4096]{1,0:T(8,128)(2,1)} %get-tuple-element.44.refs_10_) | copy-start | bytes 393220
  31.0 15.4 %copy-start.9 = (bf16[16,128]{1,0:T(8,128)(2,1)S(1)}, bf16[16,128]{1,0:T(8,128)(2,1)}, u32[]{:S(2)}) copy-start(bf16[16,128]{1,0:T(8,128)(2,1)} %get-tuple-element.41.refs_7_) | copy-start | bytes 12292
  31.0 15.4 %copy-start.10 = (bf16[16,128]{1,0:T(8,128)(2,1)S(1)}, bf16[16,128]{1,0:T(8,128)(2,1)}, u32[]{:S(2)}) copy-start(bf16[16,128]{1,0:T(8,128)(2,1)} %get-tuple-element.42.refs_8_) | copy-start | bytes 12292
  31.0 15.4 %copy-start.11 = (bf16[16,128]{1,0:T(8,128)(2,1)S(1)}, bf16[16,128]{1,0:T(8,128)(2,1)}, u32[]{:S(2)}) copy-start(bf16[16,128]{1,0:T(8,128)(2,1)} %get-tuple-element.45.refs_11_) | copy-start | bytes 12292
  31.1 15.4 %copy-start.12 = (bf16[16,128]{1,0:T(8,128)(2,1)S(1)}, bf16[16,128]{1,0:T(8,128)(2,1)}, u32[]{:S(2)}) copy-start(bf16[16,128]{1,0:T(8,128)(2,1)} %get-tuple-element.46.refs_12_) | copy-start | bytes 12292
  35.3 22.3 %copy-start.4 = (bf16[3,16,4224]{2,1,0:T(8,128)(2,1)S(1)}, bf16[3,16,4224]{2,1,0:T(8,128)(2,1)}, u32[]{:S(2)}) copy-start(bf16[3,16,4224]{2,1,0:T(8,128)(2,1)} %copy-done.2) | copy-start | bytes 1216516
  35.3 2.1 %collective-permute-start.3 = (bf16[16,8320]{1,0:T(8,128)(2,1)S(1)}, bf16[16,8320]{1,0:T(8,128)(2,1)S(1)}, u32[]{:S(2)}, u32[]{:S(2)}) collective-permute-start(bf16[16,8320]{1,0:T(8,128)(2,1)S(1)} %get-tuple-element.33), channel_id=1, source_target_pairs={{0,1},{1,0},{2,3},{3,2},{4,5},{5,4},{6,7},{7,6},{8,9},{9,8},{10,11... | collective-permute-start | bytes 798728 | tf_op jit(solution)/shard_map/ppermute | solution.py:38
  35.9 1.5 %collective-permute-start.7 = (bf16[2,16,4096]{2,1,0:T(8,128)(2,1)S(1)}, bf16[2,16,4096]{2,1,0:T(8,128)(2,1)S(1)}, u32[]{:S(2)}, u32[]{:S(2)}) collective-permute-start(bf16[2,16,4096]{2,1,0:T(8,128)(2,1)S(1)} %collective-permute-done.5.refs_3_.refs_5_), channel_id=1, source_target_pairs={{0,1},{1,0},{2,3},{3,2},{4,5},{5,4},{6,7},{7,6},{8,9},{9,8},{10,11... | collective-permute-start | bytes 786440 | tf_op jit(solution)/shard_map/ppermute | solution.py:38
  36.0 3.8 %collective-permute-start.8 = (bf16[16,8320]{1,0:T(8,128)(2,1)S(1)}, bf16[16,8320]{1,0:T(8,128)(2,1)S(1)}, u32[]{:S(2)}, u32[]{:S(2)}) collective-permute-start(bf16[16,8320]{1,0:T(8,128)(2,1)S(1)} %get-tuple-element.37), channel_id=1, source_target_pairs={{0,1},{1,0},{2,3},{3,2},{4,5},{5,4},{6,7},{7,6},{8,9},{9,8},{10,11... | collective-permute-start | bytes 798728 | tf_op jit(solution)/shard_map/ppermute | solution.py:38
  37.7 8.7 %collective-permute-start.10 = (bf16[16,4224]{1,0:T(8,128)(2,1)S(1)}, bf16[16,4224]{1,0:T(8,128)(2,1)S(1)}, u32[]{:S(2)}, u32[]{:S(2)}) collective-permute-start(bf16[16,4224]{1,0:T(8,128)(2,1)S(1)} %get-tuple-element.36.own), channel_id=1, source_target_pairs={{0,2},{1,3},{2,0},{3,1},{4,6},{5,7},{6,4},{7,5},{8,10},{9,11},{10,... | collective-permute-start | bytes 405512 | tf_op jit(solution)/shard_map/ppermute | solution.py:38
  38.3 8.1 %collective-permute-start.9 = (bf16[16,4096]{1,0:T(8,128)(2,1)S(1)}, bf16[16,4096]{1,0:T(8,128)(2,1)S(1)}, u32[]{:S(2)}, u32[]{:S(2)}) collective-permute-start(bf16[16,4096]{1,0:T(8,128)(2,1)S(1)} %get-tuple-element.38), channel_id=1, source_target_pairs={{0,2},{1,3},{2,0},{3,1},{4,6},{5,7},{6,4},{7,5},{8,10},{9,11},{10,... | collective-permute-start | bytes 393224 | tf_op jit(solution)/shard_map/ppermute | solution.py:38
  47.1 19.8 %collective-permute-start.13 = (bf16[16,4224]{1,0:T(8,128)(2,1)S(1)}, bf16[16,4224]{1,0:T(8,128)(2,1)S(1)}, u32[]{:S(2)}, u32[]{:S(2)}) collective-permute-start(bf16[16,4224]{1,0:T(8,128)(2,1)S(1)} %get-tuple-element.49), channel_id=1, source_target_pairs={{0,28},{4,8},{8,4},{12,16},{16,12},{20,24},{24,20},{28,0},{1,29},{... | collective-permute-start | bytes 405512 | tf_op jit(solution)/shard_map/ppermute | solution.py:516
  47.3 19.5 %collective-permute-start.11 = (bf16[16,4096]{1,0:T(8,128)(2,1)S(1)}, bf16[16,4096]{1,0:T(8,128)(2,1)S(1)}, u32[]{:S(2)}, u32[]{:S(2)}) collective-permute-start(bf16[16,4096]{1,0:T(8,128)(2,1)S(1)} %get-tuple-element.47), channel_id=1, source_target_pairs={{0,4},{4,0},{8,12},{12,8},{16,20},{20,16},{24,28},{28,24},{1,5},{5... | collective-permute-start | bytes 393224 | tf_op jit(solution)/shard_map/ppermute | solution.py:515
  47.3 10.3 %collective-permute-start.15 = (bf16[4,16,896]{2,1,0:T(8,128)(2,1)S(1)}, bf16[4,16,896]{2,1,0:T(8,128)(2,1)S(1)}, u32[]{:S(2)}, u32[]{:S(2)}) collective-permute-start(bf16[4,16,896]{2,1,0:T(8,128)(2,1)S(1)} %get-tuple-element.53.refs_8_), channel_id=1, source_target_pairs={{0,28},{4,24},{8,20},{12,16},{16,12},{20,8},{24,4},{28,0},{1,29},{... | collective-permute-start | bytes 344072 | tf_op jit(solution)/shard_map/ppermute | solution.py:514

commit v5 on v4

--- a/solution.py
+++ b/solution.py
@@ -123,8 +123,13 @@
     first[...] = rows[:slots, :]
     width = rows.shape[1]
     later[:, :width] = rows[slots:, :]
-    if later.shape[1] > width:
+    spare = later.shape[1] - width
+    if spare == tokens:
         later[:, width:] = jnp.broadcast_to(where, (later.shape[0], tokens)).astype(BF16)
+    else:
+        row = lax.broadcasted_iota(jnp.int32, (later.shape[0], spare), 0)
+        halves = [where[:, k * spare : (k + 1) * spare] for k in (0, 1)]
+        later[:, width:] = jnp.where(row % 2 == 0, halves[0], halves[1]).astype(BF16)
 
 
 def gates(ids, logits, topk, expert):
@@ -173,9 +178,22 @@
 
 def expert_kernel(blocks, topk, mine, *refs):
     pieces, refs = refs[:blocks], refs[blocks:]
-    (router, gate_up, down), refs = refs[:3], refs[3:]
+    sources, refs = refs[:3], refs[3:]
     parts, refs = refs[:blocks], refs[blocks:]
-    basis_out, factors, rows, grads, ids = refs
+    basis_out, factors, rows, grads, ids, router, gate_up, down, sems = refs
+    copies = [
+        pltpu.make_async_copy(source, here, sems.at[k])
+        for k, (source, here) in enumerate(
+            (
+                (sources[1].at[0], gate_up.at[0]),
+                (sources[1].at[1], gate_up.at[1]),
+                (sources[2], down),
+                (sources[0], router),
+            )
+        )
+    ]
+    for copy in copies:
+        copy.start()
     slot_count = pieces[0].shape[1]
     width, hidden_width = gate_up.shape[1], gate_up.shape[2]
     half = blocks * slot_count
@@ -188,10 +206,14 @@
         grads[here, :] = piece[1, :, :width]
         ids[here, :] = piece[0, :, width:].astype(F32)
         ids[there, :] = piece[2, :, width:].astype(F32)
+    copies[0].wait()
+    act_gate = dot(rows[...], gate_up[0])
+    copies[1].wait()
+    act_up = dot(rows[...], gate_up[1])
+    copies[2].wait()
+    back = dot(grads[...], down[...], last_last)
+    copies[3].wait()
     weight, basis = gates(ids[...], dot(rows[...], router[...]), topk, mine[0].astype(F32))
-    act_gate = dot(rows[...], gate_up[0])
-    act_up = dot(rows[...], gate_up[1])
-    back = dot(grads[...], down[...], last_last)
     logistic = jax.nn.sigmoid(act_gate)
     hidden = act_gate * logistic * act_up
     weight_b = weight[:half]
@@ -321,19 +343,48 @@
     router[...] = dot(stacked(pieces_all, 0, mine), lg, first_first).astype(BF16)
 
 
-def place_kernel(odd, last_near, near, last_far, far, *refs):
+def order_of(places):
+    tokens = places.shape[1]
+    place = lax.broadcasted_iota(jnp.int32, (tokens, tokens), 0).astype(F32)
+    return (place == places).astype(F32).astype(BF16)
+
+
+def place_kernel(near, far, near_out, far_out, places):
+    tokens, width = far_out.shape
+    step = width // 4
+    for k, (block, out) in enumerate(((near, near_out), (far, far_out))):
+        spare = block.shape[1] - width
+        if spare == tokens:
+            at = block[:1, width:].astype(F32)
+        else:
+            rows = block[:16, width:]
+            from_lane, to_lane = (
+                lax.broadcasted_iota(jnp.int32, (spare, tokens), axis) for axis in (0, 1)
+            )
+            halves = [
+                dot(rows, (to_lane == from_lane + h * spare).astype(F32).astype(BF16)) for h in (0, 1)
+            ]
+            at = halves[0][:1] + halves[1][1:2]
+        places[k : k + 1] = at
+        order = order_of(at)
+        for c in range(4):
+            cols = slice(c * step, (c + 1) * step)
+            out[:, cols] = dot(order[tokens - block.shape[0] :], block[:, cols], first_first).astype(
+                BF16
+            )
+
+
+def finish_kernel(odd, near, last_near, far, last_far, places, *refs):
     outs, held, sems = refs[:2], refs[2:4], refs[4]
-    tokens, width = held[0].shape
+    tokens, width = near.shape
     step = width // 4
-    place = lax.broadcasted_iota(jnp.int32, (tokens, tokens), 0).astype(F32)
-    orders = [
-        (place == at[:1, width:].astype(F32)).astype(F32).astype(BF16) for at in (near, last_far)
-    ]
+    parts = (near, last_near), (far, last_far)
+    orders = [order_of(places[k : k + 1])[: last.shape[0]] for k, (_, last) in enumerate(parts)]
     for c in range(4):
         cols = slice(c * step, (c + 1) * step)
-        for k, (last, later) in enumerate(((last_near, near), (last_far, far))):
-            rows = jnp.concatenate([last[:, cols], later[:, cols]])
-            held[k][:, cols] = dot(orders[k], rows, first_first).astype(BF16)
+        for k, (early, last) in enumerate(parts):
+            late = dot(orders[k], last[:, cols], first_first)
+            held[k][:, cols] = early[:, cols] + late.astype(BF16)
             for out, from_odd in ((outs[0], k == 0), (outs[1], k == 1)):
 
                 @pl.when((odd[0] == 1) == from_odd)
@@ -347,12 +398,21 @@
 
 
 def placed(odd, last_near, near, last_far, far):
-    tokens, width = far.shape[0] + last_far.shape[0], far.shape[1]
+    slots, width = last_far.shape
+    tokens = far.shape[0] + slots
+    shape = ((tokens, width), BF16)
+    early_near, early_far, places = call(
+        place_kernel,
+        [shape, shape, ((2, tokens), F32)],
+        (near, far),
+        in_specs=[whole] * 2,
+        out_specs=[whole] * 3,
+    )
     return call(
-        place_kernel,
-        [((tokens, width), BF16)] * 2,
-        (odd, last_near, near, last_far, far),
-        in_specs=[scalar] + [whole] * 4,
+        finish_kernel,
+        [shape] * 2,
+        (odd, early_near, last_near, early_far, last_far, places),
+        in_specs=[scalar] + [whole] * 5,
         out_specs=[outside] * 2,
         scratch_shapes=[pltpu.VMEM((tokens, width), BF16)] * 2 + [pltpu.SemaphoreType.DMA((2,))],
     )
@@ -433,7 +493,7 @@
     own_all = everywhere(packed)
     first_near, at_near, to_near = ordered(0, tok_rows, ())
     from_near = lax.ppermute(to_near, "pipe", near(pipe))
-    first_far, at_far, to_far = ordered(1, 0, own_all[1:2])
+    first_far, at_far, to_far = ordered(1, tok_rows // 2, own_all[1:2])
     from_far = lax.ppermute(to_far, "pipe", far(pipe))
     twin_all = everywhere(lax.ppermute(twin_rows, "pipe", twins(pipe)))
     twin = [of_mine(p) for p in twin_all]
@@ -446,12 +506,17 @@
         [((slot_count, lanes), BF16)] * groups
         + [((groups, slot_count, experts), F32), ((rows_all, 3 * hidden_width), BF16)],
         (mine.reshape(1), *own, router_table, gate_up[0], down_proj[0]),
-        in_specs=[scalar] + [whole] * (groups + 3),
+        limit=50,
+        in_specs=[scalar] + [whole] * groups + [outside] * 3,
         out_specs=[whole] * (groups + 2),
         scratch_shapes=[
             pltpu.VMEM((2 * rows_all, width), BF16),
             pltpu.VMEM((rows_all, width), BF16),
             pltpu.VMEM((2 * rows_all, experts), F32),
+            pltpu.VMEM((width, experts), BF16),
+            pltpu.VMEM((2, width, hidden_width), BF16),
+            pltpu.VMEM((hidden_width, width), BF16),
+            pltpu.SemaphoreType.DMA((4,)),
         ],
     )
     if flight > 1:
@@ -491,7 +556,7 @@
         functools.partial(last_kernel, groups, span, len(terms[0])),
         [
             ((slots, width), BF16),
-            ((slots, width + tok_rows), BF16),
+            ((slots, width), BF16),
             ((groups, slot_count, 3 * hidden_width + flight * experts), BF16),
         ],
         (

time: 70.2 us -> 69.2 us (0.986)
  Pallas kernels: 23.1 us -> 27.1 us
  local copies, waits for them, and re-layouts: 5.56 us -> 1.78 us
  waiting for transfers between devices: 17.9 us -> 16.8 us
    pallas_call x8 -> x9, Pallas kernels: 23.1 us -> 27.1 us  [call(): pl.pallas_call(kernel, out_shape=[jax.ShapeDtypeStruct(shape, dtype) for...]
    unnamed x26 -> x20, local copies, waits for them, and re-layouts: 5.56 us -> 1.78 us
    ppermute x1, waiting for transfers between devices: 2.63 us -> 0.24 us  [on_device(): last_near = lax.ppermute(last_near, 'pipe', near(pipe))]
    ppermute x1, starting transfers between devices: 4.56 us -> 2.88 us  [on_device(): twin_wide = lax.ppermute(wide, 'pipe', twins(pipe))]
    ppermute x1, starting transfers between devices: 0.23 us -> 1.9 us  [on_device(): last_far = lax.ppermute(last_far, 'pipe', far(pipe))]
    ppermute x1, waiting for transfers between devices: 0.08 us -> 1.38 us  [on_device(): from_near = lax.ppermute(to_near, 'pipe', near(pipe))]
  transfers between devices with their start and end apart: 16 -> 16, of which waited for: 6 -> 6; matrix products, arithmetic and copies ran while one was open for 0% -> 0% of each run, Pallas kernels for 24% -> 32%
where the time goes in v5:
time: 69.2 us; the launch traced here: 68.9 us
  Pallas kernels  27.1 us (39%)
  starting transfers between devices  22.5 us (33%)
  waiting for transfers between devices  16.8 us (24%)
  local copies, waits for them, and re-layouts  1.78 us (3%)
  between operations  0.81 us (1%)
    pallas_call x9, Pallas kernels, call(): pl.pallas_call(kernel, out_shape=[jax.ShapeDtypeStruct(shape, dtype) for...  27.1 us
    ppermute x10, waiting for transfers between devices, exchanged(): return lax.ppermute(block, 'expert', [(i, i ^ bit) for i in range(count)])  9.49 us
    ppermute x10, starting transfers between devices, exchanged(): return lax.ppermute(block, 'expert', [(i, i ^ bit) for i in range(count)])  7.68 us
    ppermute x1, waiting for transfers between devices, on_device(): twin_wide = lax.ppermute(wide, 'pipe', twins(pipe))  5.65 us
    ppermute x1, starting transfers between devices, on_device(): from_far = lax.ppermute(to_far, 'pipe', far(pipe))  4.87 us
    ppermute x1, starting transfers between devices, on_device(): twin_all = everywhere(lax.ppermute(twin_rows, 'pipe', twins(pipe)))  4.56 us
    ppermute x1, starting transfers between devices, on_device(): twin_wide = lax.ppermute(wide, 'pipe', twins(pipe))  2.88 us
    ppermute x1, starting transfers between devices, on_device(): last_far = lax.ppermute(last_far, 'pipe', far(pipe))  1.9 us
  transfers between devices with their start and end apart: 16, of which 6 were waited for; matrix products, arithmetic and copies ran while one was open for 0% of the time, Pallas kernels for 32%

profile of v5, /device:TPU:0, one launch (start us, length us, event | category | flops | bytes accessed | tf_op | source)
XLA Modules:
  0.0 68.9 jit_solution(1043771699716524191)
XLA Ops:
  0.6 0.0 copy-start
  0.6 3.2 %shard_map.120 = (bf16[3,16,4224]{2,1,0:T(8,128)(2,1)}, bf16[2,16,4096]{2,1,0:T(8,128)(2,1)}, bf16[16,128]{1,0:T(8,128)(2,1)}, bf16[16,128]{1,0:T(8,128)(2,1)}) custom-call(s32[8,128]{1,0:T(8,128)} %bitcast.34, s32[8,128]{1,0:T(8,128)} %bitcast.31, bf16[128,4096]{1,0:T(8,128)(2,1)} %bitcast.30, bf16[128,4096]{1,0:T(8,128)(2,1)} %bitcast.25, ...), custom_call_target="tpu_custom_call" | custom-call | tf_op jit(solution)/shard_map/pallas_call | solution.py:42
  3.9 0.0 copy-start.3
  3.9 3.0 %collective-permute-start.1 = (bf16[3,16,4224]{2,1,0:T(8,128)(2,1)}, bf16[3,16,4224]{2,1,0:T(8,128)(2,1)S(1)}, u32[]{:S(2)}, u32[]{:S(2)}) collective-permute-start(bf16[3,16,4224]{2,1,0:T(8,128)(2,1)} %get-tuple-element.35.refs_0_), channel_id=1, source_target_pairs={{0,2},{1,3},{2,0},{3,1},{4,6},{5,7},{6,4},{7,5},{8,10},{9,11},{10,... | collective-permute-start | bytes 1216520 | tf_op jit(solution)/shard_map/ppermute | solution.py:38
  6.9 0.0 collective-permute-start.3
  6.9 4.6 %collective-permute-start.6 = (bf16[2,16,4096]{2,1,0:T(8,128)(2,1)}, bf16[2,16,4096]{2,1,0:T(8,128)(2,1)S(1)}, u32[]{:S(2)}, u32[]{:S(2)}) collective-permute-start(bf16[2,16,4096]{2,1,0:T(8,128)(2,1)} %get-tuple-element.41), channel_id=1, source_target_pairs={{0,28},{4,24},{8,20},{12,16},{16,12},{20,8},{24,4},{28,0},{1,29},{... | collective-permute-start | bytes 786440 | tf_op jit(solution)/shard_map/ppermute | solution.py:498
  11.4 2.6 %shard_map.119 = (bf16[16,4096]{1,0:T(8,128)(2,1)}, bf16[16,128]{1,0:T(8,128)(2,1)}, bf16[112,4224]{1,0:T(8,128)(2,1)}) custom-call(s32[1]{0:T(128)} %bitcast.odd, s32[8,128]{1,0:T(8,128)} %bitcast.32, s32[8,128]{1,0:T(8,128)} %bitcast.35, bf16[128,4096]{1,0:T(8,128)(2,1)} %bitcast.23, bf16[128,4096]{1,0:T(8,128)(2,1)} %bitcast.26), custom_call_target="tpu_custom_call" | custom-call | tf_op jit(solution)/shard_map/pallas_call | solution.py:42
  14.1 0.6 collective-permute-start
  14.7 1.8 %collective-permute-done.1.refs_0_.refs_1_ = bf16[3,16,4224]{2,1,0:T(8,128)(2,1)S(1)} collective-permute-done((bf16[3,16,4224]{2,1,0:T(8,128)(2,1)}, bf16[3,16,4224]{2,1,0:T(8,128)(2,1)S(1)}, u32[]{:S(2)}, u32[]{:S(2)}) %collective-permute-start.1) | collective-permute-done | bytes 405536 | tf_op jit(solution)/shard_map/ppermute | solution.py:38
  16.5 0.0 collective-permute-start.4
  16.5 0.7 %copy-done.1 = bf16[3,16,4224]{2,1,0:T(8,128)(2,1)} copy-done((bf16[3,16,4224]{2,1,0:T(8,128)(2,1)}, bf16[3,16,4224]{2,1,0:T(8,128)(2,1)S(1)}, u32[]{:S(2)}) %copy-start.1) | copy-done | bytes 405528
  17.2 2.6 %shard_map.121 = (bf16[16,4096]{1,0:T(8,128)(2,1)}, bf16[16,128]{1,0:T(8,128)(2,1)}, bf16[112,4160]{1,0:T(8,128)(2,1)}) custom-call(s32[1]{0:T(128)} %bitcast.odd, s32[8,128]{1,0:T(8,128)} %bitcast.33, s32[8,128]{1,0:T(8,128)} %bitcast.36, bf16[128,4096]{1,0:T(8,128)(2,1)} %bitcast.24, bf16[128,4096]{1,0:T(8,128)(2,1)} %bitcast.27, ...), custom_call_target="tpu_custom_call" | custom-call | tf_op jit(solution)/shard_map/pallas_call | solution.py:42
  19.9 4.9 %collective-permute-start.2 = (bf16[112,4160]{1,0:T(8,128)(2,1)}, bf16[112,4160]{1,0:T(8,128)(2,1)}, u32[]{:S(2)}, u32[]{:S(2)}) collective-permute-start(bf16[112,4160]{1,0:T(8,128)(2,1)} %get-tuple-element.36), channel_id=1, source_target_pairs={{0,28},{4,8},{8,4},{12,16},{16,12},{20,24},{24,20},{28,0},{1,29},{... | collective-permute-start | bytes 2795528 | tf_op jit(solution)/shard_map/ppermute | solution.py:497
  24.7 0.0 collective-permute-done.6.refs_2_.refs_4_
  24.7 1.5 %collective-permute-start.7 = (bf16[2,16,4096]{2,1,0:T(8,128)(2,1)S(1)}, bf16[2,16,4096]{2,1,0:T(8,128)(2,1)S(1)}, u32[]{:S(2)}, u32[]{:S(2)}) collective-permute-start(bf16[2,16,4096]{2,1,0:T(8,128)(2,1)S(1)} %collective-permute-done.6.refs_2_.refs_4_), channel_id=1, source_target_pairs={{0,2},{1,3},{2,0},{3,1},{4,6},{5,7},{6,4},{7,5},{8,10},{9,11},{10,... | collective-permute-start | bytes 786440 | tf_op jit(solution)/shard_map/ppermute | solution.py:38
  26.2 0.0 collective-permute-done.3.refs_2_
  26.2 0.0 collective-permute-start.8
  26.2 0.0 collective-permute-done.4.refs_3_
  26.2 0.0 copy-done
  26.3 0.0 copy-start.2
  26.3 1.0 %copy-done.2 = bf16[3,16,4224]{2,1,0:T(8,128)(2,1)S(1)} copy-done((bf16[3,16,4224]{2,1,0:T(8,128)(2,1)S(1)}, bf16[3,16,4224]{2,1,0:T(8,128)(2,1)}, u32[]{:S(2)}) %copy-start.2) | copy-done | bytes 405528
  27.3 7.3 %shard_map.123 = (bf16[16,8320]{1,0:T(8,128)(2,1)S(1)}, bf16[16,8320]{1,0:T(8,128)(2,1)S(1)}, bf16[16,8320]{1,0:T(8,128)(2,1)S(1)}, bf16[16,8320]{1,0:T(8,128)(2...) custom-call(s32[1]{0:T(128)} %bitcast.10.mine, bf16[3,16,4224]{2,1,0:T(8,128)(2,1)S(1)} %copy-done.3, ...), custom_call_target="tpu_custom_call" | custom-call | tf_op jit(solution)/shard_map/pallas_call | solution.py:42
  34.6 0.6 collective-permute-start.5
  35.1 0.0 collective-permute-done.7.refs_3_.refs_5_
  35.1 0.1 collective-permute-start.9
  35.2 0.0 collective-permute-done.8.refs_4_.refs_6_
  35.2 0.4 collective-permute-start.10
  35.7 1.0 %collective-permute-done.9.refs_5_.refs_7_ = bf16[2,16,4096]{2,1,0:T(8,128)(2,1)S(1)} collective-permute-done((bf16[2,16,4096]{2,1,0:T(8,128)(2,1)S(1)}, bf16[2,16,4096]{2,1,0:T(8,128)(2,1)S(1)}, u32[]{:S(2)}, u32[]{:S(2)}) %collective-permute-start.9) | collective-permute-done | bytes 262176 | tf_op jit(solution)/shard_map/ppermute | solution.py:38
  36.7 0.0 collective-permute-done.5.other.refs_1_
  36.7 0.3 shard_map.124
  36.9 0.6 collective-permute-start.12
  37.6 1.5 %collective-permute-start.11 = (bf16[16,4096]{1,0:T(8,128)(2,1)S(1)}, bf16[16,4096]{1,0:T(8,128)(2,1)S(1)}, u32[]{:S(2)}, u32[]{:S(2)}) collective-permute-start(bf16[16,4096]{1,0:T(8,128)(2,1)S(1)} %get-tuple-element.44), channel_id=1, source_target_pairs={{0,2},{1,3},{2,0},{3,1},{4,6},{5,7},{6,4},{7,5},{8,10},{9,11},{10,... | collective-permute-start | bytes 393224 | tf_op jit(solution)/shard_map/ppermute | solution.py:38
  39.1 0.0 collective-permute-done.10.refs_1_
  39.1 6.6 %collective-permute-done.11.refs_2_ = bf16[16,4096]{1,0:T(8,128)(2,1)S(1)} collective-permute-done((bf16[16,4096]{1,0:T(8,128)(2,1)S(1)}, bf16[16,4096]{1,0:T(8,128)(2,1)S(1)}, u32[]{:S(2)}, u32[]{:S(2)}) %collective-permute-start.11) | collective-permute-done | bytes 131104 | tf_op jit(solution)/shard_map/ppermute | solution.py:38
  45.7 0.0 collective-permute-done.12.refs_3_
  45.7 0.0 copy-done.4
  45.7 0.6 shard_map.125
  46.3 0.1 collective-permute-start.13
  46.4 1.9 %collective-permute-start.14 = (bf16[16,4096]{1,0:T(8,128)(2,1)S(1)}, bf16[16,4096]{1,0:T(8,128)(2,1)S(1)}, u32[]{:S(2)}, u32[]{:S(2)}) collective-permute-start(bf16[16,4096]{1,0:T(8,128)(2,1)S(1)} %get-tuple-element.55), channel_id=1, source_target_pairs={{0,28},{4,8},{8,4},{12,16},{16,12},{20,24},{24,20},{28,0},{1,29},{... | collective-permute-start | bytes 393224 | tf_op jit(solution)/shard_map/ppermute | solution.py:581
  48.3 2.9 %collective-permute-start.15 = (bf16[4,16,896]{2,1,0:T(8,128)(2,1)S(1)}, bf16[4,16,896]{2,1,0:T(8,128)(2,1)S(1)}, u32[]{:S(2)}, u32[]{:S(2)}) collective-permute-start(bf16[4,16,896]{2,1,0:T(8,128)(2,1)S(1)} %get-tuple-element.59.refs_8_), channel_id=1, source_target_pairs={{0,28},{4,24},{8,20},{12,16},{16,12},{20,8},{24,4},{28,0},{1,29},{... | collective-permute-start | bytes 344072 | tf_op jit(solution)/shard_map/ppermute | solution.py:579
  51.2 5.7 %collective-permute-done.15.refs_9_ = bf16[4,16,896]{2,1,0:T(8,128)(2,1)S(1)} collective-permute-done((bf16[4,16,896]{2,1,0:T(8,128)(2,1)S(1)}, bf16[4,16,896]{2,1,0:T(8,128)(2,1)S(1)}, u32[]{:S(2)}, u32[]{:S(2)}) %collective-permute-start.15) | collective-permute-done | bytes 114720 | tf_op jit(solution)/shard_map/ppermute | solution.py:579
  56.8 6.5 %shard_map.127 = (bf16[2,4096,256]{2,1,0:T(8,128)(2,1)}, bf16[256,4096]{1,0:T(8,128)(2,1)}, bf16[1024,128]{1,0:T(8,128)(2,1)}) custom-call(s32[1]{0:T(128)} %bitcast.16.me, bf16[3,16,4224]{2,1,0:T(8,128)(2,1)S(1)} %copy-done.3, bf16[3,16,4224]{2,1,0:T(8,128)(2,1)S(1)} %copy-done.2, bf16[3,16,4224]{2,1,0:T(8,128)(2,1)S(1)} %collective-permute-done.3.refs_2_, ...), custom_call_target="tpu_custom_call" | custom-call | tf_op jit(solution)/shard_map/pallas_call | solution.py:42
  63.3 1.4 %collective-permute-done.near = bf16[112,4224]{1,0:T(8,128)(2,1)} collective-permute-done((bf16[112,4224]{1,0:T(8,128)(2,1)}, bf16[112,4224]{1,0:T(8,128)(2,1)}, u32[]{:S(2)}, u32[]{:S(2)}) %collective-permute-start) | collective-permute-done | bytes 946208 | tf_op jit(solution)/shard_map/ppermute | solution.py:495
  64.7 0.0 collective-permute-done.2.far
  64.7 2.4 %shard_map.122 = (bf16[128,4096]{1,0:T(8,128)(2,1)S(1)}, bf16[128,4096]{1,0:T(8,128)(2,1)S(1)}, f32[2,128]{1,0:T(2,128)S(1)}) custom-call(bf16[112,4224]{1,0:T(8,128)(2,1)} %collective-permute-done.near, bf16[112,4160]{1,0:T(8,128)(2,1)} %collective-permute-done.2.far), custom_call_target="tpu_custom_call" | custom-call | tf_op jit(solution)/shard_map/pallas_call | solution.py:42
  67.1 0.2 collective-permute-done.13.last_near
  67.4 0.0 collective-permute-done.14.last_far
  67.4 1.6 %shard_map.126 = (bf16[128,4096]{1,0:T(8,128)(2,1)}, bf16[128,4096]{1,0:T(8,128)(2,1)}) custom-call(s32[1]{0:T(128)} %bitcast.odd, bf16[128,4096]{1,0:T(8,128)(2,1)S(1)} %get-tuple-element.37.near, bf16[16,4096]{1,0:T(8,128)(2,1)S(1)} %collective-permute-done.13.last_near, bf16[128,4096]{1,0:T(8,128)(2,1)S(1)} %get-tuple-element.54.far, ...), custom_call_target="tpu_custom_call" | custom-call | tf_op jit(solution)/shard_map/pallas_call | solution.py:42
  (13 shorter events, 0.0 us)
Async XLA Ops:
  0.6 25.6 %copy-start = (bf16[1,4096,128]{2,1,0:T(8,128)(2,1)S(1)}, bf16[1,4096,128]{2,1,0:T(8,128)(2,1)}, u32[]{:S(2)}) copy-start(bf16[1,4096,128]{2,1,0:T(8,128)(2,1)} %param.10) | copy-start | bytes 3145732
  3.9 22.4 %copy-start.3 = (bf16[3,16,4224]{2,1,0:T(8,128)(2,1)S(1)}, bf16[3,16,4224]{2,1,0:T(8,128)(2,1)}, u32[]{:S(2)}) copy-start(bf16[3,16,4224]{2,1,0:T(8,128)(2,1)} %get-tuple-element.35.refs_0_) | copy-start | bytes 1216516
  3.9 12.6 %collective-permute-start.1 = (bf16[3,16,4224]{2,1,0:T(8,128)(2,1)}, bf16[3,16,4224]{2,1,0:T(8,128)(2,1)S(1)}, u32[]{:S(2)}, u32[]{:S(2)}) collective-permute-start(bf16[3,16,4224]{2,1,0:T(8,128)(2,1)} %get-tuple-element.35.refs_0_), channel_id=1, source_target_pairs={{0,2},{1,3},{2,0},{3,1},{4,6},{5,7},{6,4},{7,5},{8,10},{9,11},{10,... | collective-permute-start | bytes 1216520 | tf_op jit(solution)/shard_map/ppermute | solution.py:38
  6.9 19.3 %collective-permute-start.3 = (bf16[3,16,4224]{2,1,0:T(8,128)(2,1)}, bf16[3,16,4224]{2,1,0:T(8,128)(2,1)S(1)}, u32[]{:S(2)}, u32[]{:S(2)}) collective-permute-start(bf16[3,16,4224]{2,1,0:T(8,128)(2,1)} %get-tuple-element.35.refs_0_), channel_id=1, source_target_pairs={{0,1},{1,0},{2,3},{3,2},{4,5},{5,4},{6,7},{7,6},{8,9},{9,8},{10,11... | collective-permute-start | bytes 1216520 | tf_op jit(solution)/shard_map/ppermute | solution.py:38
  6.9 17.8 %collective-permute-start.6 = (bf16[2,16,4096]{2,1,0:T(8,128)(2,1)}, bf16[2,16,4096]{2,1,0:T(8,128)(2,1)S(1)}, u32[]{:S(2)}, u32[]{:S(2)}) collective-permute-start(bf16[2,16,4096]{2,1,0:T(8,128)(2,1)} %get-tuple-element.41), channel_id=1, source_target_pairs={{0,28},{4,24},{8,20},{12,16},{16,12},{20,8},{24,4},{28,0},{1,29},{... | collective-permute-start | bytes 786440 | tf_op jit(solution)/shard_map/ppermute | solution.py:498
  14.1 50.6 %collective-permute-start = (bf16[112,4224]{1,0:T(8,128)(2,1)}, bf16[112,4224]{1,0:T(8,128)(2,1)}, u32[]{:S(2)}, u32[]{:S(2)}) collective-permute-start(bf16[112,4224]{1,0:T(8,128)(2,1)} %get-tuple-element.34), channel_id=1, source_target_pairs={{0,4},{4,0},{8,12},{12,8},{16,20},{20,16},{24,28},{28,24},{1,5},{5... | collective-permute-start | bytes 2838536 | tf_op jit(solution)/shard_map/ppermute | solution.py:495
  16.5 0.8 %copy-start.1 = (bf16[3,16,4224]{2,1,0:T(8,128)(2,1)}, bf16[3,16,4224]{2,1,0:T(8,128)(2,1)S(1)}, u32[]{:S(2)}) copy-start(bf16[3,16,4224]{2,1,0:T(8,128)(2,1)S(1)} %collective-permute-done.1.refs_0_.refs_1_) | copy-start | bytes 1216516
  16.5 9.8 %collective-permute-start.4 = (bf16[3,16,4224]{2,1,0:T(8,128)(2,1)S(1)}, bf16[3,16,4224]{2,1,0:T(8,128)(2,1)S(1)}, u32[]{:S(2)}, u32[]{:S(2)}) collective-permute-start(bf16[3,16,4224]{2,1,0:T(8,128)(2,1)S(1)} %collective-permute-done.1.refs_0_.refs_1_), channel_id=1, source_target_pairs={{0,1},{1,0},{2,3},{3,2},{4,5},{5,4},{6,7},{7,6},{8,9},{9,8},{10,11... | collective-permute-start | bytes 1216520 | tf_op jit(solution)/shard_map/ppermute | solution.py:38
  19.9 44.9 %collective-permute-start.2 = (bf16[112,4160]{1,0:T(8,128)(2,1)}, bf16[112,4160]{1,0:T(8,128)(2,1)}, u32[]{:S(2)}, u32[]{:S(2)}) collective-permute-start(bf16[112,4160]{1,0:T(8,128)(2,1)} %get-tuple-element.36), channel_id=1, source_target_pairs={{0,28},{4,8},{8,4},{12,16},{16,12},{20,24},{24,20},{28,0},{1,29},{... | collective-permute-start | bytes 2795528 | tf_op jit(solution)/shard_map/ppermute | solution.py:497
  24.7 10.4 %collective-permute-start.7 = (bf16[2,16,4096]{2,1,0:T(8,128)(2,1)S(1)}, bf16[2,16,4096]{2,1,0:T(8,128)(2,1)S(1)}, u32[]{:S(2)}, u32[]{:S(2)}) collective-permute-start(bf16[2,16,4096]{2,1,0:T(8,128)(2,1)S(1)} %collective-permute-done.6.refs_2_.refs_4_), channel_id=1, source_target_pairs={{0,2},{1,3},{2,0},{3,1},{4,6},{5,7},{6,4},{7,5},{8,10},{9,11},{10,... | collective-permute-start | bytes 786440 | tf_op jit(solution)/shard_map/ppermute | solution.py:38
  26.2 9.0 %collective-permute-start.8 = (bf16[2,16,4096]{2,1,0:T(8,128)(2,1)S(1)}, bf16[2,16,4096]{2,1,0:T(8,128)(2,1)}, u32[]{:S(2)}, u32[]{:S(2)}) collective-permute-start(bf16[2,16,4096]{2,1,0:T(8,128)(2,1)S(1)} %collective-permute-done.6.refs_2_.refs_4_), channel_id=1, source_target_pairs={{0,1},{1,0},{2,3},{3,2},{4,5},{5,4},{6,7},{7,6},{8,9},{9,8},{10,11... | collective-permute-start | bytes 786440 | tf_op jit(solution)/shard_map/ppermute | solution.py:38
  26.3 1.0 %copy-start.2 = (bf16[3,16,4224]{2,1,0:T(8,128)(2,1)S(1)}, bf16[3,16,4224]{2,1,0:T(8,128)(2,1)}, u32[]{:S(2)}) copy-start(bf16[3,16,4224]{2,1,0:T(8,128)(2,1)} %copy-done.1) | copy-start | bytes 1216516
  27.3 18.4 %copy-start.4 = (bf16[16,4096]{1,0:T(8,128)(2,1)S(1)}, bf16[16,4096]{1,0:T(8,128)(2,1)}, u32[]{:S(2)}) copy-start(bf16[16,4096]{1,0:T(8,128)(2,1)} %get-tuple-element.49.refs_9_) | copy-start | bytes 393220
  27.3 18.4 %copy-start.5 = (bf16[16,4096]{1,0:T(8,128)(2,1)S(1)}, bf16[16,4096]{1,0:T(8,128)(2,1)}, u32[]{:S(2)}) copy-start(bf16[16,4096]{1,0:T(8,128)(2,1)} %get-tuple-element.50.refs_10_) | copy-start | bytes 393220
  27.3 18.4 %copy-start.6 = (bf16[16,128]{1,0:T(8,128)(2,1)S(1)}, bf16[16,128]{1,0:T(8,128)(2,1)}, u32[]{:S(2)}) copy-start(bf16[16,128]{1,0:T(8,128)(2,1)} %get-tuple-element.47.refs_7_) | copy-start | bytes 12292
  27.3 18.4 %copy-start.7 = (bf16[16,128]{1,0:T(8,128)(2,1)S(1)}, bf16[16,128]{1,0:T(8,128)(2,1)}, u32[]{:S(2)}) copy-start(bf16[16,128]{1,0:T(8,128)(2,1)} %get-tuple-element.48.refs_8_) | copy-start | bytes 12292
  27.3 18.4 %copy-start.8 = (bf16[16,128]{1,0:T(8,128)(2,1)S(1)}, bf16[16,128]{1,0:T(8,128)(2,1)}, u32[]{:S(2)}) copy-start(bf16[16,128]{1,0:T(8,128)(2,1)} %get-tuple-element.51.refs_11_) | copy-start | bytes 12292
  27.3 18.4 %copy-start.9 = (bf16[16,128]{1,0:T(8,128)(2,1)S(1)}, bf16[16,128]{1,0:T(8,128)(2,1)}, u32[]{:S(2)}) copy-start(bf16[16,128]{1,0:T(8,128)(2,1)} %get-tuple-element.52.refs_12_) | copy-start | bytes 12292
  34.6 2.1 %collective-permute-start.5 = (bf16[16,8320]{1,0:T(8,128)(2,1)S(1)}, bf16[16,8320]{1,0:T(8,128)(2,1)S(1)}, u32[]{:S(2)}, u32[]{:S(2)}) collective-permute-start(bf16[16,8320]{1,0:T(8,128)(2,1)S(1)} %get-tuple-element.39), channel_id=1, source_target_pairs={{0,1},{1,0},{2,3},{3,2},{4,5},{5,4},{6,7},{7,6},{8,9},{9,8},{10,11... | collective-permute-start | bytes 798728 | tf_op jit(solution)/shard_map/ppermute | solution.py:38
  35.1 1.5 %collective-permute-start.9 = (bf16[2,16,4096]{2,1,0:T(8,128)(2,1)S(1)}, bf16[2,16,4096]{2,1,0:T(8,128)(2,1)S(1)}, u32[]{:S(2)}, u32[]{:S(2)}) collective-permute-start(bf16[2,16,4096]{2,1,0:T(8,128)(2,1)S(1)} %collective-permute-done.7.refs_3_.refs_5_), channel_id=1, source_target_pairs={{0,1},{1,0},{2,3},{3,2},{4,5},{5,4},{6,7},{7,6},{8,9},{9,8},{10,11... | collective-permute-start | bytes 786440 | tf_op jit(solution)/shard_map/ppermute | solution.py:38
  35.2 3.8 %collective-permute-start.10 = (bf16[16,8320]{1,0:T(8,128)(2,1)S(1)}, bf16[16,8320]{1,0:T(8,128)(2,1)S(1)}, u32[]{:S(2)}, u32[]{:S(2)}) collective-permute-start(bf16[16,8320]{1,0:T(8,128)(2,1)S(1)} %get-tuple-element.43), channel_id=1, source_target_pairs={{0,1},{1,0},{2,3},{3,2},{4,5},{5,4},{6,7},{7,6},{8,9},{9,8},{10,11... | collective-permute-start | bytes 798728 | tf_op jit(solution)/shard_map/ppermute | solution.py:38
  36.9 8.7 %collective-permute-start.12 = (bf16[16,4224]{1,0:T(8,128)(2,1)S(1)}, bf16[16,4224]{1,0:T(8,128)(2,1)S(1)}, u32[]{:S(2)}, u32[]{:S(2)}) collective-permute-start(bf16[16,4224]{1,0:T(8,128)(2,1)S(1)} %get-tuple-element.42.own), channel_id=1, source_target_pairs={{0,2},{1,3},{2,0},{3,1},{4,6},{5,7},{6,4},{7,5},{8,10},{9,11},{10,... | collective-permute-start | bytes 405512 | tf_op jit(solution)/shard_map/ppermute | solution.py:38
  37.6 8.1 %collective-permute-start.11 = (bf16[16,4096]{1,0:T(8,128)(2,1)S(1)}, bf16[16,4096]{1,0:T(8,128)(2,1)S(1)}, u32[]{:S(2)}, u32[]{:S(2)}) collective-permute-start(bf16[16,4096]{1,0:T(8,128)(2,1)S(1)} %get-tuple-element.44), channel_id=1, source_target_pairs={{0,2},{1,3},{2,0},{3,1},{4,6},{5,7},{6,4},{7,5},{8,10},{9,11},{10,... | collective-permute-start | bytes 393224 | tf_op jit(solution)/shard_map/ppermute | solution.py:38
  46.3 21.0 %collective-permute-start.13 = (bf16[16,4096]{1,0:T(8,128)(2,1)S(1)}, bf16[16,4096]{1,0:T(8,128)(2,1)S(1)}, u32[]{:S(2)}, u32[]{:S(2)}) collective-permute-start(bf16[16,4096]{1,0:T(8,128)(2,1)S(1)} %get-tuple-element.53), channel_id=1, source_target_pairs={{0,4},{4,0},{8,12},{12,8},{16,20},{20,16},{24,28},{28,24},{1,5},{5... | collective-permute-start | bytes 393224 | tf_op jit(solution)/shard_map/ppermute | solution.py:580
  46.4 21.0 %collective-permute-start.14 = (bf16[16,4096]{1,0:T(8,128)(2,1)S(1)}, bf16[16,4096]{1,0:T(8,128)(2,1)S(1)}, u32[]{:S(2)}, u32[]{:S(2)}) collective-permute-start(bf16[16,4096]{1,0:T(8,128)(2,1)S(1)} %get-tuple-element.55), channel_id=1, source_target_pairs={{0,28},{4,8},{8,4},{12,16},{16,12},{20,24},{24,20},{28,0},{1,29},{... | collective-permute-start | bytes 393224 | tf_op jit(solution)/shard_map/ppermute | solution.py:581
  48.3 8.5 %collective-permute-start.15 = (bf16[4,16,896]{2,1,0:T(8,128)(2,1)S(1)}, bf16[4,16,896]{2,1,0:T(8,128)(2,1)S(1)}, u32[]{:S(2)}, u32[]{:S(2)}) collective-permute-start(bf16[4,16,896]{2,1,0:T(8,128)(2,1)S(1)} %get-tuple-element.59.refs_8_), channel_id=1, source_target_pairs={{0,28},{4,24},{8,20},{12,16},{16,12},{20,8},{24,4},{28,0},{1,29},{... | collective-permute-start | bytes 344072 | tf_op jit(solution)/shard_map/ppermute | solution.py:579

commit v6 on v4

--- a/solution.py
+++ b/solution.py
@@ -64,67 +64,86 @@
     return jnp.concatenate(picked, axis=0).astype(BF16)
 
 
-def pick_kernel(flight, slot_count, topk, *refs):
+def token_places(ids, flight):
+    tokens = ids.shape[1]
+    earlier = (
+        lax.broadcasted_iota(jnp.int32, (tokens, tokens), 0)
+        < lax.broadcasted_iota(jnp.int32, (tokens, tokens), 1)
+    ).astype(F32).astype(BF16)
+    token = lax.broadcasted_iota(jnp.int32, (8, tokens), 1).astype(F32)
+    named = jnp.max((ids < flight).astype(F32), axis=0, keepdims=True)
+    named = jnp.broadcast_to(named, (8, tokens))
+    rank = dot(named.astype(BF16), earlier)
+    count = jnp.sum(named, axis=1, keepdims=True)
+    return jnp.where(named > 0.0, rank, count + token - rank)[:1]
+
+
+def order_of(places):
+    tokens = places.shape[1]
+    place = lax.broadcasted_iota(jnp.int32, (tokens, tokens), 0).astype(F32)
+    return (place == places).astype(F32).astype(BF16)
+
+
+def pick_kernel(flight, slot_count, topk, odd, *refs):
     sources, refs = refs[:5], refs[5:]
-    packed, twin, sel_a, sel_b = refs[:4]
-    held, sems = refs[4:9], refs[9]
+    packed, twin, sel_a, sel_b, first_near, first_far, at_near, at_far, to_near, to_far = refs[:10]
+    held, blocks, sems = refs[10:15], refs[15:17], refs[17]
     copies = [
         pltpu.make_async_copy(source, here, sems.at[k])
         for k, (source, here) in enumerate(zip(sources, held))
     ]
-    for copy in copies:
-        copy.start()
+    onward = [
+        pltpu.make_async_copy(block, out, sems.at[5 + k])
+        for k, (block, out) in enumerate(zip(blocks, (to_near, to_far)))
+    ]
     ids_b, ids_a, x_b, grad, x_a = held
     tokens, width = x_b.shape
+    slots = first_near.shape[0]
     lanes = packed.shape[2] - width
-    for k, (ids_ref, select_ref) in enumerate(((ids_b, sel_b), (ids_a, sel_a))):
-        copies[k].wait()
+
+    def send(k, ids_ref, block_ref):
+        first, at, block = ((first_near, at_near), (first_far, at_far))[k] + (blocks[k],)
+        places = token_places(ids_ref[...], flight)
+        at[...] = jnp.broadcast_to(places, at.shape).astype(BF16)
+        rows = dot(order_of(places), block_ref[...]).astype(BF16)
+        first[...] = rows[:slots]
+        block[:, :width] = rows[slots:]
+        if block.shape[1] > width:
+            block[:, width:] = jnp.broadcast_to(places, (tokens - slots, tokens)).astype(BF16)
+        onward[k].start()
+
+    def pick(ids_ref, select_ref, wanted):
         ids = ids_ref[...]
         select = slot_select(ids, flight, slot_count)
         select_ref[...] = select
         spare = jnp.zeros((lanes - topk, tokens), F32)
         numbers = jnp.concatenate([ids.astype(F32), spare], axis=0).astype(BF16)
         slot_ids = dot(select, numbers, last_last).astype(BF16)
-        for place, source in ((0, 2), (1, 3)) if k == 0 else ((2, 4),):
-            copies[source].wait()
+        for place, source in wanted:
             rows = dot(select, held[source][...]).astype(BF16)
             packed[place, :, :width] = rows
             packed[place, :, width:] = slot_ids
             if place < 2:
                 twin[place] = rows
 
-
-def order_kernel(flight, slots, sends_a, odd, ids_a, ids_b, x_a, grad, *refs):
-    first, at, later, ids, block, sems = refs[-6:]
-    for mine, ids_ref, block_ref in ((sends_a, ids_a, x_a), (1 - sends_a, ids_b, grad)):
+    for mine, near, far in ((0, (1, 4), (0, 3)), (1, (0, 3), (1, 4))):
 
         @pl.when(odd[0] == mine)
-        def _(ids_ref=ids_ref, block_ref=block_ref):
-            pltpu.make_async_copy(ids_ref, ids, sems.at[0]).start()
-            pltpu.make_async_copy(block_ref, block, sems.at[1]).start()
-
-    tokens = block.shape[0]
-    earlier = (
-        lax.broadcasted_iota(jnp.int32, (tokens, tokens), 0)
-        < lax.broadcasted_iota(jnp.int32, (tokens, tokens), 1)
-    ).astype(F32).astype(BF16)
-    place = lax.broadcasted_iota(jnp.int32, (tokens, tokens), 0).astype(F32)
-    token = lax.broadcasted_iota(jnp.int32, (8, tokens), 1).astype(F32)
-    pltpu.make_async_copy(ids_a, ids, sems.at[0]).wait()
-    named = jnp.max((ids[...] < flight).astype(F32), axis=0, keepdims=True)
-    named = jnp.broadcast_to(named, (8, tokens))
-    rank = dot(named.astype(BF16), earlier)
-    count = jnp.sum(named, axis=1, keepdims=True)
-    where = jnp.where(named > 0.0, rank, count + token - rank)[:1]
-    at[...] = jnp.broadcast_to(where, at.shape).astype(BF16)
-    order = (place == where).astype(F32).astype(BF16)
-    pltpu.make_async_copy(x_a, block, sems.at[1]).wait()
-    rows = dot(order, block[...]).astype(BF16)
-    first[...] = rows[:slots, :]
-    width = rows.shape[1]
-    later[:, :width] = rows[slots:, :]
-    if later.shape[1] > width:
-        later[:, width:] = jnp.broadcast_to(where, (later.shape[0], tokens)).astype(BF16)
+        def _(near=near, far=far):
+            for k in (*near, *far, 2):
+                copies[k].start()
+            for k in near:
+                copies[k].wait()
+            send(0, *(held[k] for k in near))
+            for k in far:
+                copies[k].wait()
+            send(1, *(held[k] for k in far))
+
+    copies[2].wait()
+    pick(ids_b, sel_b, ((0, 2), (1, 3)))
+    pick(ids_a, sel_a, ((2, 4),))
+    for copy in onward:
+        copy.wait()
 
 
 def gates(ids, logits, topk, expert):
@@ -173,9 +192,22 @@
 
 def expert_kernel(blocks, topk, mine, *refs):
     pieces, refs = refs[:blocks], refs[blocks:]
-    (router, gate_up, down), refs = refs[:3], refs[3:]
+    sources, refs = refs[:3], refs[3:]
     parts, refs = refs[:blocks], refs[blocks:]
-    basis_out, factors, rows, grads, ids = refs
+    basis_out, factors, rows, grads, ids, router, gate_up, down, sems = refs
+    copies = [
+        pltpu.make_async_copy(source, here, sems.at[k])
+        for k, (source, here) in enumerate(
+            (
+                (sources[1].at[0], gate_up.at[0]),
+                (sources[1].at[1], gate_up.at[1]),
+                (sources[2], down),
+                (sources[0], router),
+            )
+        )
+    ]
+    for copy in copies:
+        copy.start()
     slot_count = pieces[0].shape[1]
     width, hidden_width = gate_up.shape[1], gate_up.shape[2]
     half = blocks * slot_count
@@ -188,10 +220,14 @@
         grads[here, :] = piece[1, :, :width]
         ids[here, :] = piece[0, :, width:].astype(F32)
         ids[there, :] = piece[2, :, width:].astype(F32)
+    copies[0].wait()
+    act_gate = dot(rows[...], gate_up[0])
+    copies[1].wait()
+    act_up = dot(rows[...], gate_up[1])
+    copies[2].wait()
+    back = dot(grads[...], down[...], last_last)
+    copies[3].wait()
     weight, basis = gates(ids[...], dot(rows[...], router[...]), topk, mine[0].astype(F32))
-    act_gate = dot(rows[...], gate_up[0])
-    act_up = dot(rows[...], gate_up[1])
-    back = dot(grads[...], down[...], last_last)
     logistic = jax.nn.sigmoid(act_gate)
     hidden = act_gate * logistic * act_up
     weight_b = weight[:half]
@@ -265,8 +301,9 @@
     ):
         more = jnp.where(sends_a, more_a, more_b)
         if slots * blocks != factors.shape[0]:
-            place = lax.broadcasted_iota(jnp.int32, at.shape, 0).astype(F32)
-            row = (place == at[...].astype(F32)).astype(F32).astype(BF16)
+            places = at[...].astype(F32)
+            row = (lax.broadcasted_iota(jnp.int32, places.shape, 0).astype(F32) == places)
+            row = row.astype(F32).astype(BF16)
             slot = jnp.where(sends_a, sel_a[...].astype(F32), sel_b[...].astype(F32)).astype(BF16)
             more = jnp.dot(dot(row, slot, last_last), more, precision=lax.Precision.HIGHEST)
         out[:, :width] = (first[...].astype(F32) + more).astype(BF16)
@@ -287,7 +324,8 @@
     pieces_all = pieces
     if not same:
         pieces_all, refs = refs[: 2 * blocks], refs[2 * blocks :]
-    own_wide, twin_wide, gate_up, down, router = refs
+    own_wide, twin_wide, gate_up, down, router, mark = refs
+    mark[...] = jnp.zeros_like(mark)
     i = pl.program_id(0)
     tile, share_tile = down.shape[1], router.shape[0]
     share = share_tile * pl.num_programs(0)
@@ -321,40 +359,87 @@
     router[...] = dot(stacked(pieces_all, 0, mine), lg, first_first).astype(BF16)
 
 
-def place_kernel(odd, last_near, near, last_far, far, *refs):
-    outs, held, sems = refs[:2], refs[2:4], refs[4]
-    tokens, width = held[0].shape
+def pass_kernel(*refs):
+    pass
+
+
+def place_kernel(to_a, odd, block, last, _, out_a, out_b, mark, held, sem):
+    tokens, width = held.shape
     step = width // 4
-    place = lax.broadcasted_iota(jnp.int32, (tokens, tokens), 0).astype(F32)
-    orders = [
-        (place == at[:1, width:].astype(F32)).astype(F32).astype(BF16) for at in (near, last_far)
-    ]
+    order = order_of(last[:1, width:].astype(F32))
     for c in range(4):
         cols = slice(c * step, (c + 1) * step)
-        for k, (last, later) in enumerate(((last_near, near), (last_far, far))):
-            rows = jnp.concatenate([last[:, cols], later[:, cols]])
-            held[k][:, cols] = dot(orders[k], rows, first_first).astype(BF16)
-            for out, from_odd in ((outs[0], k == 0), (outs[1], k == 1)):
-
-                @pl.when((odd[0] == 1) == from_odd)
-                def _(out=out, k=k, cols=cols):
-                    pltpu.make_async_copy(
-                        held[k].at[:, cols], out.at[:, cols], sems.at[k]
-                    ).start()
-
-    for k, block in enumerate(held):
-        pltpu.make_async_copy(block, outs[k], sems.at[k]).wait()
-
-
-def placed(odd, last_near, near, last_far, far):
-    tokens, width = far.shape[0] + last_far.shape[0], far.shape[1]
+        rows = jnp.concatenate([last[:, cols], block[:, cols]])
+        held[:, cols] = dot(order, rows, first_first).astype(BF16)
+        for mine, out in ((to_a, out_a), (1 - to_a, out_b)):
+
+            @pl.when(odd[0] == mine)
+            def _(out=out, cols=cols):
+                pltpu.make_async_copy(held.at[:, cols], out.at[:, cols], sem).start()
+
+    mark[...] = jnp.zeros_like(mark)
+    pltpu.make_async_copy(held, out_a, sem).wait()
+
+
+def placed(to_a, odd, block, last, after):
+    width = block.shape[1]
+    tokens = block.shape[0] + last.shape[0]
     return call(
-        place_kernel,
+        functools.partial(place_kernel, to_a),
+        [((tokens, width), BF16)] * 2 + [((8, 128), F32)],
+        (odd, block, last, after),
+        in_specs=[scalar] + [whole] * 3,
+        out_specs=[outside] * 2 + [whole],
+        scratch_shapes=[pltpu.VMEM((tokens, width), BF16), pltpu.SemaphoreType.DMA],
+    )
+
+
+def early_kernel(block, _, out, places):
+    tokens, width = out.shape
+    step = width // 4
+    places[...] = jnp.broadcast_to(block[:1, width:].astype(F32), places.shape)
+    order = order_of(places[:1, :])[tokens - block.shape[0] :]
+    for c in range(4):
+        cols = slice(c * step, (c + 1) * step)
+        out[:, cols] = dot(order, block[:, cols], first_first).astype(BF16)
+
+
+def finish_kernel(to_a, odd, early, places, last, *refs):
+    outs, held, sem = refs[-4:-2], refs[-2], refs[-1]
+    tokens, width = held.shape
+    step = width // 4
+    order = order_of(places[:1, :])[: last.shape[0]]
+    for c in range(4):
+        cols = slice(c * step, (c + 1) * step)
+        late = dot(order, last[:, cols], first_first).astype(BF16)
+        held[:, cols] = early[:, cols] + late
+        for mine, out in ((to_a, outs[0]), (1 - to_a, outs[1])):
+
+            @pl.when(odd[0] == mine)
+            def _(out=out, cols=cols):
+                pltpu.make_async_copy(held.at[:, cols], out.at[:, cols], sem).start()
+
+    pltpu.make_async_copy(held, outs[0], sem).wait()
+
+
+def placed_in_two(to_a, odd, block, last, before, after):
+    slots, width = last.shape
+    tokens = block.shape[0] + slots
+    early, places = call(
+        early_kernel,
+        [((tokens, width), BF16), ((8, tokens), F32)],
+        (block, after),
+        in_specs=[whole] * 2,
+        out_specs=[whole] * 2,
+    )
+    return call(
+        functools.partial(finish_kernel, to_a),
         [((tokens, width), BF16)] * 2,
-        (odd, last_near, near, last_far, far),
-        in_specs=[scalar] + [whole] * 4,
+        (odd, early, places, last, *before),
+        in_specs=[scalar] + [whole] * 3 + [outside] * 2,
         out_specs=[outside] * 2,
-        scratch_shapes=[pltpu.VMEM((tokens, width), BF16)] * 2 + [pltpu.SemaphoreType.DMA((2,))],
+        scratch_shapes=[pltpu.VMEM((tokens, width), BF16), pltpu.SemaphoreType.DMA],
+        input_output_aliases={4: 0, 5: 1},
     )
 
 
@@ -375,41 +460,33 @@
     bits = [1 << k for k in reversed(range(groups.bit_length() - 1))]
 
     odd = lax.axis_index("pipe") % 2
-    packed, twin_rows, sel_a, sel_b = call(
+    sources = (route_b[0].T, route_a[0].T, section_in_b[0], grad_out_b[0], section_in_a[0])
+    packed, twin_rows, sel_a, sel_b, first_near, first_far, at_near, at_far, to_near, to_far = call(
         functools.partial(pick_kernel, flight, slot_count, topk),
         [
             ((3, slots, width + experts), BF16),
             ((2, slots, width), BF16),
             ((slots, tok_rows), BF16),
             ((slots, tok_rows), BF16),
+            ((slots, width), BF16),
+            ((slots, width), BF16),
+            ((slots, tok_rows), BF16),
+            ((slots, tok_rows), BF16),
+            ((tok_rows - slots, width + tok_rows), BF16),
+            ((tok_rows - slots, width), BF16),
         ],
-        (route_b[0].T, route_a[0].T, section_in_b[0], grad_out_b[0], section_in_a[0]),
+        (odd.reshape(1), *sources),
         limit=61,
-        in_specs=[outside] * 5,
-        out_specs=[whole] * 4,
+        in_specs=[scalar] + [outside] * 5,
+        out_specs=[whole] * 8 + [outside] * 2,
         scratch_shapes=[pltpu.VMEM((topk, tok_rows), jnp.int32)] * 2
         + [pltpu.VMEM((tok_rows, width), BF16)] * 3
-        + [pltpu.SemaphoreType.DMA((5,))],
-    )
-
-    def ordered(sends_a, lanes, after):
-        return call(
-            functools.partial(order_kernel, flight, slots, sends_a),
-            [
-                ((slots, width), BF16),
-                ((slots, tok_rows), BF16),
-                ((tok_rows - slots, width + lanes), BF16),
-            ],
-            (odd.reshape(1), route_a[0].T, route_b[0].T, section_in_a[0], grad_out_b[0], *after),
-            limit=61,
-            in_specs=[scalar] + [outside] * 4 + [anywhere] * len(after),
-            out_specs=[whole] * 3,
-            scratch_shapes=[
-                pltpu.VMEM((topk, tok_rows), jnp.int32),
-                pltpu.VMEM((tok_rows, width), BF16),
-                pltpu.SemaphoreType.DMA((2,)),
-            ],
-        )
+        + [
+            pltpu.VMEM((tok_rows - slots, width + tok_rows), BF16),
+            pltpu.VMEM((tok_rows - slots, width), BF16),
+        ]
+        + [pltpu.SemaphoreType.DMA((7,))],
+    )
 
     def everywhere(block):
         pieces = [block]
@@ -431,11 +508,18 @@
         return full.reshape(values.shape[:-2] + (slots, values.shape[-1]))
 
     own_all = everywhere(packed)
-    first_near, at_near, to_near = ordered(0, tok_rows, ())
     from_near = lax.ppermute(to_near, "pipe", near(pipe))
-    first_far, at_far, to_far = ordered(1, 0, own_all[1:2])
+    from_twin = lax.ppermute(twin_rows, "pipe", twins(pipe))
+    (to_far,) = call(
+        pass_kernel,
+        [(to_far.shape, BF16)],
+        (to_far, from_twin),
+        in_specs=[outside, anywhere],
+        out_specs=[outside],
+        input_output_aliases={0: 0},
+    )
     from_far = lax.ppermute(to_far, "pipe", far(pipe))
-    twin_all = everywhere(lax.ppermute(twin_rows, "pipe", twins(pipe)))
+    twin_all = everywhere(from_twin)
     twin = [of_mine(p) for p in twin_all]
     own = [of_mine(p) for p in own_all]
     rows_all = groups * slot_count
@@ -446,12 +530,17 @@
         [((slot_count, lanes), BF16)] * groups
         + [((groups, slot_count, experts), F32), ((rows_all, 3 * hidden_width), BF16)],
         (mine.reshape(1), *own, router_table, gate_up[0], down_proj[0]),
-        in_specs=[scalar] + [whole] * (groups + 3),
+        limit=50,
+        in_specs=[scalar] + [whole] * groups + [outside] * 3,
         out_specs=[whole] * (groups + 2),
         scratch_shapes=[
             pltpu.VMEM((2 * rows_all, width), BF16),
             pltpu.VMEM((rows_all, width), BF16),
             pltpu.VMEM((2 * rows_all, experts), F32),
+            pltpu.VMEM((width, experts), BF16),
+            pltpu.VMEM((2, width, hidden_width), BF16),
+            pltpu.VMEM((hidden_width, width), BF16),
+            pltpu.SemaphoreType.DMA((4,)),
         ],
     )
     if flight > 1:
@@ -520,12 +609,13 @@
     tile = width // tiles
     same = flight == 1
     held = (*own, *twin) if same else (*own, *twin, *own_all, *twin_all)
-    grad_gate_up, grad_down, grad_router = call(
+    grad_gate_up, grad_down, grad_router, mark = call(
         functools.partial(grads_kernel, groups, hidden_width, experts, same),
         [
             ((2, width, hidden_width), BF16),
             ((hidden_width, width), BF16),
             ((share, experts), BF16),
+            ((8, 128), F32),
         ],
         (me.reshape(1), *held, wide, twin_wide),
         grid=(tiles,),
@@ -534,9 +624,12 @@
             pl.BlockSpec((2, tile, hidden_width), lambda i: (0, i, 0)),
             pl.BlockSpec((hidden_width, tile), lambda i: (0, i)),
             pl.BlockSpec((share // tiles, experts), lambda i: (i, 0)),
+            pl.BlockSpec((8, 128), lambda i: (0, 0)),
         ],
     )
-    section_out_a, grad_in_b = placed(odd.reshape(1), last_near, from_near, last_far, from_far)
+    odd = odd.reshape(1)
+    *outs, mark = placed(0, odd, from_far, last_far, mark)
+    section_out_a, grad_in_b = placed_in_two(1, odd, from_near, last_near, outs, mark)
     return (
         section_out_a[None],
         grad_in_b[None],

time: 70.2 us -> 68.5 us (0.976)
  local copies, waits for them, and re-layouts: 5.56 us -> 1.02 us
  waiting for transfers between devices: 17.9 us -> 21.1 us
    unnamed x26 -> x16, local copies, waits for them, and re-layouts: 5.56 us -> 1.02 us
    ppermute x10, waiting for transfers between devices: 9.49 us -> 12.2 us  [exchanged(): return lax.ppermute(block, 'expert', [(i, i ^ bit) for i in range(count)])]
    ppermute x1, starting transfers between devices: 0.01 us -> 1.98 us  [on_device(): last_near = lax.ppermute(last_near, 'pipe', near(pipe))]
    ppermute x1, waiting for transfers between devices: 0.08 us -> 1.76 us  [on_device(): from_near = lax.ppermute(to_near, 'pipe', near(pipe))]
    ppermute x1, waiting for transfers between devices: 2.63 us -> 1 us  [on_device(): last_near = lax.ppermute(last_near, 'pipe', near(pipe))]
    ppermute x1, waiting for transfers between devices: 0.01 us -> 1.41 us  [on_device(): from_twin = lax.ppermute(twin_rows, 'pipe', twins(pipe))]
    ppermute x1, starting transfers between devices: 4.56 us -> 3.44 us  [on_device(): twin_wide = lax.ppermute(wide, 'pipe', twins(pipe))]
    ppermute x1, waiting for transfers between devices: 5.73 us -> 4.74 us  [on_device(): twin_wide = lax.ppermute(wide, 'pipe', twins(pipe))]
  transfers between devices with their start and end apart: 16 -> 16, of which waited for: 6 -> 7; matrix products, arithmetic and copies ran while one was open for 0% -> 0% of each run, Pallas kernels for 24% -> 26%
where the time goes in v6:
time: 68.5 us; the launch traced here: 68.2 us
  Pallas kernels  23.3 us (34%)
  starting transfers between devices  22 us (32%)
  waiting for transfers between devices  21.1 us (31%)
  local copies, waits for them, and re-layouts  1.02 us (1%)
  between operations  0.79 us (1%)
    pallas_call x9, Pallas kernels, call(): pl.pallas_call(kernel, out_shape=[jax.ShapeDtypeStruct(shape, dtype) for...  23.3 us
    ppermute x10, waiting for transfers between devices, exchanged(): return lax.ppermute(block, 'expert', [(i, i ^ bit) for i in range(count)])  12.2 us
    ppermute x10, starting transfers between devices, exchanged(): return lax.ppermute(block, 'expert', [(i, i ^ bit) for i in range(count)])  6.76 us
    ppermute x1, waiting for transfers between devices, on_device(): twin_wide = lax.ppermute(wide, 'pipe', twins(pipe))  4.74 us
    ppermute x1, starting transfers between devices, on_device(): from_twin = lax.ppermute(twin_rows, 'pipe', twins(pipe))  4.56 us
    ppermute x1, starting transfers between devices, on_device(): from_far = lax.ppermute(to_far, 'pipe', far(pipe))  4.39 us
    ppermute x1, starting transfers between devices, on_device(): twin_wide = lax.ppermute(wide, 'pipe', twins(pipe))  3.44 us
    ppermute x1, starting transfers between devices, on_device(): last_near = lax.ppermute(last_near, 'pipe', near(pipe))  1.98 us
  transfers between devices with their start and end apart: 16, of which 7 were waited for; matrix products, arithmetic and copies ran while one was open for 0% of the time, Pallas kernels for 26%

profile of v6, /device:TPU:0, one launch (start us, length us, event | category | flops | bytes accessed | tf_op | source)
XLA Modules:
  0.0 68.2 jit_solution(10928896681347969818)
XLA Ops:
  0.6 0.0 copy-start
  0.7 4.3 %shard_map.119 = (bf16[3,16,4224]{2,1,0:T(8,128)(2,1)}, bf16[2,16,4096]{2,1,0:T(8,128)(2,1)}, bf16[16,128]{1,0:T(8,128)(2,1)}, bf16[16,128]{1,0:T(8,128)(2,1)}, ...) custom-call(s32[1]{0:T(128)} %bitcast.odd, ...), custom_call_target="tpu_custom_call" | custom-call | tf_op jit(solution)/shard_map/pallas_call | solution.py:42
  5.0 3.0 %collective-permute-start.3 = (bf16[3,16,4224]{2,1,0:T(8,128)(2,1)}, bf16[3,16,4224]{2,1,0:T(8,128)(2,1)S(1)}, u32[]{:S(2)}, u32[]{:S(2)}) collective-permute-start(bf16[3,16,4224]{2,1,0:T(8,128)(2,1)} %get-tuple-element.40.refs_0_), channel_id=1, source_target_pairs={{0,2},{1,3},{2,0},{3,1},{4,6},{5,7},{6,4},{7,5},{8,10},{9,11},{10,... | collective-permute-start | bytes 1216520 | tf_op jit(solution)/shard_map/ppermute | solution.py:38
  8.0 4.6 %collective-permute-start.1 = (bf16[2,16,4096]{2,1,0:T(8,128)(2,1)}, bf16[2,16,4096]{2,1,0:T(8,128)(2,1)S(1)}, u32[]{:S(2)}, u32[]{:S(2)}) collective-permute-start(bf16[2,16,4096]{2,1,0:T(8,128)(2,1)} %get-tuple-element.39), channel_id=1, source_target_pairs={{0,28},{4,24},{8,20},{12,16},{16,12},{20,8},{24,4},{28,0},{1,29},{... | collective-permute-start | bytes 786440 | tf_op jit(solution)/shard_map/ppermute | solution.py:512
  12.6 0.0 collective-permute-start.4
  12.6 0.5 collective-permute-start
  13.1 4.5 %collective-permute-done.3.refs_1_ = bf16[3,16,4224]{2,1,0:T(8,128)(2,1)S(1)} collective-permute-done((bf16[3,16,4224]{2,1,0:T(8,128)(2,1)}, bf16[3,16,4224]{2,1,0:T(8,128)(2,1)S(1)}, u32[]{:S(2)}, u32[]{:S(2)}) %collective-permute-start.3) | collective-permute-done | bytes 405536 | tf_op jit(solution)/shard_map/ppermute | solution.py:38
  17.6 0.0 collective-permute-start.5
  17.6 1.4 %collective-permute-done.1.refs_1_.refs_2_.refs_4_ = bf16[2,16,4096]{2,1,0:T(8,128)(2,1)S(1)} collective-permute-done((bf16[2,16,4096]{2,1,0:T(8,128)(2,1)}, bf16[2,16,4096]{2,1,0:T(8,128)(2,1)S(1)}, u32[]{:S(2)}, u32[]{:S(2)}) %collective-permute-start.1) | collective-permute-done | bytes 262176 | tf_op jit(solution)/shard_map/ppermute | solution.py:512
  19.0 4.4 %collective-permute-start.2 = (bf16[112,4096]{1,0:T(8,128)(2,1)}, bf16[112,4096]{1,0:T(8,128)(2,1)}, u32[]{:S(2)}, u32[]{:S(2)}) collective-permute-start(bf16[112,4096]{1,0:T(8,128)(2,1)} %shard_map.120), channel_id=1, source_target_pairs={{0,28},{4,8},{8,4},{12,16},{16,12},{20,24},{24,20},{28,0},{1,29},{... | collective-permute-start | bytes 2752520 | tf_op jit(solution)/shard_map/ppermute | solution.py:521
  23.4 0.6 collective-permute-start.7
  24.0 0.0 collective-permute-done.4.refs_2_
  24.0 0.0 collective-permute-start.8
  24.0 0.0 collective-permute-done.5.refs_3_
  24.0 0.0 copy-done
  24.0 0.0 copy-start.1
  24.0 1.0 %copy-done.1 = bf16[3,16,4224]{2,1,0:T(8,128)(2,1)S(1)} copy-done((bf16[3,16,4224]{2,1,0:T(8,128)(2,1)S(1)}, bf16[3,16,4224]{2,1,0:T(8,128)(2,1)}, u32[]{:S(2)}) %copy-start.1) | copy-done | bytes 405528
  25.0 7.3 %shard_map.121 = (bf16[16,8320]{1,0:T(8,128)(2,1)S(1)}, bf16[16,8320]{1,0:T(8,128)(2,1)S(1)}, bf16[16,8320]{1,0:T(8,128)(2,1)S(1)}, bf16[16,8320]{1,0:T(8,128)(2...) custom-call(s32[1]{0:T(128)} %bitcast.8.mine, bf16[3,16,4224]{2,1,0:T(8,128)(2,1)S(1)} %copy-done.1, ...), custom_call_target="tpu_custom_call" | custom-call | tf_op jit(solution)/shard_map/pallas_call | solution.py:42
  32.3 0.6 collective-permute-start.6
  32.9 0.0 collective-permute-done.7.refs_3_.refs_5_
  32.9 0.1 collective-permute-start.9
  33.0 0.0 collective-permute-done.8.refs_4_.refs_6_
  33.0 0.4 collective-permute-start.10
  33.4 1.0 %collective-permute-done.9.refs_5_.refs_7_ = bf16[2,16,4096]{2,1,0:T(8,128)(2,1)S(1)} collective-permute-done((bf16[2,16,4096]{2,1,0:T(8,128)(2,1)S(1)}, bf16[2,16,4096]{2,1,0:T(8,128)(2,1)S(1)}, u32[]{:S(2)}, u32[]{:S(2)}) %collective-permute-start.9) | collective-permute-done | bytes 262176 | tf_op jit(solution)/shard_map/ppermute | solution.py:38
  34.4 0.0 collective-permute-done.6.other.refs_1_
  34.4 0.3 shard_map.122
  34.7 1.5 %collective-permute-start.12 = (bf16[16,4224]{1,0:T(8,128)(2,1)S(1)}, bf16[16,4224]{1,0:T(8,128)(2,1)S(1)}, u32[]{:S(2)}, u32[]{:S(2)}) collective-permute-start(bf16[16,4224]{1,0:T(8,128)(2,1)S(1)} %get-tuple-element.44.own), channel_id=1, source_target_pairs={{0,2},{1,3},{2,0},{3,1},{4,6},{5,7},{6,4},{7,5},{8,10},{9,11},{10,... | collective-permute-start | bytes 405512 | tf_op jit(solution)/shard_map/ppermute | solution.py:38
  36.2 0.6 collective-permute-start.11
  36.8 0.0 collective-permute-done.10.refs_1_
  36.8 6.6 %collective-permute-done.11.refs_2_ = bf16[16,4096]{1,0:T(8,128)(2,1)S(1)} collective-permute-done((bf16[16,4096]{1,0:T(8,128)(2,1)S(1)}, bf16[16,4096]{1,0:T(8,128)(2,1)S(1)}, u32[]{:S(2)}, u32[]{:S(2)}) %collective-permute-start.11) | collective-permute-done | bytes 131104 | tf_op jit(solution)/shard_map/ppermute | solution.py:38
  43.4 0.0 collective-permute-done.12.refs_3_
  43.4 0.0 copy-done.4
  43.4 0.0 copy-done.5
  43.4 0.0 copy-done.6
  43.5 0.0 copy-done.7
  43.5 0.6 shard_map.123
  44.1 0.4 collective-permute-start.13
  44.4 2.0 %collective-permute-start.15 = (bf16[16,4096]{1,0:T(8,128)(2,1)S(1)}, bf16[16,4096]{1,0:T(8,128)(2,1)S(1)}, u32[]{:S(2)}, u32[]{:S(2)}) collective-permute-start(bf16[16,4096]{1,0:T(8,128)(2,1)S(1)} %get-tuple-element.61), channel_id=1, source_target_pairs={{0,4},{4,0},{8,12},{12,8},{16,20},{20,16},{24,28},{28,24},{1,5},{5... | collective-permute-start | bytes 393224 | tf_op jit(solution)/shard_map/ppermute | solution.py:604
  46.4 3.4 %collective-permute-start.14 = (bf16[4,16,896]{2,1,0:T(8,128)(2,1)S(1)}, bf16[4,16,896]{2,1,0:T(8,128)(2,1)S(1)}, u32[]{:S(2)}, u32[]{:S(2)}) collective-permute-start(bf16[4,16,896]{2,1,0:T(8,128)(2,1)S(1)} %get-tuple-element.56.refs_8_), channel_id=1, source_target_pairs={{0,28},{4,24},{8,20},{12,16},{16,12},{20,8},{24,4},{28,0},{1,29},{... | collective-permute-start | bytes 344072 | tf_op jit(solution)/shard_map/ppermute | solution.py:603
  49.8 4.7 %collective-permute-done.14.refs_9_ = bf16[4,16,896]{2,1,0:T(8,128)(2,1)S(1)} collective-permute-done((bf16[4,16,896]{2,1,0:T(8,128)(2,1)S(1)}, bf16[4,16,896]{2,1,0:T(8,128)(2,1)S(1)}, u32[]{:S(2)}, u32[]{:S(2)}) %collective-permute-start.14) | collective-permute-done | bytes 114720 | tf_op jit(solution)/shard_map/ppermute | solution.py:603
  54.6 5.5 %shard_map.124 = (bf16[2,4096,256]{2,1,0:T(8,128)(2,1)}, bf16[256,4096]{1,0:T(8,128)(2,1)}, bf16[1024,128]{1,0:T(8,128)(2,1)}, f32[8,128]{1,0:T(8,128)S(1)}) custom-call(s32[1]{0:T(128)} %bitcast.12.me, bf16[3,16,4224]{2,1,0:T(8,128)(2,1)S(1)} %copy-done.1, bf16[3,16,4224]{2,1,0:T(8,128)(2,1)S(1)} %collective-permute-done.3.refs_1_, ...), custom_call_target="tpu_custom_call" | custom-call | tf_op jit(solution)/shard_map/pallas_call | solution.py:42
  60.1 0.0 collective-permute-done.2.block
  60.1 0.0 collective-permute-done.13.last
  60.1 2.4 %shard_map.125 = (bf16[128,4096]{1,0:T(8,128)(2,1)}, bf16[128,4096]{1,0:T(8,128)(2,1)}, f32[8,128]{1,0:T(8,128)S(1)}) custom-call(s32[1]{0:T(128)} %bitcast.odd, bf16[112,4096]{1,0:T(8,128)(2,1)} %collective-permute-done.2.block, bf16[16,4224]{1,0:T(8,128)(2,1)S(1)} %collective-permute-done.13.last, f32[8,128]{1,0:T(8,128)S(1)} %get-tuple-element.57._), custom_call_target="tpu_custom_call" | custom-call | tf_op jit(solution)/shard_map/pallas_call | solution.py:42
  62.6 1.8 %collective-permute-done.block = bf16[112,4224]{1,0:T(8,128)(2,1)} collective-permute-done((bf16[112,4224]{1,0:T(8,128)(2,1)}, bf16[112,4224]{1,0:T(8,128)(2,1)}, u32[]{:S(2)}, u32[]{:S(2)}) %collective-permute-start) | collective-permute-done | bytes 946208 | tf_op jit(solution)/shard_map/ppermute | solution.py:511
  64.3 1.7 %shard_map.126 = (bf16[128,4096]{1,0:T(8,128)(2,1)S(1)}, f32[8,128]{1,0:T(8,128)S(1)}) custom-call(bf16[112,4224]{1,0:T(8,128)(2,1)} %collective-permute-done.block, f32[8,128]{1,0:T(8,128)S(1)} %get-tuple-element.58._), custom_call_target="tpu_custom_call" | custom-call | tf_op jit(solution)/shard_map/pallas_call | solution.py:42
  66.0 1.0 %collective-permute-done.15.last = bf16[16,4096]{1,0:T(8,128)(2,1)S(1)} collective-permute-done((bf16[16,4096]{1,0:T(8,128)(2,1)S(1)}, bf16[16,4096]{1,0:T(8,128)(2,1)S(1)}, u32[]{:S(2)}, u32[]{:S(2)}) %collective-permute-start.15) | collective-permute-done | bytes 131104 | tf_op jit(solution)/shard_map/ppermute | solution.py:604
  67.0 1.2 %shard_map.127 = (bf16[128,4096]{1,0:T(8,128)(2,1)}, bf16[128,4096]{1,0:T(8,128)(2,1)}) custom-call(s32[1]{0:T(128)} %bitcast.odd, bf16[128,4096]{1,0:T(8,128)(2,1)S(1)} %get-tuple-element.59.early, f32[8,128]{1,0:T(8,128)S(1)} %get-tuple-element.60.places, ...), custom_call_target="tpu_custom_call", output_to_operand_aliasing={{0}: (4, {}), {1}: (5, {})} | custom-call | tf_op jit(solution)/shard_map/pallas_call | solution.py:42
  (9 shorter events, 0.0 us)
Async XLA Ops:
  0.6 23.3 %copy-start = (bf16[1,4096,128]{2,1,0:T(8,128)(2,1)S(1)}, bf16[1,4096,128]{2,1,0:T(8,128)(2,1)}, u32[]{:S(2)}) copy-start(bf16[1,4096,128]{2,1,0:T(8,128)(2,1)} %param.10) | copy-start | bytes 3145732
  5.0 12.6 %collective-permute-start.3 = (bf16[3,16,4224]{2,1,0:T(8,128)(2,1)}, bf16[3,16,4224]{2,1,0:T(8,128)(2,1)S(1)}, u32[]{:S(2)}, u32[]{:S(2)}) collective-permute-start(bf16[3,16,4224]{2,1,0:T(8,128)(2,1)} %get-tuple-element.40.refs_0_), channel_id=1, source_target_pairs={{0,2},{1,3},{2,0},{3,1},{4,6},{5,7},{6,4},{7,5},{8,10},{9,11},{10,... | collective-permute-start | bytes 1216520 | tf_op jit(solution)/shard_map/ppermute | solution.py:38
  8.0 11.0 %collective-permute-start.1 = (bf16[2,16,4096]{2,1,0:T(8,128)(2,1)}, bf16[2,16,4096]{2,1,0:T(8,128)(2,1)S(1)}, u32[]{:S(2)}, u32[]{:S(2)}) collective-permute-start(bf16[2,16,4096]{2,1,0:T(8,128)(2,1)} %get-tuple-element.39), channel_id=1, source_target_pairs={{0,28},{4,24},{8,20},{12,16},{16,12},{20,8},{24,4},{28,0},{1,29},{... | collective-permute-start | bytes 786440 | tf_op jit(solution)/shard_map/ppermute | solution.py:512
  12.6 11.4 %collective-permute-start.4 = (bf16[3,16,4224]{2,1,0:T(8,128)(2,1)}, bf16[3,16,4224]{2,1,0:T(8,128)(2,1)S(1)}, u32[]{:S(2)}, u32[]{:S(2)}) collective-permute-start(bf16[3,16,4224]{2,1,0:T(8,128)(2,1)} %get-tuple-element.40.refs_0_), channel_id=1, source_target_pairs={{0,1},{1,0},{2,3},{3,2},{4,5},{5,4},{6,7},{7,6},{8,9},{9,8},{10,11... | collective-permute-start | bytes 1216520 | tf_op jit(solution)/shard_map/ppermute | solution.py:38
  12.6 51.8 %collective-permute-start = (bf16[112,4224]{1,0:T(8,128)(2,1)}, bf16[112,4224]{1,0:T(8,128)(2,1)}, u32[]{:S(2)}, u32[]{:S(2)}) collective-permute-start(bf16[112,4224]{1,0:T(8,128)(2,1)} %get-tuple-element.37), channel_id=1, source_target_pairs={{0,4},{4,0},{8,12},{12,8},{16,20},{20,16},{24,28},{28,24},{1,5},{5... | collective-permute-start | bytes 2838536 | tf_op jit(solution)/shard_map/ppermute | solution.py:511
  17.6 6.4 %collective-permute-start.5 = (bf16[3,16,4224]{2,1,0:T(8,128)(2,1)S(1)}, bf16[3,16,4224]{2,1,0:T(8,128)(2,1)S(1)}, u32[]{:S(2)}, u32[]{:S(2)}) collective-permute-start(bf16[3,16,4224]{2,1,0:T(8,128)(2,1)S(1)} %collective-permute-done.3.refs_1_), channel_id=1, source_target_pairs={{0,1},{1,0},{2,3},{3,2},{4,5},{5,4},{6,7},{7,6},{8,9},{9,8},{10,11... | collective-permute-start | bytes 1216520 | tf_op jit(solution)/shard_map/ppermute | solution.py:38
  19.0 41.1 %collective-permute-start.2 = (bf16[112,4096]{1,0:T(8,128)(2,1)}, bf16[112,4096]{1,0:T(8,128)(2,1)}, u32[]{:S(2)}, u32[]{:S(2)}) collective-permute-start(bf16[112,4096]{1,0:T(8,128)(2,1)} %shard_map.120), channel_id=1, source_target_pairs={{0,28},{4,8},{8,4},{12,16},{16,12},{20,24},{24,20},{28,0},{1,29},{... | collective-permute-start | bytes 2752520 | tf_op jit(solution)/shard_map/ppermute | solution.py:521
  23.4 9.5 %collective-permute-start.7 = (bf16[2,16,4096]{2,1,0:T(8,128)(2,1)S(1)}, bf16[2,16,4096]{2,1,0:T(8,128)(2,1)S(1)}, u32[]{:S(2)}, u32[]{:S(2)}) collective-permute-start(bf16[2,16,4096]{2,1,0:T(8,128)(2,1)S(1)} %collective-permute-done.1.refs_1_.refs_2_.refs_4_), channel_id=1, source_target_pairs={{0,2},{1,3},{2,0},{3,1},{4,6},{5,7},{6,4},{7,5},{8,10},{9,11},{10,... | collective-permute-start | bytes 786440 | tf_op jit(solution)/shard_map/ppermute | solution.py:38
  24.0 9.0 %collective-permute-start.8 = (bf16[2,16,4096]{2,1,0:T(8,128)(2,1)S(1)}, bf16[2,16,4096]{2,1,0:T(8,128)(2,1)S(1)}, u32[]{:S(2)}, u32[]{:S(2)}) collective-permute-start(bf16[2,16,4096]{2,1,0:T(8,128)(2,1)S(1)} %collective-permute-done.1.refs_1_.refs_2_.refs_4_), channel_id=1, source_target_pairs={{0,1},{1,0},{2,3},{3,2},{4,5},{5,4},{6,7},{7,6},{8,9},{9,8},{10,11... | collective-permute-start | bytes 786440 | tf_op jit(solution)/shard_map/ppermute | solution.py:38
  24.0 1.0 %copy-start.1 = (bf16[3,16,4224]{2,1,0:T(8,128)(2,1)S(1)}, bf16[3,16,4224]{2,1,0:T(8,128)(2,1)}, u32[]{:S(2)}) copy-start(bf16[3,16,4224]{2,1,0:T(8,128)(2,1)} %get-tuple-element.40.refs_0_) | copy-start | bytes 1216516
  25.0 18.4 %copy-start.2 = (bf16[16,4096]{1,0:T(8,128)(2,1)S(1)}, bf16[16,4096]{1,0:T(8,128)(2,1)}, u32[]{:S(2)}) copy-start(bf16[16,4096]{1,0:T(8,128)(2,1)} %get-tuple-element.51.refs_9_) | copy-start | bytes 393220
  25.0 18.4 %copy-start.3 = (bf16[16,4096]{1,0:T(8,128)(2,1)S(1)}, bf16[16,4096]{1,0:T(8,128)(2,1)}, u32[]{:S(2)}) copy-start(bf16[16,4096]{1,0:T(8,128)(2,1)} %get-tuple-element.52.refs_10_) | copy-start | bytes 393220
  25.0 18.4 %copy-start.4 = (bf16[16,128]{1,0:T(8,128)(2,1)S(1)}, bf16[16,128]{1,0:T(8,128)(2,1)}, u32[]{:S(2)}) copy-start(bf16[16,128]{1,0:T(8,128)(2,1)} %get-tuple-element.49.refs_7_) | copy-start | bytes 12292
  25.0 18.5 %copy-start.5 = (bf16[16,128]{1,0:T(8,128)(2,1)S(1)}, bf16[16,128]{1,0:T(8,128)(2,1)}, u32[]{:S(2)}) copy-start(bf16[16,128]{1,0:T(8,128)(2,1)} %get-tuple-element.50.refs_8_) | copy-start | bytes 12292
  25.0 18.5 %copy-start.6 = (bf16[16,128]{1,0:T(8,128)(2,1)S(1)}, bf16[16,128]{1,0:T(8,128)(2,1)}, u32[]{:S(2)}) copy-start(bf16[16,128]{1,0:T(8,128)(2,1)} %get-tuple-element.53.refs_11_) | copy-start | bytes 12292
  25.0 18.5 %copy-start.7 = (bf16[16,128]{1,0:T(8,128)(2,1)S(1)}, bf16[16,128]{1,0:T(8,128)(2,1)}, u32[]{:S(2)}) copy-start(bf16[16,128]{1,0:T(8,128)(2,1)} %get-tuple-element.54.refs_12_) | copy-start | bytes 12292
  32.3 2.1 %collective-permute-start.6 = (bf16[16,8320]{1,0:T(8,128)(2,1)S(1)}, bf16[16,8320]{1,0:T(8,128)(2,1)S(1)}, u32[]{:S(2)}, u32[]{:S(2)}) collective-permute-start(bf16[16,8320]{1,0:T(8,128)(2,1)S(1)} %get-tuple-element.42), channel_id=1, source_target_pairs={{0,1},{1,0},{2,3},{3,2},{4,5},{5,4},{6,7},{7,6},{8,9},{9,8},{10,11... | collective-permute-start | bytes 798728 | tf_op jit(solution)/shard_map/ppermute | solution.py:38
  32.9 1.5 %collective-permute-start.9 = (bf16[2,16,4096]{2,1,0:T(8,128)(2,1)S(1)}, bf16[2,16,4096]{2,1,0:T(8,128)(2,1)S(1)}, u32[]{:S(2)}, u32[]{:S(2)}) collective-permute-start(bf16[2,16,4096]{2,1,0:T(8,128)(2,1)S(1)} %collective-permute-done.7.refs_3_.refs_5_), channel_id=1, source_target_pairs={{0,1},{1,0},{2,3},{3,2},{4,5},{5,4},{6,7},{7,6},{8,9},{9,8},{10,11... | collective-permute-start | bytes 786440 | tf_op jit(solution)/shard_map/ppermute | solution.py:38
  33.0 3.8 %collective-permute-start.10 = (bf16[16,8320]{1,0:T(8,128)(2,1)S(1)}, bf16[16,8320]{1,0:T(8,128)(2,1)S(1)}, u32[]{:S(2)}, u32[]{:S(2)}) collective-permute-start(bf16[16,8320]{1,0:T(8,128)(2,1)S(1)} %get-tuple-element.45), channel_id=1, source_target_pairs={{0,1},{1,0},{2,3},{3,2},{4,5},{5,4},{6,7},{7,6},{8,9},{9,8},{10,11... | collective-permute-start | bytes 798728 | tf_op jit(solution)/shard_map/ppermute | solution.py:38
  34.7 8.7 %collective-permute-start.12 = (bf16[16,4224]{1,0:T(8,128)(2,1)S(1)}, bf16[16,4224]{1,0:T(8,128)(2,1)S(1)}, u32[]{:S(2)}, u32[]{:S(2)}) collective-permute-start(bf16[16,4224]{1,0:T(8,128)(2,1)S(1)} %get-tuple-element.44.own), channel_id=1, source_target_pairs={{0,2},{1,3},{2,0},{3,1},{4,6},{5,7},{6,4},{7,5},{8,10},{9,11},{10,... | collective-permute-start | bytes 405512 | tf_op jit(solution)/shard_map/ppermute | solution.py:38
  36.2 7.2 %collective-permute-start.11 = (bf16[16,4096]{1,0:T(8,128)(2,1)S(1)}, bf16[16,4096]{1,0:T(8,128)(2,1)S(1)}, u32[]{:S(2)}, u32[]{:S(2)}) collective-permute-start(bf16[16,4096]{1,0:T(8,128)(2,1)S(1)} %get-tuple-element.46), channel_id=1, source_target_pairs={{0,2},{1,3},{2,0},{3,1},{4,6},{5,7},{6,4},{7,5},{8,10},{9,11},{10,... | collective-permute-start | bytes 393224 | tf_op jit(solution)/shard_map/ppermute | solution.py:38
  44.1 16.1 %collective-permute-start.13 = (bf16[16,4224]{1,0:T(8,128)(2,1)S(1)}, bf16[16,4224]{1,0:T(8,128)(2,1)S(1)}, u32[]{:S(2)}, u32[]{:S(2)}) collective-permute-start(bf16[16,4224]{1,0:T(8,128)(2,1)S(1)} %get-tuple-element.55), channel_id=1, source_target_pairs={{0,28},{4,8},{8,4},{12,16},{16,12},{20,24},{24,20},{28,0},{1,29},{... | collective-permute-start | bytes 405512 | tf_op jit(solution)/shard_map/ppermute | solution.py:605
  44.4 22.6 %collective-permute-start.15 = (bf16[16,4096]{1,0:T(8,128)(2,1)S(1)}, bf16[16,4096]{1,0:T(8,128)(2,1)S(1)}, u32[]{:S(2)}, u32[]{:S(2)}) collective-permute-start(bf16[16,4096]{1,0:T(8,128)(2,1)S(1)} %get-tuple-element.61), channel_id=1, source_target_pairs={{0,4},{4,0},{8,12},{12,8},{16,20},{20,16},{24,28},{28,24},{1,5},{5... | collective-permute-start | bytes 393224 | tf_op jit(solution)/shard_map/ppermute | solution.py:604
  46.4 8.2 %collective-permute-start.14 = (bf16[4,16,896]{2,1,0:T(8,128)(2,1)S(1)}, bf16[4,16,896]{2,1,0:T(8,128)(2,1)S(1)}, u32[]{:S(2)}, u32[]{:S(2)}) collective-permute-start(bf16[4,16,896]{2,1,0:T(8,128)(2,1)S(1)} %get-tuple-element.56.refs_8_), channel_id=1, source_target_pairs={{0,28},{4,24},{8,20},{12,16},{16,12},{20,8},{24,4},{28,0},{1,29},{... | collective-permute-start | bytes 344072 | tf_op jit(solution)/shard_map/ppermute | solution.py:603

commit v7 on v6

--- a/solution.py
+++ b/solution.py
@@ -407,9 +407,9 @@
 def finish_kernel(to_a, odd, early, places, last, *refs):
     outs, held, sem = refs[-4:-2], refs[-2], refs[-1]
     tokens, width = held.shape
-    step = width // 4
+    step = width // 8
     order = order_of(places[:1, :])[: last.shape[0]]
-    for c in range(4):
+    for c in range(8):
         cols = slice(c * step, (c + 1) * step)
         late = dot(order, last[:, cols], first_first).astype(BF16)
         held[:, cols] = early[:, cols] + late

time: 68.5 us -> 68.4 us (level)
  no operation moved by 1% of the time
where the time goes in v7:
time: 68.4 us; the launch traced here: 68.2 us
  Pallas kernels  23.3 us (34%)
  starting transfers between devices  22 us (32%)
  waiting for transfers between devices  21.1 us (31%)
  local copies, waits for them, and re-layouts  1.02 us (1%)
  between operations  0.79 us (1%)
    pallas_call x9, Pallas kernels, call(): pl.pallas_call(kernel, out_shape=[jax.ShapeDtypeStruct(shape, dtype) for...  23.3 us
    ppermute x10, waiting for transfers between devices, exchanged(): return lax.ppermute(block, 'expert', [(i, i ^ bit) for i in range(count)])  12.2 us
    ppermute x10, starting transfers between devices, exchanged(): return lax.ppermute(block, 'expert', [(i, i ^ bit) for i in range(count)])  6.76 us
    ppermute x1, waiting for transfers between devices, on_device(): twin_wide = lax.ppermute(wide, 'pipe', twins(pipe))  4.74 us
    ppermute x1, starting transfers between devices, on_device(): from_twin = lax.ppermute(twin_rows, 'pipe', twins(pipe))  4.56 us
    ppermute x1, starting transfers between devices, on_device(): from_far = lax.ppermute(to_far, 'pipe', far(pipe))  4.39 us
    ppermute x1, starting transfers between devices, on_device(): twin_wide = lax.ppermute(wide, 'pipe', twins(pipe))  3.44 us
    ppermute x1, starting transfers between devices, on_device(): last_near = lax.ppermute(last_near, 'pipe', near(pipe))  1.98 us
  transfers between devices with their start and end apart: 16, of which 7 were waited for; matrix products, arithmetic and copies ran while one was open for 0% of the time, Pallas kernels for 26%

profile of v7, /device:TPU:0, one launch (start us, length us, event | category | flops | bytes accessed | tf_op | source)
XLA Modules:
  0.0 68.2 jit_solution(8675312274876611295)
XLA Ops:
  0.6 0.0 copy-start
  0.7 4.3 %shard_map.119 = (bf16[3,16,4224]{2,1,0:T(8,128)(2,1)}, bf16[2,16,4096]{2,1,0:T(8,128)(2,1)}, bf16[16,128]{1,0:T(8,128)(2,1)}, bf16[16,128]{1,0:T(8,128)(2,1)}, ...) custom-call(s32[1]{0:T(128)} %bitcast.odd, ...), custom_call_target="tpu_custom_call" | custom-call | tf_op jit(solution)/shard_map/pallas_call | solution.py:42
  5.0 3.0 %collective-permute-start.3 = (bf16[3,16,4224]{2,1,0:T(8,128)(2,1)}, bf16[3,16,4224]{2,1,0:T(8,128)(2,1)S(1)}, u32[]{:S(2)}, u32[]{:S(2)}) collective-permute-start(bf16[3,16,4224]{2,1,0:T(8,128)(2,1)} %get-tuple-element.40.refs_0_), channel_id=1, source_target_pairs={{0,2},{1,3},{2,0},{3,1},{4,6},{5,7},{6,4},{7,5},{8,10},{9,11},{10,... | collective-permute-start | bytes 1216520 | tf_op jit(solution)/shard_map/ppermute | solution.py:38
  8.0 4.6 %collective-permute-start.1 = (bf16[2,16,4096]{2,1,0:T(8,128)(2,1)}, bf16[2,16,4096]{2,1,0:T(8,128)(2,1)S(1)}, u32[]{:S(2)}, u32[]{:S(2)}) collective-permute-start(bf16[2,16,4096]{2,1,0:T(8,128)(2,1)} %get-tuple-element.39), channel_id=1, source_target_pairs={{0,28},{4,24},{8,20},{12,16},{16,12},{20,8},{24,4},{28,0},{1,29},{... | collective-permute-start | bytes 786440 | tf_op jit(solution)/shard_map/ppermute | solution.py:512
  12.6 0.0 collective-permute-start.4
  12.6 0.5 collective-permute-start
  13.1 4.5 %collective-permute-done.3.refs_1_ = bf16[3,16,4224]{2,1,0:T(8,128)(2,1)S(1)} collective-permute-done((bf16[3,16,4224]{2,1,0:T(8,128)(2,1)}, bf16[3,16,4224]{2,1,0:T(8,128)(2,1)S(1)}, u32[]{:S(2)}, u32[]{:S(2)}) %collective-permute-start.3) | collective-permute-done | bytes 405536 | tf_op jit(solution)/shard_map/ppermute | solution.py:38
  17.6 0.0 collective-permute-start.5
  17.6 1.4 %collective-permute-done.1.refs_1_.refs_2_.refs_4_ = bf16[2,16,4096]{2,1,0:T(8,128)(2,1)S(1)} collective-permute-done((bf16[2,16,4096]{2,1,0:T(8,128)(2,1)}, bf16[2,16,4096]{2,1,0:T(8,128)(2,1)S(1)}, u32[]{:S(2)}, u32[]{:S(2)}) %collective-permute-start.1) | collective-permute-done | bytes 262176 | tf_op jit(solution)/shard_map/ppermute | solution.py:512
  19.0 4.4 %collective-permute-start.2 = (bf16[112,4096]{1,0:T(8,128)(2,1)}, bf16[112,4096]{1,0:T(8,128)(2,1)}, u32[]{:S(2)}, u32[]{:S(2)}) collective-permute-start(bf16[112,4096]{1,0:T(8,128)(2,1)} %shard_map.120), channel_id=1, source_target_pairs={{0,28},{4,8},{8,4},{12,16},{16,12},{20,24},{24,20},{28,0},{1,29},{... | collective-permute-start | bytes 2752520 | tf_op jit(solution)/shard_map/ppermute | solution.py:521
  23.4 0.6 collective-permute-start.7
  24.0 0.0 collective-permute-done.4.refs_2_
  24.0 0.0 collective-permute-start.8
  24.0 0.0 collective-permute-done.5.refs_3_
  24.0 0.0 copy-done
  24.0 0.0 copy-start.1
  24.0 1.0 %copy-done.1 = bf16[3,16,4224]{2,1,0:T(8,128)(2,1)S(1)} copy-done((bf16[3,16,4224]{2,1,0:T(8,128)(2,1)S(1)}, bf16[3,16,4224]{2,1,0:T(8,128)(2,1)}, u32[]{:S(2)}) %copy-start.1) | copy-done | bytes 405528
  25.0 7.3 %shard_map.121 = (bf16[16,8320]{1,0:T(8,128)(2,1)S(1)}, bf16[16,8320]{1,0:T(8,128)(2,1)S(1)}, bf16[16,8320]{1,0:T(8,128)(2,1)S(1)}, bf16[16,8320]{1,0:T(8,128)(2...) custom-call(s32[1]{0:T(128)} %bitcast.8.mine, bf16[3,16,4224]{2,1,0:T(8,128)(2,1)S(1)} %copy-done.1, ...), custom_call_target="tpu_custom_call" | custom-call | tf_op jit(solution)/shard_map/pallas_call | solution.py:42
  32.3 0.6 collective-permute-start.6
  32.9 0.0 collective-permute-done.7.refs_3_.refs_5_
  32.9 0.1 collective-permute-start.9
  33.0 0.0 collective-permute-done.8.refs_4_.refs_6_
  33.0 0.4 collective-permute-start.10
  33.4 1.0 %collective-permute-done.9.refs_5_.refs_7_ = bf16[2,16,4096]{2,1,0:T(8,128)(2,1)S(1)} collective-permute-done((bf16[2,16,4096]{2,1,0:T(8,128)(2,1)S(1)}, bf16[2,16,4096]{2,1,0:T(8,128)(2,1)S(1)}, u32[]{:S(2)}, u32[]{:S(2)}) %collective-permute-start.9) | collective-permute-done | bytes 262176 | tf_op jit(solution)/shard_map/ppermute | solution.py:38
  34.4 0.0 collective-permute-done.6.other.refs_1_
  34.4 0.3 shard_map.122
  34.7 1.5 %collective-permute-start.12 = (bf16[16,4224]{1,0:T(8,128)(2,1)S(1)}, bf16[16,4224]{1,0:T(8,128)(2,1)S(1)}, u32[]{:S(2)}, u32[]{:S(2)}) collective-permute-start(bf16[16,4224]{1,0:T(8,128)(2,1)S(1)} %get-tuple-element.44.own), channel_id=1, source_target_pairs={{0,2},{1,3},{2,0},{3,1},{4,6},{5,7},{6,4},{7,5},{8,10},{9,11},{10,... | collective-permute-start | bytes 405512 | tf_op jit(solution)/shard_map/ppermute | solution.py:38
  36.2 0.6 collective-permute-start.11
  36.8 0.0 collective-permute-done.10.refs_1_
  36.8 6.6 %collective-permute-done.11.refs_2_ = bf16[16,4096]{1,0:T(8,128)(2,1)S(1)} collective-permute-done((bf16[16,4096]{1,0:T(8,128)(2,1)S(1)}, bf16[16,4096]{1,0:T(8,128)(2,1)S(1)}, u32[]{:S(2)}, u32[]{:S(2)}) %collective-permute-start.11) | collective-permute-done | bytes 131104 | tf_op jit(solution)/shard_map/ppermute | solution.py:38
  43.4 0.0 collective-permute-done.12.refs_3_
  43.4 0.0 copy-done.4
  43.4 0.0 copy-done.5
  43.4 0.0 copy-done.6
  43.5 0.0 copy-done.7
  43.5 0.6 shard_map.123
  44.1 0.4 collective-permute-start.13
  44.4 2.0 %collective-permute-start.15 = (bf16[16,4096]{1,0:T(8,128)(2,1)S(1)}, bf16[16,4096]{1,0:T(8,128)(2,1)S(1)}, u32[]{:S(2)}, u32[]{:S(2)}) collective-permute-start(bf16[16,4096]{1,0:T(8,128)(2,1)S(1)} %get-tuple-element.61), channel_id=1, source_target_pairs={{0,4},{4,0},{8,12},{12,8},{16,20},{20,16},{24,28},{28,24},{1,5},{5... | collective-permute-start | bytes 393224 | tf_op jit(solution)/shard_map/ppermute | solution.py:604
  46.4 3.4 %collective-permute-start.14 = (bf16[4,16,896]{2,1,0:T(8,128)(2,1)S(1)}, bf16[4,16,896]{2,1,0:T(8,128)(2,1)S(1)}, u32[]{:S(2)}, u32[]{:S(2)}) collective-permute-start(bf16[4,16,896]{2,1,0:T(8,128)(2,1)S(1)} %get-tuple-element.56.refs_8_), channel_id=1, source_target_pairs={{0,28},{4,24},{8,20},{12,16},{16,12},{20,8},{24,4},{28,0},{1,29},{... | collective-permute-start | bytes 344072 | tf_op jit(solution)/shard_map/ppermute | solution.py:603
  49.8 4.7 %collective-permute-done.14.refs_9_ = bf16[4,16,896]{2,1,0:T(8,128)(2,1)S(1)} collective-permute-done((bf16[4,16,896]{2,1,0:T(8,128)(2,1)S(1)}, bf16[4,16,896]{2,1,0:T(8,128)(2,1)S(1)}, u32[]{:S(2)}, u32[]{:S(2)}) %collective-permute-start.14) | collective-permute-done | bytes 114720 | tf_op jit(solution)/shard_map/ppermute | solution.py:603
  54.6 5.5 %shard_map.124 = (bf16[2,4096,256]{2,1,0:T(8,128)(2,1)}, bf16[256,4096]{1,0:T(8,128)(2,1)}, bf16[1024,128]{1,0:T(8,128)(2,1)}, f32[8,128]{1,0:T(8,128)S(1)}) custom-call(s32[1]{0:T(128)} %bitcast.12.me, bf16[3,16,4224]{2,1,0:T(8,128)(2,1)S(1)} %copy-done.1, bf16[3,16,4224]{2,1,0:T(8,128)(2,1)S(1)} %collective-permute-done.3.refs_1_, ...), custom_call_target="tpu_custom_call" | custom-call | tf_op jit(solution)/shard_map/pallas_call | solution.py:42
  60.1 0.0 collective-permute-done.2.block
  60.1 0.0 collective-permute-done.13.last
  60.1 2.4 %shard_map.125 = (bf16[128,4096]{1,0:T(8,128)(2,1)}, bf16[128,4096]{1,0:T(8,128)(2,1)}, f32[8,128]{1,0:T(8,128)S(1)}) custom-call(s32[1]{0:T(128)} %bitcast.odd, bf16[112,4096]{1,0:T(8,128)(2,1)} %collective-permute-done.2.block, bf16[16,4224]{1,0:T(8,128)(2,1)S(1)} %collective-permute-done.13.last, f32[8,128]{1,0:T(8,128)S(1)} %get-tuple-element.57._), custom_call_target="tpu_custom_call" | custom-call | tf_op jit(solution)/shard_map/pallas_call | solution.py:42
  62.6 1.8 %collective-permute-done.block = bf16[112,4224]{1,0:T(8,128)(2,1)} collective-permute-done((bf16[112,4224]{1,0:T(8,128)(2,1)}, bf16[112,4224]{1,0:T(8,128)(2,1)}, u32[]{:S(2)}, u32[]{:S(2)}) %collective-permute-start) | collective-permute-done | bytes 946208 | tf_op jit(solution)/shard_map/ppermute | solution.py:511
  64.3 1.7 %shard_map.126 = (bf16[128,4096]{1,0:T(8,128)(2,1)S(1)}, f32[8,128]{1,0:T(8,128)S(1)}) custom-call(bf16[112,4224]{1,0:T(8,128)(2,1)} %collective-permute-done.block, f32[8,128]{1,0:T(8,128)S(1)} %get-tuple-element.58._), custom_call_target="tpu_custom_call" | custom-call | tf_op jit(solution)/shard_map/pallas_call | solution.py:42
  66.0 1.0 %collective-permute-done.15.last = bf16[16,4096]{1,0:T(8,128)(2,1)S(1)} collective-permute-done((bf16[16,4096]{1,0:T(8,128)(2,1)S(1)}, bf16[16,4096]{1,0:T(8,128)(2,1)S(1)}, u32[]{:S(2)}, u32[]{:S(2)}) %collective-permute-start.15) | collective-permute-done | bytes 131104 | tf_op jit(solution)/shard_map/ppermute | solution.py:604
  67.0 1.2 %shard_map.127 = (bf16[128,4096]{1,0:T(8,128)(2,1)}, bf16[128,4096]{1,0:T(8,128)(2,1)}) custom-call(s32[1]{0:T(128)} %bitcast.odd, bf16[128,4096]{1,0:T(8,128)(2,1)S(1)} %get-tuple-element.59.early, f32[8,128]{1,0:T(8,128)S(1)} %get-tuple-element.60.places, ...), custom_call_target="tpu_custom_call", output_to_operand_aliasing={{0}: (4, {}), {1}: (5, {})} | custom-call | tf_op jit(solution)/shard_map/pallas_call | solution.py:42
  (9 shorter events, 0.0 us)
Async XLA Ops:
  0.6 23.3 %copy-start = (bf16[1,4096,128]{2,1,0:T(8,128)(2,1)S(1)}, bf16[1,4096,128]{2,1,0:T(8,128)(2,1)}, u32[]{:S(2)}) copy-start(bf16[1,4096,128]{2,1,0:T(8,128)(2,1)} %param.10) | copy-start | bytes 3145732
  5.0 12.6 %collective-permute-start.3 = (bf16[3,16,4224]{2,1,0:T(8,128)(2,1)}, bf16[3,16,4224]{2,1,0:T(8,128)(2,1)S(1)}, u32[]{:S(2)}, u32[]{:S(2)}) collective-permute-start(bf16[3,16,4224]{2,1,0:T(8,128)(2,1)} %get-tuple-element.40.refs_0_), channel_id=1, source_target_pairs={{0,2},{1,3},{2,0},{3,1},{4,6},{5,7},{6,4},{7,5},{8,10},{9,11},{10,... | collective-permute-start | bytes 1216520 | tf_op jit(solution)/shard_map/ppermute | solution.py:38
  8.0 11.0 %collective-permute-start.1 = (bf16[2,16,4096]{2,1,0:T(8,128)(2,1)}, bf16[2,16,4096]{2,1,0:T(8,128)(2,1)S(1)}, u32[]{:S(2)}, u32[]{:S(2)}) collective-permute-start(bf16[2,16,4096]{2,1,0:T(8,128)(2,1)} %get-tuple-element.39), channel_id=1, source_target_pairs={{0,28},{4,24},{8,20},{12,16},{16,12},{20,8},{24,4},{28,0},{1,29},{... | collective-permute-start | bytes 786440 | tf_op jit(solution)/shard_map/ppermute | solution.py:512
  12.6 11.4 %collective-permute-start.4 = (bf16[3,16,4224]{2,1,0:T(8,128)(2,1)}, bf16[3,16,4224]{2,1,0:T(8,128)(2,1)S(1)}, u32[]{:S(2)}, u32[]{:S(2)}) collective-permute-start(bf16[3,16,4224]{2,1,0:T(8,128)(2,1)} %get-tuple-element.40.refs_0_), channel_id=1, source_target_pairs={{0,1},{1,0},{2,3},{3,2},{4,5},{5,4},{6,7},{7,6},{8,9},{9,8},{10,11... | collective-permute-start | bytes 1216520 | tf_op jit(solution)/shard_map/ppermute | solution.py:38
  12.6 51.8 %collective-permute-start = (bf16[112,4224]{1,0:T(8,128)(2,1)}, bf16[112,4224]{1,0:T(8,128)(2,1)}, u32[]{:S(2)}, u32[]{:S(2)}) collective-permute-start(bf16[112,4224]{1,0:T(8,128)(2,1)} %get-tuple-element.37), channel_id=1, source_target_pairs={{0,4},{4,0},{8,12},{12,8},{16,20},{20,16},{24,28},{28,24},{1,5},{5... | collective-permute-start | bytes 2838536 | tf_op jit(solution)/shard_map/ppermute | solution.py:511
  17.6 6.4 %collective-permute-start.5 = (bf16[3,16,4224]{2,1,0:T(8,128)(2,1)S(1)}, bf16[3,16,4224]{2,1,0:T(8,128)(2,1)S(1)}, u32[]{:S(2)}, u32[]{:S(2)}) collective-permute-start(bf16[3,16,4224]{2,1,0:T(8,128)(2,1)S(1)} %collective-permute-done.3.refs_1_), channel_id=1, source_target_pairs={{0,1},{1,0},{2,3},{3,2},{4,5},{5,4},{6,7},{7,6},{8,9},{9,8},{10,11... | collective-permute-start | bytes 1216520 | tf_op jit(solution)/shard_map/ppermute | solution.py:38
  19.0 41.1 %collective-permute-start.2 = (bf16[112,4096]{1,0:T(8,128)(2,1)}, bf16[112,4096]{1,0:T(8,128)(2,1)}, u32[]{:S(2)}, u32[]{:S(2)}) collective-permute-start(bf16[112,4096]{1,0:T(8,128)(2,1)} %shard_map.120), channel_id=1, source_target_pairs={{0,28},{4,8},{8,4},{12,16},{16,12},{20,24},{24,20},{28,0},{1,29},{... | collective-permute-start | bytes 2752520 | tf_op jit(solution)/shard_map/ppermute | solution.py:521
  23.4 9.5 %collective-permute-start.7 = (bf16[2,16,4096]{2,1,0:T(8,128)(2,1)S(1)}, bf16[2,16,4096]{2,1,0:T(8,128)(2,1)S(1)}, u32[]{:S(2)}, u32[]{:S(2)}) collective-permute-start(bf16[2,16,4096]{2,1,0:T(8,128)(2,1)S(1)} %collective-permute-done.1.refs_1_.refs_2_.refs_4_), channel_id=1, source_target_pairs={{0,2},{1,3},{2,0},{3,1},{4,6},{5,7},{6,4},{7,5},{8,10},{9,11},{10,... | collective-permute-start | bytes 786440 | tf_op jit(solution)/shard_map/ppermute | solution.py:38
  24.0 9.0 %collective-permute-start.8 = (bf16[2,16,4096]{2,1,0:T(8,128)(2,1)S(1)}, bf16[2,16,4096]{2,1,0:T(8,128)(2,1)S(1)}, u32[]{:S(2)}, u32[]{:S(2)}) collective-permute-start(bf16[2,16,4096]{2,1,0:T(8,128)(2,1)S(1)} %collective-permute-done.1.refs_1_.refs_2_.refs_4_), channel_id=1, source_target_pairs={{0,1},{1,0},{2,3},{3,2},{4,5},{5,4},{6,7},{7,6},{8,9},{9,8},{10,11... | collective-permute-start | bytes 786440 | tf_op jit(solution)/shard_map/ppermute | solution.py:38
  24.0 1.0 %copy-start.1 = (bf16[3,16,4224]{2,1,0:T(8,128)(2,1)S(1)}, bf16[3,16,4224]{2,1,0:T(8,128)(2,1)}, u32[]{:S(2)}) copy-start(bf16[3,16,4224]{2,1,0:T(8,128)(2,1)} %get-tuple-element.40.refs_0_) | copy-start | bytes 1216516
  25.0 18.4 %copy-start.2 = (bf16[16,4096]{1,0:T(8,128)(2,1)S(1)}, bf16[16,4096]{1,0:T(8,128)(2,1)}, u32[]{:S(2)}) copy-start(bf16[16,4096]{1,0:T(8,128)(2,1)} %get-tuple-element.51.refs_9_) | copy-start | bytes 393220
  25.0 18.4 %copy-start.3 = (bf16[16,4096]{1,0:T(8,128)(2,1)S(1)}, bf16[16,4096]{1,0:T(8,128)(2,1)}, u32[]{:S(2)}) copy-start(bf16[16,4096]{1,0:T(8,128)(2,1)} %get-tuple-element.52.refs_10_) | copy-start | bytes 393220
  25.0 18.4 %copy-start.4 = (bf16[16,128]{1,0:T(8,128)(2,1)S(1)}, bf16[16,128]{1,0:T(8,128)(2,1)}, u32[]{:S(2)}) copy-start(bf16[16,128]{1,0:T(8,128)(2,1)} %get-tuple-element.49.refs_7_) | copy-start | bytes 12292
  25.0 18.5 %copy-start.5 = (bf16[16,128]{1,0:T(8,128)(2,1)S(1)}, bf16[16,128]{1,0:T(8,128)(2,1)}, u32[]{:S(2)}) copy-start(bf16[16,128]{1,0:T(8,128)(2,1)} %get-tuple-element.50.refs_8_) | copy-start | bytes 12292
  25.0 18.5 %copy-start.6 = (bf16[16,128]{1,0:T(8,128)(2,1)S(1)}, bf16[16,128]{1,0:T(8,128)(2,1)}, u32[]{:S(2)}) copy-start(bf16[16,128]{1,0:T(8,128)(2,1)} %get-tuple-element.53.refs_11_) | copy-start | bytes 12292
  25.0 18.5 %copy-start.7 = (bf16[16,128]{1,0:T(8,128)(2,1)S(1)}, bf16[16,128]{1,0:T(8,128)(2,1)}, u32[]{:S(2)}) copy-start(bf16[16,128]{1,0:T(8,128)(2,1)} %get-tuple-element.54.refs_12_) | copy-start | bytes 12292
  32.3 2.1 %collective-permute-start.6 = (bf16[16,8320]{1,0:T(8,128)(2,1)S(1)}, bf16[16,8320]{1,0:T(8,128)(2,1)S(1)}, u32[]{:S(2)}, u32[]{:S(2)}) collective-permute-start(bf16[16,8320]{1,0:T(8,128)(2,1)S(1)} %get-tuple-element.42), channel_id=1, source_target_pairs={{0,1},{1,0},{2,3},{3,2},{4,5},{5,4},{6,7},{7,6},{8,9},{9,8},{10,11... | collective-permute-start | bytes 798728 | tf_op jit(solution)/shard_map/ppermute | solution.py:38
  32.9 1.5 %collective-permute-start.9 = (bf16[2,16,4096]{2,1,0:T(8,128)(2,1)S(1)}, bf16[2,16,4096]{2,1,0:T(8,128)(2,1)S(1)}, u32[]{:S(2)}, u32[]{:S(2)}) collective-permute-start(bf16[2,16,4096]{2,1,0:T(8,128)(2,1)S(1)} %collective-permute-done.7.refs_3_.refs_5_), channel_id=1, source_target_pairs={{0,1},{1,0},{2,3},{3,2},{4,5},{5,4},{6,7},{7,6},{8,9},{9,8},{10,11... | collective-permute-start | bytes 786440 | tf_op jit(solution)/shard_map/ppermute | solution.py:38
  33.0 3.8 %collective-permute-start.10 = (bf16[16,8320]{1,0:T(8,128)(2,1)S(1)}, bf16[16,8320]{1,0:T(8,128)(2,1)S(1)}, u32[]{:S(2)}, u32[]{:S(2)}) collective-permute-start(bf16[16,8320]{1,0:T(8,128)(2,1)S(1)} %get-tuple-element.45), channel_id=1, source_target_pairs={{0,1},{1,0},{2,3},{3,2},{4,5},{5,4},{6,7},{7,6},{8,9},{9,8},{10,11... | collective-permute-start | bytes 798728 | tf_op jit(solution)/shard_map/ppermute | solution.py:38
  34.7 8.7 %collective-permute-start.12 = (bf16[16,4224]{1,0:T(8,128)(2,1)S(1)}, bf16[16,4224]{1,0:T(8,128)(2,1)S(1)}, u32[]{:S(2)}, u32[]{:S(2)}) collective-permute-start(bf16[16,4224]{1,0:T(8,128)(2,1)S(1)} %get-tuple-element.44.own), channel_id=1, source_target_pairs={{0,2},{1,3},{2,0},{3,1},{4,6},{5,7},{6,4},{7,5},{8,10},{9,11},{10,... | collective-permute-start | bytes 405512 | tf_op jit(solution)/shard_map/ppermute | solution.py:38
  36.2 7.2 %collective-permute-start.11 = (bf16[16,4096]{1,0:T(8,128)(2,1)S(1)}, bf16[16,4096]{1,0:T(8,128)(2,1)S(1)}, u32[]{:S(2)}, u32[]{:S(2)}) collective-permute-start(bf16[16,4096]{1,0:T(8,128)(2,1)S(1)} %get-tuple-element.46), channel_id=1, source_target_pairs={{0,2},{1,3},{2,0},{3,1},{4,6},{5,7},{6,4},{7,5},{8,10},{9,11},{10,... | collective-permute-start | bytes 393224 | tf_op jit(solution)/shard_map/ppermute | solution.py:38
  44.1 16.1 %collective-permute-start.13 = (bf16[16,4224]{1,0:T(8,128)(2,1)S(1)}, bf16[16,4224]{1,0:T(8,128)(2,1)S(1)}, u32[]{:S(2)}, u32[]{:S(2)}) collective-permute-start(bf16[16,4224]{1,0:T(8,128)(2,1)S(1)} %get-tuple-element.55), channel_id=1, source_target_pairs={{0,28},{4,8},{8,4},{12,16},{16,12},{20,24},{24,20},{28,0},{1,29},{... | collective-permute-start | bytes 405512 | tf_op jit(solution)/shard_map/ppermute | solution.py:605
  44.4 22.6 %collective-permute-start.15 = (bf16[16,4096]{1,0:T(8,128)(2,1)S(1)}, bf16[16,4096]{1,0:T(8,128)(2,1)S(1)}, u32[]{:S(2)}, u32[]{:S(2)}) collective-permute-start(bf16[16,4096]{1,0:T(8,128)(2,1)S(1)} %get-tuple-element.61), channel_id=1, source_target_pairs={{0,4},{4,0},{8,12},{12,8},{16,20},{20,16},{24,28},{28,24},{1,5},{5... | collective-permute-start | bytes 393224 | tf_op jit(solution)/shard_map/ppermute | solution.py:604
  46.4 8.2 %collective-permute-start.14 = (bf16[4,16,896]{2,1,0:T(8,128)(2,1)S(1)}, bf16[4,16,896]{2,1,0:T(8,128)(2,1)S(1)}, u32[]{:S(2)}, u32[]{:S(2)}) collective-permute-start(bf16[4,16,896]{2,1,0:T(8,128)(2,1)S(1)} %get-tuple-element.56.refs_8_), channel_id=1, source_target_pairs={{0,28},{4,24},{8,20},{12,16},{16,12},{20,8},{24,4},{28,0},{1,29},{... | collective-permute-start | bytes 344072 | tf_op jit(solution)/shard_map/ppermute | solution.py:603
